TPU v7x, 128 devices: a whole 4x4x4 slice. The times are simulated.
128 devices in a mesh: row: 8 (over x_lo, z), col: 16 (over y, x_hi, core).
Axes of the slice: x: 4 (x_hi: 2, x_lo: 2; x = x_hi * 2 + x_lo), y: 4, z: 4, core: 2. Of those that a mesh axis runs over, the one named last changes fastest.
Arguments:
- grad_first: float32 [4096, 20480], P('row', 'col'), may hold values from -1000 to 1000
- grad_second: float32 [4096, 20480], P('row', 'col'), may hold values from -1000 to 1000
Outputs:
- update: float32 [4096, 20480], P('row', 'col')
All inputs are finite; a program needn't handle non-finite values.
Results may differ from a plain program's by a relative error of at most 0.00014.
Values sent between devices are 32-bit elements; how exact they have to be, the bound alone decides.
No kernel may reach another device: no remote copies, remote signals or barrier semaphores. Data moves between devices by JAX's collectives and lax.ppermute only.
A program may use at most 128 MiB of HBM per device.

v0:
```python
import functools

import jax
import jax.numpy as jnp
import numpy as np
from jax import lax
from jax.experimental import pallas as pl
from jax.experimental.pallas import tpu as pltpu
from jax.sharding import PartitionSpec as P

D = 4096
FF = 20480
BLOCK = 256
HALF = 128
ITERS = 6
DAMPING = 0.001
ROWS = 8
COLS = 16
RIGHT = 5
PACK = BLOCK + 8

f32 = jnp.float32
bf16 = jnp.bfloat16

OWNERS = ((0, 2, 1, 5, 7), (4, 6, 7, 1, 3))


def block_of(core, row):
    return OWNERS[core].index(row) if row in OWNERS[core] else -1


def order_table():
    table = np.zeros((2, ROWS, 2 * RIGHT), np.int32)
    for core in range(2):
        for row in range(ROWS):
            slots = [d for d in range(ROWS) if block_of(core, row ^ d) >= 0]
            table[core, row, :RIGHT] = slots
            table[core, row, RIGHT:] = [block_of(core, row ^ d) for d in slots]
    return table


def pairs_to_owners(d):
    return [
        (row * COLS + col, (row ^ d) * COLS + col)
        for row in range(ROWS)
        for col in range(COLS)
        if block_of(col % 2, row ^ d) >= 0
    ]


def pairs_from_owners(d):
    return [
        (row * COLS + col, (row ^ d) * COLS + col)
        for row in range(ROWS)
        for col in range(COLS)
        if block_of(col % 2, row) >= 0
    ]


def swap(value, d):
    return lax.ppermute(value, "col", [(i, i ^ d) for i in range(COLS)])


def parts(value):
    high = value.astype(bf16)
    return high, (value - high.astype(f32)).astype(bf16)


def dot(left, right, dims=((1,), (0,))):
    return lax.dot_general(left, right, (dims, ((), ())), preferred_element_type=f32)


def product(left, right, dims=((1,), (0,))):
    (lh, ll), (rh, rl) = left, right
    return dot(lh, rh, dims) + (dot(lh, rl, dims) + dot(ll, rh, dims))


def iotas(n):
    return (
        lax.broadcasted_iota(jnp.int32, (n, n), 0),
        lax.broadcasted_iota(jnp.int32, (n, n), 1),
    )


def store_packed(ref, start, block):
    i, j = iotas(HALF)
    first, last = block[:HALF, :HALF], block[HALF:, HALF:]
    ref[pl.ds(start, HALF), :] = block[:HALF, HALF:]
    ref[pl.ds(start + HALF, HALF), :] = jnp.where(i >= j, first, last)
    diagonal = jnp.sum(jnp.where(i == j, last, 0.0), axis=0, keepdims=True)
    ref[pl.ds(start + BLOCK, 8), :] = jnp.broadcast_to(diagonal, (8, HALF))


def unpacked(packed):
    i, j = iotas(HALF)
    upper, mixed, diagonal = packed[:HALF], packed[HALF:BLOCK], packed[BLOCK : BLOCK + 1]
    turned = mixed.T
    first = jnp.where(i >= j, mixed, turned)
    last = jnp.where(i < j, mixed, jnp.where(i == j, jnp.broadcast_to(diagonal, (HALF, HALF)), turned))
    return jnp.concatenate(
        [
            jnp.concatenate([first, upper], axis=1),
            jnp.concatenate([upper.T, last], axis=1),
        ],
        axis=0,
    )


def roots(statistics):
    i, j = iotas(BLOCK)
    identity = jnp.where(i == j, 1.0, 0.0).astype(f32)
    currents, scaleds = [], []
    for statistic in statistics:
        damped = statistic + DAMPING * identity
        norm = jnp.sqrt(jnp.sum(damped * damped, axis=(0, 1), keepdims=True))
        currents.append(lax.rsqrt(jnp.sqrt(norm)))
        scaleds.append(damped / norm)
    for iteration in range(ITERS):
        factors = [(5.0 * identity - scaled) * 0.25 for scaled in scaleds]
        split = [parts(factor) for factor in factors]
        if iteration == 0:
            currents = [current * factor for current, factor in zip(currents, factors)]
        else:
            currents = [product(parts(current), fs) for current, fs in zip(currents, split)]
        if iteration < ITERS - 1:
            squares = [parts(product(fs, fs)) for fs in split]
            fourths = [parts(product(sq, sq)) for sq in squares]
            scaleds = [product(fo, parts(scaled)) for fo, scaled in zip(fourths, scaleds)]
    return currents


def right_stats_kernel(table, first, second, *outs):
    step = pl.program_id(0)
    dims = ((0,), (0,))
    one = parts(first[...])
    two = parts(second[...])
    sum_one = product(one, one, dims) * (1.0 / D)
    sum_two = sum_one + product(two, two, dims) * (1.0 / D)
    for d in range(ROWS):

        @pl.when(table[step] == d)
        def _(d=d):
            store_packed(outs[d], 0, sum_one)
            store_packed(outs[d], PACK, sum_two)


def left_stats_kernel(info, first, second, keep, send):
    core = info[0]
    dims = ((1,), (1,))
    for out, block in ((keep, core), (send, 1 - core)):
        rows = pl.ds(pl.multiple_of(block * BLOCK, BLOCK), BLOCK)
        one = parts(first[rows, :])
        two = parts(second[rows, :])
        sum_one = product(one, one, dims) * (1.0 / FF)
        sum_two = sum_one + product(two, two, dims) * (1.0 / FF)
        store_packed(out, 0, sum_one)
        store_packed(out, PACK, sum_two)


def right_roots_kernel(*refs):
    ins, out = refs[:-1], refs[-1]
    total = ins[0][...]
    for ref in ins[1:]:
        total = total + ref[...]
    one, two = roots([unpacked(total[:PACK]), unpacked(total[PACK:])])
    store_packed(out, 0, one)
    store_packed(out, PACK, two)


def left_root_kernel(*refs):
    ins, out = refs[:-1], refs[-1]
    total = ins[0][...]
    for ref in ins[1:]:
        total = total + ref[...]
    (one,) = roots([unpacked(total)])
    store_packed(out, 0, one)


def halfway_kernel(info, first, second, mine, other, high_one, low_one, high_two, low_two, high, low):
    core = info[0]

    @pl.when(pl.program_id(0) == 0)
    def _():
        for b, ref in enumerate((mine, other)):
            for s in range(2):
                root = unpacked(ref[s * PACK : (s + 1) * PACK, :])
                high[2 * b + s], low[2 * b + s] = parts(root)

    for b, block in ((0, core), (1, 1 - core)):
        rows = pl.ds(pl.multiple_of(block * BLOCK, BLOCK), BLOCK)
        for s, source, high_out, low_out in ((0, first, high_one, low_one), (1, second, high_two, low_two)):
            result = product((high[2 * b + s], low[2 * b + s]), parts(source[rows, :]))
            high_out[rows, :], low_out[rows, :] = parts(result)


def apply_kernel(table, high_one, low_one, high_two, low_two, *refs):
    ins, out, held = refs[:ROWS], refs[ROWS], refs[ROWS + 1]
    step = pl.program_id(0)
    for d in range(ROWS):

        @pl.when(table[step] == d)
        def _(d=d):
            held[...] = ins[d][...]

    packed = held[...]
    one = parts(unpacked(packed[:PACK]))
    two = parts(unpacked(packed[PACK:]))
    out[...] = product((high_one[...], low_one[...]), one) + product((high_two[...], low_two[...]), two)


VMEM = pl.BlockSpec(memory_space=pltpu.VMEM)
SMEM = pl.BlockSpec(memory_space=pltpu.SMEM)


def params():
    return pltpu.CompilerParams(vmem_limit_bytes=40 * 1024 * 1024)


def cost(flops, moved):
    return pl.CostEstimate(flops=int(flops), bytes_accessed=int(moved), transcendentals=0)


def body(grad_first, grad_second):
    rows, cols = grad_first.shape
    row, col = lax.axis_index("row"), lax.axis_index("col")
    core = lax.rem(col, 2)
    high_x = lax.rem(col // 2, 2)
    table = jnp.asarray(order_table())[core, row]
    info = core.reshape(1).astype(jnp.int32)
    pair = jax.ShapeDtypeStruct((2 * PACK, HALF), f32)
    single = jax.ShapeDtypeStruct((PACK, HALF), f32)
    grads = 2 * rows * cols * 4
    passes = 3 * 2 * BLOCK * rows * cols * 2

    whole_pair = pl.BlockSpec((2 * PACK, HALF), lambda k, t: (0, 0))
    column = pl.BlockSpec((rows, BLOCK), lambda k, t: (0, t[RIGHT + k]))
    right_parts = pl.pallas_call(
        right_stats_kernel,
        grid_spec=pltpu.PrefetchScalarGridSpec(
            num_scalar_prefetch=1,
            grid=(RIGHT,),
            in_specs=[column, column],
            out_specs=[whole_pair] * ROWS,
        ),
        out_shape=[pair] * ROWS,
        compiler_params=params(),
        cost_estimate=cost(passes, grads),
        name="right_stats",
    )(table, grad_first, grad_second)
    arrived = [right_parts[0]] + [
        lax.ppermute(right_parts[d], ("row", "col"), pairs_to_owners(d)) for d in range(1, ROWS)
    ]

    keep, send = pl.pallas_call(
        left_stats_kernel,
        in_specs=[SMEM, VMEM, VMEM],
        out_specs=[VMEM, VMEM],
        out_shape=[pair, pair],
        compiler_params=params(),
        cost_estimate=cost(passes, grads),
        name="left_stats",
    )(info, grad_first, grad_second)
    both = (keep + swap(send, 1)).reshape(2, PACK, HALF)
    own = lax.dynamic_index_in_dim(both, high_x, 0, keepdims=False)
    own = own + swap(lax.dynamic_index_in_dim(both, 1 - high_x, 0, keepdims=False), 2)
    left_root = pl.pallas_call(
        left_root_kernel,
        in_specs=[VMEM] * 4,
        out_specs=VMEM,
        out_shape=single,
        compiler_params=params(),
        cost_estimate=cost(20 * 6 * BLOCK**3, 5 * PACK * HALF * 4),
        name="left_root",
    )(own, swap(own, 4), swap(own, 8), swap(own, 12))
    left_other = swap(left_root, 2)
    mine = jnp.where(
        high_x == 0,
        jnp.concatenate([left_root, left_other]),
        jnp.concatenate([left_other, left_root]),
    )
    other = swap(mine, 1)

    right_root = pl.pallas_call(
        right_roots_kernel,
        in_specs=[VMEM] * ROWS,
        out_specs=VMEM,
        out_shape=pair,
        compiler_params=params(),
        cost_estimate=cost(2 * 20 * 6 * BLOCK**3, 18 * PACK * HALF * 4),
        name="right_roots",
    )(*arrived)
    gathered = [right_root] + [
        lax.ppermute(right_root, ("row", "col"), pairs_from_owners(d)) for d in range(1, ROWS)
    ]

    halves = jax.ShapeDtypeStruct((rows, cols), bf16)
    tile = pl.BlockSpec((rows, BLOCK), lambda k: (0, k))
    halfway = pl.pallas_call(
        halfway_kernel,
        grid=(RIGHT,),
        in_specs=[SMEM, tile, tile, VMEM, VMEM],
        out_specs=[tile] * 4,
        out_shape=[halves] * 4,
        scratch_shapes=[pltpu.VMEM((4, BLOCK, BLOCK), bf16), pltpu.VMEM((4, BLOCK, BLOCK), bf16)],
        compiler_params=params(),
        cost_estimate=cost(passes, 2 * grads),
        name="halfway",
    )(info, grad_first, grad_second, mine, other)

    return pl.pallas_call(
        apply_kernel,
        grid_spec=pltpu.PrefetchScalarGridSpec(
            num_scalar_prefetch=1,
            grid=(RIGHT,),
            in_specs=[column] * 4 + [whole_pair] * ROWS,
            out_specs=column,
            scratch_shapes=[pltpu.VMEM((2 * PACK, HALF), f32)],
        ),
        out_shape=jax.ShapeDtypeStruct((rows, cols), f32),
        compiler_params=params(),
        cost_estimate=cost(passes, 2 * grads),
        name="apply",
    )(table, *halfway, *gathered)


def solution(mesh):
    in_specs = (P("row", "col"), P("row", "col"))
    out_specs = P("row", "col")
    return jax.shard_map(body, mesh=mesh, in_specs=in_specs, out_specs=out_specs, check_vma=False)
```

profile of v0, /device:TPU:4, one launch (start us, length us, event | category | flops | bytes accessed | tf_op | source)
XLA Modules:
  0.0 109.8 jit_solution(14899732824824927515)
XLA Ops:
  0.0 1.7 %copy-done = f32[512,1280]{1,0:T(8,128)S(1)} copy-done((f32[512,1280]{1,0:T(8,128)S(1)}, f32[512,1280]{1,0:T(8,128)}, u32[]{:S(2)}) %copy-start) | copy-done | bytes 2621464
  1.7 1.7 %copy-done.2 = f32[512,1280]{1,0:T(8,128)S(1)} copy-done((f32[512,1280]{1,0:T(8,128)S(1)}, f32[512,1280]{1,0:T(8,128)}, u32[]{:S(2)}) %copy-start.2) | copy-done | bytes 2621464
  3.5 2.3 %left_stats.1 = (f32[528,128]{1,0:T(8,128)S(1)}, f32[528,128]{1,0:T(8,128)S(1)}) custom-call(s32[1]{0:T(128)} %bitcast.1.info, f32[512,1280]{1,0:T(8,128)S(1)} %copy-done, f32[512,1280]{1,0:T(8,128)S(1)} %copy-done.2), custom_call_target="tpu_custom_call" | custom-call | flops 2013265920 | bytes 5242880 | tf_op jit(solution)/shard_map/left_stats/pallas_call | solution.py:254
  5.8 0.1 collective-permute-start
  5.9 0.7 fusion.table
  6.6 0.8 collective-permute-done
  7.4 0.0 copy-start.15
  7.5 0.7 copy-done.15
  8.1 0.4 collective-permute-start.1
  8.6 1.7 %copy-done.3 = f32[512,1280]{1,0:T(8,128)S(1)} copy-done((f32[512,1280]{1,0:T(8,128)S(1)}, f32[512,1280]{1,0:T(8,128)}, u32[]{:S(2)}) %copy-start.3) | copy-done | bytes 2621464
  10.3 5.4 %right_stats.1 = (f32[528,128]{1,0:T(8,128)S(1)}, f32[528,128]{1,0:T(8,128)}, f32[528,128]{1,0:T(8,128)}, f32[528,128]{1,0:T(8,128)S(1)}, f32[528,128]{1,0:T(8,1...) custom-call(s32[10]{0:T(128)S(1)} %fusion.table, f32[512,1280]{1,0:T(8,128)S(1)} %copy-done.1, ...), custom_call_target="tpu_custom_call" | custom-call | flops 2013265920 | bytes 5242880 | tf_op jit(solution)/shard_map/right_stats/pallas_call | solution.py:237
  15.7 0.7 copy-done.5
  16.4 0.7 copy-done.6
  17.1 0.7 copy-done.7
  17.9 0.7 copy-done.8
  18.6 0.7 copy-done.13
  19.3 3.9 %collective-permute-start.7 = (f32[528,128]{1,0:T(8,128)}, f32[528,128]{1,0:T(8,128)S(1)}, u32[]{:S(2)}, u32[]{:S(2)}) collective-permute-start(f32[528,128]{1,0:T(8,128)} %get-tuple-element.26), channel_id=1, source_target_pairs={{0,16},{1,17},{2,18},{3,19},{4,20},{5,21},{6,22},{7,23},{8,24},{9,... | collective-permute-start | bytes 811016 | tf_op jit(solution)/shard_map/ppermute | solution.py:251
  23.2 3.3 %collective-permute-start.8 = (f32[528,128]{1,0:T(8,128)}, f32[528,128]{1,0:T(8,128)}, u32[]{:S(2)}, u32[]{:S(2)}) collective-permute-start(f32[528,128]{1,0:T(8,128)} %get-tuple-element.27), channel_id=1, source_target_pairs={{0,32},{2,34},{4,36},{6,38},{8,40},{10,42},{12,44},{14,46},{17,49}... | collective-permute-start | bytes 811016 | tf_op jit(solution)/shard_map/ppermute | solution.py:251
  26.5 0.9 bitcast_add_fusion.refs_0_
  27.4 3.1 %collective-permute-start.4 = (f32[264,128]{1,0:T(8,128)S(1)}, f32[264,128]{1,0:T(8,128)S(1)}, u32[]{:S(2)}, u32[]{:S(2)}) collective-permute-start(f32[264,128]{1,0:T(8,128)S(1)} %bitcast_add_fusion.refs_0_), channel_id=1, source_target_pairs={{0,12},{1,13},{2,14},{3,15},{4,8},{5,9},{6,10},{7,11},{8,4},{9,5},... | collective-permute-start | bytes 405512 | tf_op jit(solution)/shard_map/ppermute | solution.py:61
  30.5 0.6 collective-permute-start.3
  31.2 0.5 collective-permute-start.2
  31.6 1.3 %collective-permute-start.9 = (f32[528,128]{1,0:T(8,128)}, f32[528,128]{1,0:T(8,128)}, u32[]{:S(2)}, u32[]{:S(2)}) collective-permute-start(f32[528,128]{1,0:T(8,128)} %copy-done.8), channel_id=1, source_target_pairs={{1,49},{3,51},{5,53},{7,55},{9,57},{11,59},{13,61},{15,63},{16,32}... | collective-permute-start | bytes 811016 | tf_op jit(solution)/shard_map/ppermute | solution.py:251
  32.9 0.5 collective-permute-done.8.refs_2_
  33.4 1.3 %collective-permute-start.10 = (f32[528,128]{1,0:T(8,128)}, f32[528,128]{1,0:T(8,128)}, u32[]{:S(2)}, u32[]{:S(2)}) collective-permute-start(f32[528,128]{1,0:T(8,128)} %copy-done.7), channel_id=1, source_target_pairs={{1,65},{3,67},{5,69},{7,71},{9,73},{11,75},{13,77},{15,79},{16,80}... | collective-permute-start | bytes 811016 | tf_op jit(solution)/shard_map/ppermute | solution.py:251
  34.7 0.2 collective-permute-done.4.refs_3_
  34.9 7.6 %collective-permute-start.11 = (f32[528,128]{1,0:T(8,128)}, f32[528,128]{1,0:T(8,128)}, u32[]{:S(2)}, u32[]{:S(2)}) collective-permute-start(f32[528,128]{1,0:T(8,128)} %copy-done.6), channel_id=1, source_target_pairs={{0,80},{2,82},{4,84},{6,86},{8,88},{10,90},{12,92},{14,94},{17,65}... | collective-permute-start | bytes 811016 | tf_op jit(solution)/shard_map/ppermute | solution.py:251
  42.5 0.6 copy-done.9
  43.2 1.3 %collective-permute-start.12 = (f32[528,128]{1,0:T(8,128)}, f32[528,128]{1,0:T(8,128)}, u32[]{:S(2)}, u32[]{:S(2)}) collective-permute-start(f32[528,128]{1,0:T(8,128)} %copy-done.5), channel_id=1, source_target_pairs={{1,97},{3,99},{5,101},{7,103},{9,105},{11,107},{13,109},{15,111},{... | collective-permute-start | bytes 811016 | tf_op jit(solution)/shard_map/ppermute | solution.py:251
  44.5 0.6 copy-done.11
  45.1 4.0 %collective-permute-start.13 = (f32[528,128]{1,0:T(8,128)S(1)}, f32[528,128]{1,0:T(8,128)}, u32[]{:S(2)}, u32[]{:S(2)}) collective-permute-start(f32[528,128]{1,0:T(8,128)S(1)} %get-tuple-element.32), channel_id=1, source_target_pairs={{0,112},{1,113},{2,114},{3,115},{4,116},{5,117},{6,118},{7,119},{8... | collective-permute-start | bytes 811016 | tf_op jit(solution)/shard_map/ppermute | solution.py:251
  49.2 0.9 copy-done.10
  50.1 0.9 copy-done.12
  51.0 5.2 %left_root.1 = f32[264,128]{1,0:T(8,128)S(1)} custom-call(f32[264,128]{1,0:T(8,128)S(1)} %bitcast_add_fusion.refs_0_, f32[264,128]{1,0:T(8,128)S(1)} %copy-done.12, f32[264,128]{1,0:T(8,128)S(1)} %copy-done.10, f32[264,128]{1,0:T(8,128)S(1)} %collective-permute-done.4.refs_3_), custom_call_target="tpu_custom_call" | custom-call | flops 2013265920 | bytes 675840 | tf_op jit(solution)/shard_map/left_root/pallas_call | solution.py:266
  56.2 3.3 %collective-permute-start.5 = (f32[264,128]{1,0:T(8,128)S(1)}, f32[264,128]{1,0:T(8,128)S(1)}, u32[]{:S(2)}, u32[]{:S(2)}) collective-permute-start(f32[264,128]{1,0:T(8,128)S(1)} %left_root.1), channel_id=1, source_target_pairs={{0,2},{1,3},{2,0},{3,1},{4,6},{5,7},{6,4},{7,5},{8,10},{9,11},{10,... | collective-permute-start | bytes 405512 | tf_op jit(solution)/shard_map/ppermute | solution.py:61
  59.6 8.1 %right_roots.1.refs_0_ = f32[528,128]{1,0:T(8,128)S(1)} custom-call(f32[528,128]{1,0:T(8,128)S(1)} %copy-done.14, f32[528,128]{1,0:T(8,128)S(1)} %collective-permute-done.7.refs_1_, f32[528,128]{1,0:T(8,128)} %collective-permute-done.8.refs_2_, f32[528,128]{1,0:T(8,128)} %collective-permute-done.9.refs_3_, f32[528,128]{1,0:T(8,128)} %collective-permute-done.10.refs_4_, ...), custom_call_target="tpu_custom_call" | custom-call | flops 4026531840 | bytes 2433024 | tf_op jit(solution)/shard_map/right_roots/pallas_call | solution.py:283
  67.7 4.5 %collective-permute-start.20 = (f32[528,128]{1,0:T(8,128)S(1)}, f32[528,128]{1,0:T(8,128)S(1)}, u32[]{:S(2)}, u32[]{:S(2)}) collective-permute-start(f32[528,128]{1,0:T(8,128)S(1)} %right_roots.1.refs_0_), channel_id=1, source_target_pairs={{0,112},{2,114},{4,116},{6,118},{8,120},{10,122},{12,124},{14,126}... | collective-permute-start | bytes 811016 | tf_op jit(solution)/shard_map/ppermute | solution.py:293
  72.2 3.0 %collective-permute-start.19 = (f32[528,128]{1,0:T(8,128)S(1)}, f32[528,128]{1,0:T(8,128)S(1)}, u32[]{:S(2)}, u32[]{:S(2)}) collective-permute-start(f32[528,128]{1,0:T(8,128)S(1)} %right_roots.1.refs_0_), channel_id=1, source_target_pairs={{0,96},{2,98},{4,100},{6,102},{8,104},{10,106},{12,108},{14,110},{... | collective-permute-start | bytes 811016 | tf_op jit(solution)/shard_map/ppermute | solution.py:293
  75.3 0.1 collective-permute-start.6
  75.4 1.9 %collective-permute-start.18 = (f32[528,128]{1,0:T(8,128)S(1)}, f32[528,128]{1,0:T(8,128)S(1)}, u32[]{:S(2)}, u32[]{:S(2)}) collective-permute-start(f32[528,128]{1,0:T(8,128)S(1)} %right_roots.1.refs_0_), channel_id=1, source_target_pairs={{0,80},{2,82},{4,84},{6,86},{8,88},{10,90},{12,92},{14,94},{16,64}... | collective-permute-start | bytes 811016 | tf_op jit(solution)/shard_map/ppermute | solution.py:293
  77.3 1.3 %collective-permute-start.17 = (f32[528,128]{1,0:T(8,128)S(1)}, f32[528,128]{1,0:T(8,128)S(1)}, u32[]{:S(2)}, u32[]{:S(2)}) collective-permute-start(f32[528,128]{1,0:T(8,128)S(1)} %right_roots.1.refs_0_), channel_id=1, source_target_pairs={{0,64},{2,66},{4,68},{6,70},{8,72},{10,74},{12,76},{14,78},{16,80}... | collective-permute-start | bytes 811016 | tf_op jit(solution)/shard_map/ppermute | solution.py:293
  78.6 5.2 %collective-permute-done.20.refs_7_ = f32[528,128]{1,0:T(8,128)S(1)} collective-permute-done((f32[528,128]{1,0:T(8,128)S(1)}, f32[528,128]{1,0:T(8,128)S(1)}, u32[]{:S(2)}, u32[]{:S(2)}) %collective-permute-start.20) | collective-permute-done | bytes 270368 | tf_op jit(solution)/shard_map/ppermute | solution.py:293
  83.8 1.3 %collective-permute-start.16 = (f32[528,128]{1,0:T(8,128)S(1)}, f32[528,128]{1,0:T(8,128)S(1)}, u32[]{:S(2)}, u32[]{:S(2)}) collective-permute-start(f32[528,128]{1,0:T(8,128)S(1)} %right_roots.1.refs_0_), channel_id=1, source_target_pairs={{0,48},{2,50},{4,52},{6,54},{8,56},{10,58},{12,60},{14,62},{16,32}... | collective-permute-start | bytes 811016 | tf_op jit(solution)/shard_map/ppermute | solution.py:293
  85.1 3.5 %collective-permute-start.15 = (f32[528,128]{1,0:T(8,128)S(1)}, f32[528,128]{1,0:T(8,128)S(1)}, u32[]{:S(2)}, u32[]{:S(2)}) collective-permute-start(f32[528,128]{1,0:T(8,128)S(1)} %right_roots.1.refs_0_), channel_id=1, source_target_pairs={{0,32},{2,34},{4,36},{6,38},{8,40},{10,42},{12,44},{14,46},{16,48}... | collective-permute-start | bytes 811016 | tf_op jit(solution)/shard_map/ppermute | solution.py:293
  88.7 5.0 %collective-permute-start.14 = (f32[528,128]{1,0:T(8,128)S(1)}, f32[528,128]{1,0:T(8,128)S(1)}, u32[]{:S(2)}, u32[]{:S(2)}) collective-permute-start(f32[528,128]{1,0:T(8,128)S(1)} %right_roots.1.refs_0_), channel_id=1, source_target_pairs={{0,16},{2,18},{4,20},{6,22},{8,24},{10,26},{12,28},{14,30},{16,0},... | collective-permute-start | bytes 811016 | tf_op jit(solution)/shard_map/ppermute | solution.py:293
  93.7 4.1 %halfway.1 = (bf16[512,1280]{1,0:T(8,128)(2,1)S(1)}, bf16[512,1280]{1,0:T(8,128)(2,1)S(1)}, bf16[512,1280]{1,0:T(8,128)(2,1)S(1)}, bf16[512,1280]{1,0:T(8,128)(2,1)S(1)}) custom-call(s32[1]{0:T(128)} %bitcast.1.info, f32[512,1280]{1,0:T(8,128)S(1)} %copy-done.1, f32[512,1280]{1,0:T(8,128)S(1)} %copy-done.4, f32[528,128]{1,0:T(8,128)S(1)} %maximum_select_fusion.mine, ...), custom_call_target="tpu_custom_call" | custom-call | flops 2013265920 | bytes 10485760 | tf_op jit(solution)/shard_map/halfway/pallas_call | solution.py:298
  97.8 6.2 %collective-permute-done.14.refs_1_ = f32[528,128]{1,0:T(8,128)S(1)} collective-permute-done((f32[528,128]{1,0:T(8,128)S(1)}, f32[528,128]{1,0:T(8,128)S(1)}, u32[]{:S(2)}, u32[]{:S(2)}) %collective-permute-start.14) | collective-permute-done | bytes 270368 | tf_op jit(solution)/shard_map/ppermute | solution.py:293
  104.0 5.8 %apply.1 = f32[512,1280]{1,0:T(8,128)} custom-call(s32[10]{0:T(128)S(1)} %fusion.table, bf16[512,1280]{1,0:T(8,128)(2,1)S(1)} %get-tuple-element.21.high_one, bf16[512,1280]{1,0:T(8,128)(2,1)S(1)} %get-tuple-element.22.low_one, bf16[512,1280]{1,0:T(8,128)(2,1)S(1)} %get-tuple-element.23.high_two, bf16[512,1280]{1,0:T(8,128)(2,1)S(1)} %get-tuple-element.24.low_two, ...), custom_call_target="tpu_custom_call" | custom-call | flops 2013265920 | bytes 10485760 | tf_op jit(solution)/shard_map/apply/pallas_call | solution.py:310
  (37 shorter events, 0.2 us)
Async XLA Ops:
  0.0 1.7 %copy-start = (f32[512,1280]{1,0:T(8,128)S(1)}, f32[512,1280]{1,0:T(8,128)}, u32[]{:S(2)}) copy-start(f32[512,1280]{1,0:T(8,128)} %first.5) | copy-start | bytes 7864324
  1.7 1.7 %copy-start.2 = (f32[512,1280]{1,0:T(8,128)S(1)}, f32[512,1280]{1,0:T(8,128)}, u32[]{:S(2)}) copy-start(f32[512,1280]{1,0:T(8,128)} %second.5) | copy-start | bytes 7864324
  3.5 5.1 %copy-start.1 = (f32[512,1280]{1,0:T(8,128)S(1)}, f32[512,1280]{1,0:T(8,128)}, u32[]{:S(2)}) copy-start(f32[512,1280]{1,0:T(8,128)} %first.5) | copy-start | bytes 7864324
  5.8 1.6 %collective-permute-start = (f32[528,128]{1,0:T(8,128)S(1)}, f32[528,128]{1,0:T(8,128)S(1)}, u32[]{:S(2)}, u32[]{:S(2)}) collective-permute-start(f32[528,128]{1,0:T(8,128)S(1)} %get-tuple-element.20), channel_id=1, source_target_pairs={{0,1},{1,0},{2,3},{3,2},{4,5},{5,4},{6,7},{7,6},{8,9},{9,8},{10,11... | collective-permute-start | bytes 811016 | tf_op jit(solution)/shard_map/ppermute | solution.py:61
  7.4 0.7 copy-start.15
  8.1 18.4 %collective-permute-start.1 = (f32[264,128]{1,0:T(8,128)S(1)}, f32[264,128]{1,0:T(8,128)S(1)}, u32[]{:S(2)}, u32[]{:S(2)}) collective-permute-start(f32[264,128]{1,0:T(8,128)S(1)} %dynamic-slice_bitcast_fusion), channel_id=1, source_target_pairs={{0,2},{1,3},{2,0},{3,1},{4,6},{5,7},{6,4},{7,5},{8,10},{9,11},{10,... | collective-permute-start | bytes 405512 | tf_op jit(solution)/shard_map/ppermute | solution.py:61
  8.6 1.7 %copy-start.3 = (f32[512,1280]{1,0:T(8,128)S(1)}, f32[512,1280]{1,0:T(8,128)}, u32[]{:S(2)}) copy-start(f32[512,1280]{1,0:T(8,128)} %second.5) | copy-start | bytes 7864324
  15.7 0.7 copy-start.5
  16.4 0.7 copy-start.6
  17.1 0.7 copy-start.7
  17.9 0.7 copy-start.8
  18.6 0.7 copy-start.13
  19.3 12.3 %collective-permute-start.7 = (f32[528,128]{1,0:T(8,128)}, f32[528,128]{1,0:T(8,128)S(1)}, u32[]{:S(2)}, u32[]{:S(2)}) collective-permute-start(f32[528,128]{1,0:T(8,128)} %get-tuple-element.26), channel_id=1, source_target_pairs={{0,16},{1,17},{2,18},{3,19},{4,20},{5,21},{6,22},{7,23},{8,24},{9,... | collective-permute-start | bytes 811016 | tf_op jit(solution)/shard_map/ppermute | solution.py:251
  23.2 10.2 %collective-permute-start.8 = (f32[528,128]{1,0:T(8,128)}, f32[528,128]{1,0:T(8,128)}, u32[]{:S(2)}, u32[]{:S(2)}) collective-permute-start(f32[528,128]{1,0:T(8,128)} %get-tuple-element.27), channel_id=1, source_target_pairs={{0,32},{2,34},{4,36},{6,38},{8,40},{10,42},{12,44},{14,46},{17,49}... | collective-permute-start | bytes 811016 | tf_op jit(solution)/shard_map/ppermute | solution.py:251
  27.4 7.5 %collective-permute-start.4 = (f32[264,128]{1,0:T(8,128)S(1)}, f32[264,128]{1,0:T(8,128)S(1)}, u32[]{:S(2)}, u32[]{:S(2)}) collective-permute-start(f32[264,128]{1,0:T(8,128)S(1)} %bitcast_add_fusion.refs_0_), channel_id=1, source_target_pairs={{0,12},{1,13},{2,14},{3,15},{4,8},{5,9},{6,10},{7,11},{8,4},{9,5},... | collective-permute-start | bytes 405512 | tf_op jit(solution)/shard_map/ppermute | solution.py:61
  30.5 12.0 %collective-permute-start.3 = (f32[264,128]{1,0:T(8,128)S(1)}, f32[264,128]{1,0:T(8,128)S(1)}, u32[]{:S(2)}, u32[]{:S(2)}) collective-permute-start(f32[264,128]{1,0:T(8,128)S(1)} %bitcast_add_fusion.refs_0_), channel_id=1, source_target_pairs={{0,8},{1,9},{2,10},{3,11},{4,12},{5,13},{6,14},{7,15},{8,0},{9,1},... | collective-permute-start | bytes 405512 | tf_op jit(solution)/shard_map/ppermute | solution.py:61
  31.2 13.3 %collective-permute-start.2 = (f32[264,128]{1,0:T(8,128)S(1)}, f32[264,128]{1,0:T(8,128)S(1)}, u32[]{:S(2)}, u32[]{:S(2)}) collective-permute-start(f32[264,128]{1,0:T(8,128)S(1)} %bitcast_add_fusion.refs_0_), channel_id=1, source_target_pairs={{0,4},{1,5},{2,6},{3,7},{4,0},{5,1},{6,2},{7,3},{8,12},{9,13},{10,... | collective-permute-start | bytes 405512 | tf_op jit(solution)/shard_map/ppermute | solution.py:61
  31.6 24.6 %collective-permute-start.9 = (f32[528,128]{1,0:T(8,128)}, f32[528,128]{1,0:T(8,128)}, u32[]{:S(2)}, u32[]{:S(2)}) collective-permute-start(f32[528,128]{1,0:T(8,128)} %copy-done.8), channel_id=1, source_target_pairs={{1,49},{3,51},{5,53},{7,55},{9,57},{11,59},{13,61},{15,63},{16,32}... | collective-permute-start | bytes 811016 | tf_op jit(solution)/shard_map/ppermute | solution.py:251
  33.4 26.1 %collective-permute-start.10 = (f32[528,128]{1,0:T(8,128)}, f32[528,128]{1,0:T(8,128)}, u32[]{:S(2)}, u32[]{:S(2)}) collective-permute-start(f32[528,128]{1,0:T(8,128)} %copy-done.7), channel_id=1, source_target_pairs={{1,65},{3,67},{5,69},{7,71},{9,73},{11,75},{13,77},{15,79},{16,80}... | collective-permute-start | bytes 811016 | tf_op jit(solution)/shard_map/ppermute | solution.py:251
  34.9 24.6 %collective-permute-start.11 = (f32[528,128]{1,0:T(8,128)}, f32[528,128]{1,0:T(8,128)}, u32[]{:S(2)}, u32[]{:S(2)}) collective-permute-start(f32[528,128]{1,0:T(8,128)} %copy-done.6), channel_id=1, source_target_pairs={{0,80},{2,82},{4,84},{6,86},{8,88},{10,90},{12,92},{14,94},{17,65}... | collective-permute-start | bytes 811016 | tf_op jit(solution)/shard_map/ppermute | solution.py:251
  42.5 0.7 copy-start.9
  43.2 16.3 %collective-permute-start.12 = (f32[528,128]{1,0:T(8,128)}, f32[528,128]{1,0:T(8,128)}, u32[]{:S(2)}, u32[]{:S(2)}) collective-permute-start(f32[528,128]{1,0:T(8,128)} %copy-done.5), channel_id=1, source_target_pairs={{1,97},{3,99},{5,101},{7,103},{9,105},{11,107},{13,109},{15,111},{... | collective-permute-start | bytes 811016 | tf_op jit(solution)/shard_map/ppermute | solution.py:251
  44.5 0.7 copy-start.11
  45.1 14.4 %collective-permute-start.13 = (f32[528,128]{1,0:T(8,128)S(1)}, f32[528,128]{1,0:T(8,128)}, u32[]{:S(2)}, u32[]{:S(2)}) collective-permute-start(f32[528,128]{1,0:T(8,128)S(1)} %get-tuple-element.32), channel_id=1, source_target_pairs={{0,112},{1,113},{2,114},{3,115},{4,116},{5,117},{6,118},{7,119},{8... | collective-permute-start | bytes 811016 | tf_op jit(solution)/shard_map/ppermute | solution.py:251
  49.2 0.9 copy-start.10
  50.1 0.9 copy-start.12
  51.0 8.6 %copy-start.14 = (f32[528,128]{1,0:T(8,128)S(1)}, f32[528,128]{1,0:T(8,128)}, u32[]{:S(2)}) copy-start(f32[528,128]{1,0:T(8,128)} %copy-done.13) | copy-start | bytes 811012
  56.2 19.0 %collective-permute-start.5 = (f32[264,128]{1,0:T(8,128)S(1)}, f32[264,128]{1,0:T(8,128)S(1)}, u32[]{:S(2)}, u32[]{:S(2)}) collective-permute-start(f32[264,128]{1,0:T(8,128)S(1)} %left_root.1), channel_id=1, source_target_pairs={{0,2},{1,3},{2,0},{3,1},{4,6},{5,7},{6,4},{7,5},{8,10},{9,11},{10,... | collective-permute-start | bytes 405512 | tf_op jit(solution)/shard_map/ppermute | solution.py:61
  59.6 34.1 %copy-start.4 = (f32[512,1280]{1,0:T(8,128)S(1)}, f32[512,1280]{1,0:T(8,128)}, u32[]{:S(2)}) copy-start(f32[512,1280]{1,0:T(8,128)} %second.5) | copy-start | bytes 7864324
  67.7 16.1 %collective-permute-start.20 = (f32[528,128]{1,0:T(8,128)S(1)}, f32[528,128]{1,0:T(8,128)S(1)}, u32[]{:S(2)}, u32[]{:S(2)}) collective-permute-start(f32[528,128]{1,0:T(8,128)S(1)} %right_roots.1.refs_0_), channel_id=1, source_target_pairs={{0,112},{2,114},{4,116},{6,118},{8,120},{10,122},{12,124},{14,126}... | collective-permute-start | bytes 811016 | tf_op jit(solution)/shard_map/ppermute | solution.py:293
  72.2 12.9 %collective-permute-start.19 = (f32[528,128]{1,0:T(8,128)S(1)}, f32[528,128]{1,0:T(8,128)S(1)}, u32[]{:S(2)}, u32[]{:S(2)}) collective-permute-start(f32[528,128]{1,0:T(8,128)S(1)} %right_roots.1.refs_0_), channel_id=1, source_target_pairs={{0,96},{2,98},{4,100},{6,102},{8,104},{10,106},{12,108},{14,110},{... | collective-permute-start | bytes 811016 | tf_op jit(solution)/shard_map/ppermute | solution.py:293
  75.3 13.3 %collective-permute-start.6 = (f32[528,128]{1,0:T(8,128)S(1)}, f32[528,128]{1,0:T(8,128)S(1)}, u32[]{:S(2)}, u32[]{:S(2)}) collective-permute-start(f32[528,128]{1,0:T(8,128)S(1)} %maximum_select_fusion.mine), channel_id=1, source_target_pairs={{0,1},{1,0},{2,3},{3,2},{4,5},{5,4},{6,7},{7,6},{8,9},{9,8},{10,11... | collective-permute-start | bytes 811016 | tf_op jit(solution)/shard_map/ppermute | solution.py:61
  75.4 22.4 %collective-permute-start.18 = (f32[528,128]{1,0:T(8,128)S(1)}, f32[528,128]{1,0:T(8,128)S(1)}, u32[]{:S(2)}, u32[]{:S(2)}) collective-permute-start(f32[528,128]{1,0:T(8,128)S(1)} %right_roots.1.refs_0_), channel_id=1, source_target_pairs={{0,80},{2,82},{4,84},{6,86},{8,88},{10,90},{12,92},{14,94},{16,64}... | collective-permute-start | bytes 811016 | tf_op jit(solution)/shard_map/ppermute | solution.py:293
  77.3 20.5 %collective-permute-start.17 = (f32[528,128]{1,0:T(8,128)S(1)}, f32[528,128]{1,0:T(8,128)S(1)}, u32[]{:S(2)}, u32[]{:S(2)}) collective-permute-start(f32[528,128]{1,0:T(8,128)S(1)} %right_roots.1.refs_0_), channel_id=1, source_target_pairs={{0,64},{2,66},{4,68},{6,70},{8,72},{10,74},{12,76},{14,78},{16,80}... | collective-permute-start | bytes 811016 | tf_op jit(solution)/shard_map/ppermute | solution.py:293
  83.8 14.0 %collective-permute-start.16 = (f32[528,128]{1,0:T(8,128)S(1)}, f32[528,128]{1,0:T(8,128)S(1)}, u32[]{:S(2)}, u32[]{:S(2)}) collective-permute-start(f32[528,128]{1,0:T(8,128)S(1)} %right_roots.1.refs_0_), channel_id=1, source_target_pairs={{0,48},{2,50},{4,52},{6,54},{8,56},{10,58},{12,60},{14,62},{16,32}... | collective-permute-start | bytes 811016 | tf_op jit(solution)/shard_map/ppermute | solution.py:293
  85.1 12.7 %collective-permute-start.15 = (f32[528,128]{1,0:T(8,128)S(1)}, f32[528,128]{1,0:T(8,128)S(1)}, u32[]{:S(2)}, u32[]{:S(2)}) collective-permute-start(f32[528,128]{1,0:T(8,128)S(1)} %right_roots.1.refs_0_), channel_id=1, source_target_pairs={{0,32},{2,34},{4,36},{6,38},{8,40},{10,42},{12,44},{14,46},{16,48}... | collective-permute-start | bytes 811016 | tf_op jit(solution)/shard_map/ppermute | solution.py:293
  88.7 15.4 %collective-permute-start.14 = (f32[528,128]{1,0:T(8,128)S(1)}, f32[528,128]{1,0:T(8,128)S(1)}, u32[]{:S(2)}, u32[]{:S(2)}) collective-permute-start(f32[528,128]{1,0:T(8,128)S(1)} %right_roots.1.refs_0_), channel_id=1, source_target_pairs={{0,16},{2,18},{4,20},{6,22},{8,24},{10,26},{12,28},{14,30},{16,0},... | collective-permute-start | bytes 811016 | tf_op jit(solution)/shard_map/ppermute | solution.py:293
where the time goes:
time: 110 us
  starting transfers between devices  51.3 us (47%)
  Pallas kernels  30.9 us (28%)
  local copies, waits for them, and re-layouts  13.3 us (12%)
  waiting for transfers between devices  12.9 us (12%)
    ppermute x7, starting transfers between devices, body(): lax.ppermute(right_parts[d], ('row', 'col'), pairs_to_owners(d))  22.6 us
    ppermute x7, starting transfers between devices, body(): lax.ppermute(right_root, ('row', 'col'), pairs_from_owners(d))  20.6 us
    unnamed x32, local copies, waits for them, and re-layouts  12.6 us
    ppermute x7, waiting for transfers between devices, body(): lax.ppermute(right_root, ('row', 'col'), pairs_from_owners(d))  11.4 us
    pallas_call x1, Pallas kernels, body(): pl.pallas_call(right_roots_kernel, in_specs=[VMEM] * ROWS, out_specs=VMEM...  8.12 us
    ppermute x7, starting transfers between devices, swap(): return lax.ppermute(value, 'col', [(i, i ^ d) for i in range(COLS)])  8.05 us
    pallas_call x1, Pallas kernels, body(): pl.pallas_call(apply_kernel, grid_spec=pltpu.PrefetchScalarGridSpec(num_s...  5.79 us
    pallas_call x1, Pallas kernels, body(): pl.pallas_call(right_stats_kernel, grid_spec=pltpu.PrefetchScalarGridSpec...  5.43 us
  transfers between devices with their start and end apart: 21, of which 5 were waited for; matrix products, arithmetic and copies ran while one was open for 2% of the time, Pallas kernels for 21%

commit v1 on v0

v1 whole, which is shorter than its diff:
```python
import jax
import jax.numpy as jnp
from jax import lax
from jax.experimental import pallas as pl
from jax.experimental.pallas import tpu as pltpu
from jax.sharding import PartitionSpec as P

D = 4096
FF = 20480
BLOCK = 256
HALF = 128
ITERS = 6
DAMPING = 0.001
ROWS = 8
COLS = 16
RIGHT = 5
SHARE = 2 * BLOCK // ROWS
SLOT = BLOCK + 8 + SHARE
EXTRA = 8 + SHARE
PACK = BLOCK + 8

f32 = jnp.float32
bf16 = jnp.bfloat16

def swap(value, d):
    return lax.ppermute(value, "col", [(i, i ^ d) for i in range(COLS)])


def exchanged(slots):
    return lax.all_to_all(slots, "row", split_axis=0, concat_axis=0, tiled=True)


def parts(value):
    high = value.astype(bf16)
    return high, (value - high.astype(f32)).astype(bf16)


def dot(left, right, dims=((1,), (0,))):
    return lax.dot_general(left, right, (dims, ((), ())), preferred_element_type=f32)


def product(left, right, dims=((1,), (0,))):
    (lh, ll), (rh, rl) = left, right
    return dot(lh, rh, dims) + (dot(lh, rl, dims) + dot(ll, rh, dims))


def iotas(n):
    return (
        lax.broadcasted_iota(jnp.int32, (n, n), 0),
        lax.broadcasted_iota(jnp.int32, (n, n), 1),
    )


def packed_parts(block):
    i, j = iotas(HALF)
    first, last = block[:HALF, :HALF], block[HALF:, HALF:]
    quarters = jnp.concatenate([block[:HALF, HALF:], jnp.where(i >= j, first, last)], axis=0)
    return quarters, jnp.sum(jnp.where(i == j, last, 0.0), axis=0, keepdims=True)


def packed_gram(even, odd):
    i, j = iotas(HALF)
    first, last = odd[:HALF, :HALF], odd[HALF:, HALF:]
    upper = even[:HALF, HALF:] + odd[:HALF, HALF:] + odd[HALF:, :HALF].T
    mixed = jnp.where(i >= j, even[:HALF, :HALF] + first, even[HALF:, HALF:] + last)
    mixed = mixed + jnp.where(i <= j, first, last).T
    diagonal = jnp.sum(jnp.where(i == j, even[HALF:, HALF:] + 2.0 * last, 0.0), axis=0, keepdims=True)
    return jnp.concatenate([upper, mixed], axis=0), diagonal


def store_packed(ref, start, block):
    quarters, diagonal = packed_parts(block)
    ref[pl.ds(start, BLOCK), :] = quarters
    ref[pl.ds(start + BLOCK, 8), :] = jnp.broadcast_to(diagonal, (8, HALF))


def unpacked(packed, diagonal=None):
    i, j = iotas(HALF)
    upper, mixed = packed[:HALF], packed[HALF:BLOCK]
    if diagonal is None:
        diagonal = packed[BLOCK : BLOCK + 1]
    turned = mixed.T
    first = jnp.where(i >= j, mixed, turned)
    last = jnp.where(i < j, mixed, jnp.where(i == j, jnp.broadcast_to(diagonal, (HALF, HALF)), turned))
    return jnp.concatenate(
        [
            jnp.concatenate([first, upper], axis=1),
            jnp.concatenate([upper.T, last], axis=1),
        ],
        axis=0,
    )


def roots(statistics):
    i, j = iotas(BLOCK)
    identity = jnp.where(i == j, 1.0, 0.0).astype(f32)
    currents, scaleds = [], []
    for statistic in statistics:
        damped = statistic + DAMPING * identity
        norm = jnp.sqrt(jnp.sum(damped * damped, axis=(0, 1), keepdims=True))
        currents.append(lax.rsqrt(jnp.sqrt(norm)))
        scaleds.append(damped / norm)
    for iteration in range(ITERS):
        factors = [(5.0 * identity - scaled) * 0.25 for scaled in scaleds]
        split = [parts(factor) for factor in factors]
        if iteration == 0:
            currents = [current * factor for current, factor in zip(currents, factors)]
        else:
            currents = [product(parts(current), fs) for current, fs in zip(currents, split)]
        if iteration < ITERS - 1:
            squares = [parts(product(fs, fs)) for fs in split]
            fourths = [parts(product(sq, sq)) for sq in squares]
            scaleds = [product(fo, parts(scaled)) for fo, scaled in zip(fourths, scaleds)]
    return currents


def fetched(sources, buffer, sems):
    tiles = []
    for b in range(RIGHT):
        columns = pl.ds(b * BLOCK, BLOCK)
        tiles.append(
            [
                pltpu.make_async_copy(source.at[:, columns], buffer.at[s, b], sems.at[s, b])
                for s, source in enumerate(sources)
            ]
        )
    for copies in tiles:
        for copy in copies:
            copy.start()
    return tiles


def right_stats_kernel(first, second, out, buffer, sems):
    tiles = fetched((first, second), buffer, sems)
    half = ROWS // 2
    for b in range(RIGHT):
        total = None
        for s in range(2):
            tiles[b][s].wait()
            high, low = parts(buffer[s, b])
            gram = dot(high, jnp.concatenate([high, low], axis=1), ((0,), (0,))) * (1.0 / D)
            gram = packed_gram(gram[:, :BLOCK], gram[:, BLOCK:])
            total = gram if s == 0 else (total[0] + gram[0], total[1] + gram[1])
            if b < RIGHT - 1:
                out[2 * b + s, :BLOCK, :] = total[0]
                out[2 * b + s, BLOCK : BLOCK + 1, :] = total[1]
            else:
                out[s * half : (s + 1) * half, BLOCK + 8 :, :] = total[0].reshape(half, SHARE, HALF)
                for slot in range(ROWS):
                    out[slot, BLOCK + 1 + s : BLOCK + 2 + s, :] = total[1]
    for slot in range(ROWS):
        out[slot, BLOCK + 3 : BLOCK + 8, :] = jnp.zeros((5, HALF), f32)


def left_stats_kernel(info, first, second, keep, send, buffer, sums, sems):
    core = info[0]
    tiles = fetched((first, second), buffer, sems)
    for b in range(RIGHT):
        for s in range(2):
            tiles[b][s].wait()
            for block in range(2):
                high, low = parts(buffer[s, b, block * BLOCK : (block + 1) * BLOCK, :])
                gram = dot(high, jnp.concatenate([high, low], axis=0), ((1,), (1,)))
                if b == 0:
                    sums[block, s] = gram
                else:
                    sums[block, s] += gram
    for out, block in ((keep, core), (send, 1 - core)):
        total = None
        for s in range(2):
            gram = sums[block, s] * (1.0 / FF)
            gram = packed_gram(gram[:, :BLOCK], gram[:, BLOCK:])
            total = gram if s == 0 else (total[0] + gram[0], total[1] + gram[1])
            out[s * PACK : s * PACK + BLOCK, :] = total[0]
            out[s * PACK + BLOCK : (s + 1) * PACK, :] = jnp.broadcast_to(total[1], (8, HALF))


def share_kernel(arrived, out, buffer, sem):
    copy = pltpu.make_async_copy(arrived.at[:, pl.ds(BLOCK, EXTRA), :], buffer, sem)
    copy.start()
    copy.wait()
    total = buffer[0]
    for slot in range(1, ROWS):
        total = total + buffer[slot]
    for slot in range(ROWS):
        out[slot] = total


def roots_kernel(arrived, left_own, left_other, right_out, left_out, buffer, sems):
    copies = [
        pltpu.make_async_copy(arrived.at[slot, pl.ds(0, PACK), :], buffer.at[slot], sems.at[slot])
        for slot in range(ROWS)
    ]
    for copy in copies:
        copy.start()
    left_total = left_own[...] + left_other[...]
    copies[0].wait()
    total = buffer[0]
    for slot in range(1, ROWS):
        copies[slot].wait()
        total = total + buffer[slot]
    right_root, left_root = roots([unpacked(total), unpacked(left_total)])
    quarters, diagonal = packed_parts(right_root)
    for slot in range(ROWS):
        right_out[slot, :BLOCK, :] = quarters
        right_out[slot, BLOCK:, :] = jnp.broadcast_to(diagonal, (8, HALF))
    store_packed(left_out, 0, left_root)


def shared_roots_kernel(gathered, out):
    half = ROWS // 2
    statistics = [
        unpacked(
            gathered[s * half : (s + 1) * half, 8:, :].reshape(BLOCK, HALF), gathered[0, 1 + s : 2 + s, :]
        )
        for s in range(2)
    ]
    for s, root in enumerate(roots(statistics)):
        out[s] = root


def halfway_kernel(info, first, second, mine, other, out, buffer, results, sems, out_sems):
    core = info[0]
    tiles = fetched((first, second), buffer, sems)
    split = [[parts(unpacked(ref[s * PACK : (s + 1) * PACK, :])) for s in range(2)] for ref in (mine, other)]
    copies = []
    for b in range(RIGHT):
        for s in range(2):
            tiles[b][s].wait()
            for place, block in enumerate((core, 1 - core)):
                rows = pl.ds(pl.multiple_of(block * BLOCK, BLOCK), BLOCK)
                result = product(split[place][s], parts(buffer[s, b, rows, :]))
                results[b, 2 * s, rows, :], results[b, 2 * s + 1, rows, :] = parts(result)
        copy = pltpu.make_async_copy(results.at[b], out.at[b], out_sems.at[b])
        copy.start()
        copies.append(copy)
    for copy in copies:
        copy.wait()


def apply_kernel(halfway, gathered, shared, out, held, roots_in, buffer, sems, root_sems, out_sems):
    order = (RIGHT - 1, *range(RIGHT - 1))
    fetches = []
    for b in order:
        fetches.append([pltpu.make_async_copy(halfway.at[b], held.at[b], sems.at[b])])
        if b < RIGHT - 1:
            fetches[-1].append(
                pltpu.make_async_copy(gathered.at[pl.ds(2 * b, 2)], roots_in.at[pl.ds(2 * b, 2)], root_sems.at[b])
            )
        for copy in fetches[-1]:
            copy.start()
    copies = []
    for b, fetch in zip(order, fetches):
        for copy in fetch:
            copy.wait()
        if b == RIGHT - 1:
            one, two = parts(shared[0]), parts(shared[1])
        else:
            one, two = parts(unpacked(roots_in[2 * b])), parts(unpacked(roots_in[2 * b + 1]))
        buffer[b] = product((held[b, 0], held[b, 1]), one) + product((held[b, 2], held[b, 3]), two)
        copy = pltpu.make_async_copy(buffer.at[b], out.at[:, pl.ds(b * BLOCK, BLOCK)], out_sems.at[b])
        copy.start()
        copies.append(copy)
    for copy in copies:
        copy.wait()


VMEM = pl.BlockSpec(memory_space=pltpu.VMEM)
SMEM = pl.BlockSpec(memory_space=pltpu.SMEM)
HBM = pl.BlockSpec(memory_space=pltpu.HBM)
ANY = pl.BlockSpec(memory_space=pl.ANY)


def in_hbm(*values):
    return [pltpu.with_memory_space_constraint(value, pltpu.HBM) for value in values]


def params():
    return pltpu.CompilerParams(vmem_limit_bytes=32 * 1024 * 1024)


def cost(flops, moved):
    return pl.CostEstimate(flops=int(flops), bytes_accessed=int(moved), transcendentals=0)


def body(grad_first, grad_second):
    rows, cols = grad_first.shape
    col = lax.axis_index("col")
    core = lax.rem(col, 2)
    low_y = lax.rem(col // 4, 2)
    info = core.reshape(1).astype(jnp.int32)
    pair = jax.ShapeDtypeStruct((2 * PACK, HALF), f32)
    single = jax.ShapeDtypeStruct((PACK, HALF), f32)
    grads = 2 * rows * cols * 4
    passes = 3 * 2 * BLOCK * rows * cols * 2
    newton = 20 * 6 * BLOCK**3
    tiles = [pltpu.VMEM((2, RIGHT, rows, BLOCK), f32)]
    tile_sems = [pltpu.SemaphoreType.DMA((2, RIGHT))]

    right_parts = pl.pallas_call(
        right_stats_kernel,
        in_specs=[HBM, HBM],
        out_specs=VMEM,
        out_shape=jax.ShapeDtypeStruct((ROWS, SLOT, HALF), f32),
        scratch_shapes=tiles + tile_sems,
        compiler_params=params(),
        cost_estimate=cost(passes, grads),
        name="right_stats",
    )(*in_hbm(grad_first, grad_second))
    arrived = exchanged(right_parts)

    info, right_parts = lax.optimization_barrier((info, right_parts))
    keep, send = pl.pallas_call(
        left_stats_kernel,
        in_specs=[SMEM, HBM, HBM],
        out_specs=[VMEM, VMEM],
        out_shape=[pair, pair],
        scratch_shapes=tiles + [pltpu.VMEM((2, 2, BLOCK, 2 * BLOCK), f32)] + tile_sems,
        compiler_params=params(),
        cost_estimate=cost(passes, grads),
        name="left_stats",
    )(info, *in_hbm(grad_first, grad_second))
    both = (keep + swap(send, 1)).reshape(2, PACK, HALF)
    own = lax.dynamic_index_in_dim(both, low_y, 0, keepdims=False)
    rest = lax.dynamic_index_in_dim(both, 1 - low_y, 0, keepdims=False)
    own = (own + swap(rest, 4)) + (swap(own, 8) + swap(rest, 12))
    left_in = [own, swap(own, 2)]

    shares = exchanged(
        pl.pallas_call(
            share_kernel,
            in_specs=[ANY],
            out_specs=VMEM,
            out_shape=jax.ShapeDtypeStruct((ROWS, EXTRA, HALF), f32),
            scratch_shapes=[pltpu.VMEM((ROWS, EXTRA, HALF), f32), pltpu.SemaphoreType.DMA(())],
            compiler_params=params(),
            cost_estimate=cost(0, 2 * ROWS * EXTRA * HALF * 4),
            name="share",
        )(arrived)
    )
    right_root, left_root = pl.pallas_call(
        roots_kernel,
        in_specs=[ANY] + [VMEM] * 2,
        out_specs=[VMEM, VMEM],
        out_shape=[jax.ShapeDtypeStruct((ROWS, PACK, HALF), f32), single],
        scratch_shapes=[pltpu.VMEM((ROWS, PACK, HALF), f32), pltpu.SemaphoreType.DMA((ROWS,))],
        compiler_params=params(),
        cost_estimate=cost(2 * newton, 2 * ROWS * PACK * HALF * 4),
        name="roots",
    )(arrived, *left_in)
    gathered = exchanged(right_root)

    left_other = swap(left_root, 4)
    mine = jnp.where(
        low_y == 0,
        jnp.concatenate([left_root, left_other]),
        jnp.concatenate([left_other, left_root]),
    )
    other = swap(mine, 1)
    shared = pl.pallas_call(
        shared_roots_kernel,
        in_specs=[VMEM],
        out_specs=VMEM,
        out_shape=jax.ShapeDtypeStruct((2, BLOCK, BLOCK), f32),
        compiler_params=params(),
        cost_estimate=cost(2 * newton, 4 * PACK * HALF * 4),
        name="shared_roots",
    )(shares)

    held = (RIGHT, 4, rows, BLOCK)
    tile_sem = pltpu.SemaphoreType.DMA((RIGHT,))
    halfway = pl.pallas_call(
        halfway_kernel,
        in_specs=[SMEM, HBM, HBM, VMEM, VMEM],
        out_specs=HBM,
        out_shape=pltpu.HBM(held, bf16),
        scratch_shapes=tiles + [pltpu.VMEM(held, bf16)] + tile_sems + [tile_sem],
        compiler_params=params(),
        cost_estimate=cost(passes, 2 * grads),
        name="halfway",
    )(info, *in_hbm(grad_first, grad_second), mine, other)

    return pl.pallas_call(
        apply_kernel,
        in_specs=[HBM, ANY, VMEM],
        out_specs=HBM,
        scratch_shapes=[
            pltpu.VMEM(held, bf16),
            pltpu.VMEM((ROWS, PACK, HALF), f32),
            pltpu.VMEM((RIGHT, rows, BLOCK), f32),
            tile_sem,
            tile_sem,
            tile_sem,
        ],
        out_shape=jax.ShapeDtypeStruct((rows, cols), f32),
        compiler_params=params(),
        cost_estimate=cost(passes, 2 * grads),
        name="apply",
    )(*in_hbm(halfway), gathered, shared)


def solution(mesh):
    in_specs = (P("row", "col"), P("row", "col"))
    out_specs = P("row", "col")
    return jax.shard_map(body, mesh=mesh, in_specs=in_specs, out_specs=out_specs, check_vma=False)
```

time: 110 us -> 79.8 us (0.73)
  the two profiles are of different devices: /device:TPU:4 before, /device:TPU:1 now
where the time goes in v1:
time: 79.8 us; the launch traced here: 79.5 us
  Pallas kernels  39.7 us (50%)
  starting transfers between devices  28.3 us (35%)
  waiting for transfers between devices  11.1 us (14%)
    all_to_all x3, starting transfers between devices, exchanged(): return lax.all_to_all(slots, 'row', split_axis=0, concat_axis=0, tiled=True)  16.8 us
    ppermute x7, starting transfers between devices, swap(): return lax.ppermute(value, 'col', [(i, i ^ d) for i in range(COLS)])  11.5 us
    ppermute x7, waiting for transfers between devices, swap(): return lax.ppermute(value, 'col', [(i, i ^ d) for i in range(COLS)])  11.1 us
    pallas_call x1, Pallas kernels, body(): pl.pallas_call(roots_kernel, in_specs=[ANY] + [VMEM] * 2, out_specs=[VMEM...  9.06 us
    pallas_call x1, Pallas kernels, body(): pl.pallas_call(apply_kernel, in_specs=[HBM, ANY, VMEM], out_specs=HBM, sc...  6.93 us
    pallas_call x1, Pallas kernels, body(): pl.pallas_call(shared_roots_kernel, in_specs=[VMEM], out_specs=VMEM, out_...  6.5 us
    pallas_call x1, Pallas kernels, body(): pl.pallas_call(halfway_kernel, in_specs=[SMEM, HBM, HBM, VMEM, VMEM], out...  6.32 us
    pallas_call x1, Pallas kernels, body(): pl.pallas_call(right_stats_kernel, in_specs=[HBM, HBM], out_specs=VMEM, o...  6.22 us
  transfers between devices with their start and end apart: 10, of which 5 were waited for; matrix products, arithmetic and copies ran while one was open for 0% of the time, Pallas kernels for 33%

profile of v1, /device:TPU:1, one launch (start us, length us, event | category | flops | bytes accessed | tf_op | source)
XLA Modules:
  0.0 79.5 jit_solution(15696447628436573627)
XLA Ops:
  0.0 6.2 %right_stats.1 = f32[8,328,128]{2,1,0:T(8,128)} custom-call(f32[512,1280]{1,0:T(8,128)} %first.5, f32[512,1280]{1,0:T(8,128)} %second.5), custom_call_target="tpu_custom_call" | custom-call | flops 2013265920 | bytes 5242880 | tf_op jit(solution)/shard_map/right_stats/pallas_call | solution.py:300
  6.2 6.8 %all-to-all-start = ((f32[8,328,128]{2,1,0:T(8,128)}), f32[8,328,128]{2,1,0:T(8,128)S(1)}, u32[]{:S(2)}, u32[]{:S(2)}) async-start(f32[8,328,128]{2,1,0:T(8,128)} %right_stats.1), calls=%async_computation | async-start | bytes 2686976 | tf_op jit(solution)/shard_map/all_to_all | solution.py:30
  13.0 3.9 %left_stats.1 = (f32[528,128]{1,0:T(8,128)S(1)}, f32[528,128]{1,0:T(8,128)S(1)}) custom-call(s32[1]{0:T(128)} %bitcast.info, f32[512,1280]{1,0:T(8,128)} %first.5, f32[512,1280]{1,0:T(8,128)} %second.5), custom_call_target="tpu_custom_call" | custom-call | flops 2013265920 | bytes 5242880 | tf_op jit(solution)/shard_map/left_stats/pallas_call | solution.py:313
  16.9 1.0 %collective-permute-start = (f32[528,128]{1,0:T(8,128)S(1)}, f32[528,128]{1,0:T(8,128)S(1)}, u32[]{:S(2)}, u32[]{:S(2)}) collective-permute-start(f32[528,128]{1,0:T(8,128)S(1)} %get-tuple-element.12), channel_id=1, source_target_pairs={{0,1},{1,0},{2,3},{3,2},{4,5},{5,4},{6,7},{7,6},{8,9},{9,8},{10,11... | collective-permute-start | bytes 811016 | tf_op jit(solution)/shard_map/ppermute | solution.py:26
  18.0 1.2 %collective-permute-done = f32[528,128]{1,0:T(8,128)S(1)} collective-permute-done((f32[528,128]{1,0:T(8,128)S(1)}, f32[528,128]{1,0:T(8,128)S(1)}, u32[]{:S(2)}, u32[]{:S(2)}) %collective-permute-start) | collective-permute-done | bytes 270368 | tf_op jit(solution)/shard_map/ppermute | solution.py:26
  19.2 2.8 %collective-permute-start.3 = (f32[264,128]{1,0:T(8,128)S(1)}, f32[264,128]{1,0:T(8,128)S(1)}, u32[]{:S(2)}, u32[]{:S(2)}) collective-permute-start(f32[264,128]{1,0:T(8,128)S(1)} %get-tuple-element.15), channel_id=1, source_target_pairs={{0,12},{1,13},{2,14},{3,15},{4,8},{5,9},{6,10},{7,11},{8,4},{9,5},... | collective-permute-start | bytes 405512 | tf_op jit(solution)/shard_map/ppermute | solution.py:26
  22.0 0.0 collective-permute-start.1
  22.0 1.3 %collective-permute-start.2 = (f32[264,128]{1,0:T(8,128)S(1)}, f32[264,128]{1,0:T(8,128)S(1)}, u32[]{:S(2)}, u32[]{:S(2)}) collective-permute-start(f32[264,128]{1,0:T(8,128)S(1)} %get-tuple-element.16), channel_id=1, source_target_pairs={{0,8},{1,9},{2,10},{3,11},{4,12},{5,13},{6,14},{7,15},{8,0},{9,1},... | collective-permute-start | bytes 405512 | tf_op jit(solution)/shard_map/ppermute | solution.py:26
  23.3 2.1 %collective-permute-done.3 = f32[264,128]{1,0:T(8,128)S(1)} collective-permute-done((f32[264,128]{1,0:T(8,128)S(1)}, f32[264,128]{1,0:T(8,128)S(1)}, u32[]{:S(2)}, u32[]{:S(2)}) %collective-permute-start.3) | collective-permute-done | bytes 135200 | tf_op jit(solution)/shard_map/ppermute | solution.py:26
  25.4 1.1 %collective-permute-done.1 = f32[264,128]{1,0:T(8,128)S(1)} collective-permute-done((f32[264,128]{1,0:T(8,128)S(1)}, f32[264,128]{1,0:T(8,128)S(1)}, u32[]{:S(2)}, u32[]{:S(2)}) %collective-permute-start.1) | collective-permute-done | bytes 135200 | tf_op jit(solution)/shard_map/ppermute | solution.py:26
  26.5 2.9 %collective-permute-done.2 = f32[264,128]{1,0:T(8,128)S(1)} collective-permute-done((f32[264,128]{1,0:T(8,128)S(1)}, f32[264,128]{1,0:T(8,128)S(1)}, u32[]{:S(2)}, u32[]{:S(2)}) %collective-permute-start.2) | collective-permute-done | bytes 135200 | tf_op jit(solution)/shard_map/ppermute | solution.py:26
  29.4 2.5 %collective-permute-start.4 = (f32[264,128]{1,0:T(8,128)S(1)}, f32[264,128]{1,0:T(8,128)S(1)}, u32[]{:S(2)}, u32[]{:S(2)}) collective-permute-start(f32[264,128]{1,0:T(8,128)S(1)} %add_add_fusion.left_own), channel_id=1, source_target_pairs={{0,2},{1,3},{2,0},{3,1},{4,6},{5,7},{6,4},{7,5},{8,10},{9,11},{10,... | collective-permute-start | bytes 405512 | tf_op jit(solution)/shard_map/ppermute | solution.py:26
  32.0 0.0 all-to-all-done.arrived
  32.0 0.8 share.1
  32.7 4.8 %all-to-all-start.2 = ((f32[8,72,128]{2,1,0:T(8,128)}), f32[8,72,128]{2,1,0:T(8,128)S(1)}, u32[]{:S(2)}, u32[]{:S(2)}) async-start(f32[8,72,128]{2,1,0:T(8,128)} %share.1), calls=%async_computation.2 | async-start | bytes 589824 | tf_op jit(solution)/shard_map/all_to_all | solution.py:30
  37.6 0.0 collective-permute-done.4.left_other
  37.6 9.1 %roots.1 = (f32[8,264,128]{2,1,0:T(8,128)}, f32[264,128]{1,0:T(8,128)S(1)}) custom-call(f32[8,328,128]{2,1,0:T(8,128)S(1)} %all-to-all-done.arrived, f32[264,128]{1,0:T(8,128)S(1)} %add_add_fusion.left_own, f32[264,128]{1,0:T(8,128)S(1)} %collective-permute-done.4.left_other), custom_call_target="tpu_custom_call" | custom-call | flops 4026531840 | bytes 2162688 | tf_op jit(solution)/shard_map/roots/pallas_call | solution.py:341
  46.6 0.0 all-to-all-done.2.gathered
  46.7 5.1 %all-to-all-start.1 = ((f32[8,264,128]{2,1,0:T(8,128)}), f32[8,264,128]{2,1,0:T(8,128)S(1)}, u32[]{:S(2)}, u32[]{:S(2)}) async-start(f32[8,264,128]{2,1,0:T(8,128)} %get-tuple-element.14), calls=%async_computation.1 | async-start | bytes 2162688 | tf_op jit(solution)/shard_map/all_to_all | solution.py:30
  51.8 0.0 collective-permute-start.5
  51.8 3.8 %collective-permute-done.5 = f32[264,128]{1,0:T(8,128)S(1)} collective-permute-done((f32[264,128]{1,0:T(8,128)S(1)}, f32[264,128]{1,0:T(8,128)S(1)}, u32[]{:S(2)}, u32[]{:S(2)}) %collective-permute-start.5) | collective-permute-done | bytes 135200 | tf_op jit(solution)/shard_map/ppermute | solution.py:26
  55.7 3.9 %collective-permute-start.6 = (f32[528,128]{1,0:T(8,128)S(1)}, f32[528,128]{1,0:T(8,128)S(1)}, u32[]{:S(2)}, u32[]{:S(2)}) collective-permute-start(f32[528,128]{1,0:T(8,128)S(1)} %maximum_select_fusion.mine), channel_id=1, source_target_pairs={{0,1},{1,0},{2,3},{3,2},{4,5},{5,4},{6,7},{7,6},{8,9},{9,8},{10,11... | collective-permute-start | bytes 811016 | tf_op jit(solution)/shard_map/ppermute | solution.py:26
  59.5 6.5 %shared_roots.1.shared = f32[2,256,256]{2,1,0:T(8,128)S(1)} custom-call(f32[8,72,128]{2,1,0:T(8,128)S(1)} %all-to-all-done.2.gathered), custom_call_target="tpu_custom_call" | custom-call | flops 4026531840 | bytes 540672 | tf_op jit(solution)/shard_map/shared_roots/pallas_call | solution.py:360
  66.1 0.0 collective-permute-done.6.other
  66.1 6.3 %halfway.1 = bf16[5,4,512,256]{3,2,1,0:T(8,128)(2,1)} custom-call(s32[1]{0:T(128)} %bitcast.info, f32[512,1280]{1,0:T(8,128)} %first.5, f32[512,1280]{1,0:T(8,128)} %second.5, f32[528,128]{1,0:T(8,128)S(1)} %maximum_select_fusion.mine, f32[528,128]{1,0:T(8,128)S(1)} %collective-permute-done.6.other), custom_call_target="tpu_custom_call" | custom-call | flops 2013265920 | bytes 10485760 | tf_op jit(solution)/shard_map/halfway/pallas_call | solution.py:372
  72.4 0.0 all-to-all-done.1.gathered
  72.4 6.9 %apply.1 = f32[512,1280]{1,0:T(8,128)} custom-call(bf16[5,4,512,256]{3,2,1,0:T(8,128)(2,1)} %halfway.1, f32[8,264,128]{2,1,0:T(8,128)S(1)} %all-to-all-done.1.gathered, f32[2,256,256]{2,1,0:T(8,128)S(1)} %shared_roots.1.shared), custom_call_target="tpu_custom_call" | custom-call | flops 2013265920 | bytes 10485760 | tf_op jit(solution)/shard_map/apply/pallas_call | solution.py:383
  (4 shorter events, 0.1 us)
Async XLA Ops:
  6.2 25.7 %all-to-all-start = ((f32[8,328,128]{2,1,0:T(8,128)}), f32[8,328,128]{2,1,0:T(8,128)S(1)}, u32[]{:S(2)}, u32[]{:S(2)}) async-start(f32[8,328,128]{2,1,0:T(8,128)} %right_stats.1), calls=%async_computation | async-start | bytes 2686976 | tf_op jit(solution)/shard_map/all_to_all | solution.py:30
  16.9 2.2 %collective-permute-start = (f32[528,128]{1,0:T(8,128)S(1)}, f32[528,128]{1,0:T(8,128)S(1)}, u32[]{:S(2)}, u32[]{:S(2)}) collective-permute-start(f32[528,128]{1,0:T(8,128)S(1)} %get-tuple-element.12), channel_id=1, source_target_pairs={{0,1},{1,0},{2,3},{3,2},{4,5},{5,4},{6,7},{7,6},{8,9},{9,8},{10,11... | collective-permute-start | bytes 811016 | tf_op jit(solution)/shard_map/ppermute | solution.py:26
  19.2 6.2 %collective-permute-start.3 = (f32[264,128]{1,0:T(8,128)S(1)}, f32[264,128]{1,0:T(8,128)S(1)}, u32[]{:S(2)}, u32[]{:S(2)}) collective-permute-start(f32[264,128]{1,0:T(8,128)S(1)} %get-tuple-element.15), channel_id=1, source_target_pairs={{0,12},{1,13},{2,14},{3,15},{4,8},{5,9},{6,10},{7,11},{8,4},{9,5},... | collective-permute-start | bytes 405512 | tf_op jit(solution)/shard_map/ppermute | solution.py:26
  22.0 4.5 %collective-permute-start.1 = (f32[264,128]{1,0:T(8,128)S(1)}, f32[264,128]{1,0:T(8,128)S(1)}, u32[]{:S(2)}, u32[]{:S(2)}) collective-permute-start(f32[264,128]{1,0:T(8,128)S(1)} %get-tuple-element.15), channel_id=1, source_target_pairs={{0,4},{1,5},{2,6},{3,7},{4,0},{5,1},{6,2},{7,3},{8,12},{9,13},{10,... | collective-permute-start | bytes 405512 | tf_op jit(solution)/shard_map/ppermute | solution.py:26
  22.0 7.4 %collective-permute-start.2 = (f32[264,128]{1,0:T(8,128)S(1)}, f32[264,128]{1,0:T(8,128)S(1)}, u32[]{:S(2)}, u32[]{:S(2)}) collective-permute-start(f32[264,128]{1,0:T(8,128)S(1)} %get-tuple-element.16), channel_id=1, source_target_pairs={{0,8},{1,9},{2,10},{3,11},{4,12},{5,13},{6,14},{7,15},{8,0},{9,1},... | collective-permute-start | bytes 405512 | tf_op jit(solution)/shard_map/ppermute | solution.py:26
  29.4 8.1 %collective-permute-start.4 = (f32[264,128]{1,0:T(8,128)S(1)}, f32[264,128]{1,0:T(8,128)S(1)}, u32[]{:S(2)}, u32[]{:S(2)}) collective-permute-start(f32[264,128]{1,0:T(8,128)S(1)} %add_add_fusion.left_own), channel_id=1, source_target_pairs={{0,2},{1,3},{2,0},{3,1},{4,6},{5,7},{6,4},{7,5},{8,10},{9,11},{10,... | collective-permute-start | bytes 405512 | tf_op jit(solution)/shard_map/ppermute | solution.py:26
  32.7 13.9 %all-to-all-start.2 = ((f32[8,72,128]{2,1,0:T(8,128)}), f32[8,72,128]{2,1,0:T(8,128)S(1)}, u32[]{:S(2)}, u32[]{:S(2)}) async-start(f32[8,72,128]{2,1,0:T(8,128)} %share.1), calls=%async_computation.2 | async-start | bytes 589824 | tf_op jit(solution)/shard_map/all_to_all | solution.py:30
  46.7 25.7 %all-to-all-start.1 = ((f32[8,264,128]{2,1,0:T(8,128)}), f32[8,264,128]{2,1,0:T(8,128)S(1)}, u32[]{:S(2)}, u32[]{:S(2)}) async-start(f32[8,264,128]{2,1,0:T(8,128)} %get-tuple-element.14), calls=%async_computation.1 | async-start | bytes 2162688 | tf_op jit(solution)/shard_map/all_to_all | solution.py:30
  51.8 3.9 %collective-permute-start.5 = (f32[264,128]{1,0:T(8,128)S(1)}, f32[264,128]{1,0:T(8,128)S(1)}, u32[]{:S(2)}, u32[]{:S(2)}) collective-permute-start(f32[264,128]{1,0:T(8,128)S(1)} %get-tuple-element.13), channel_id=1, source_target_pairs={{0,4},{1,5},{2,6},{3,7},{4,0},{5,1},{6,2},{7,3},{8,12},{9,13},{10,... | collective-permute-start | bytes 405512 | tf_op jit(solution)/shard_map/ppermute | solution.py:26
  55.7 10.4 %collective-permute-start.6 = (f32[528,128]{1,0:T(8,128)S(1)}, f32[528,128]{1,0:T(8,128)S(1)}, u32[]{:S(2)}, u32[]{:S(2)}) collective-permute-start(f32[528,128]{1,0:T(8,128)S(1)} %maximum_select_fusion.mine), channel_id=1, source_target_pairs={{0,1},{1,0},{2,3},{3,2},{4,5},{5,4},{6,7},{7,6},{8,9},{9,8},{10,11... | collective-permute-start | bytes 811016 | tf_op jit(solution)/shard_map/ppermute | solution.py:26

commit v2 on v1

--- a/solution.py
+++ b/solution.py
@@ -16,7 +16,6 @@
 RIGHT = 5
 SHARE = 2 * BLOCK // ROWS
 SLOT = BLOCK + 8 + SHARE
-EXTRA = 8 + SHARE
 PACK = BLOCK + 8
 
 f32 = jnp.float32
@@ -91,7 +90,7 @@
     )
 
 
-def roots(statistics):
+def root_steps(statistics, found):
     i, j = iotas(BLOCK)
     identity = jnp.where(i == j, 1.0, 0.0).astype(f32)
     currents, scaleds = [], []
@@ -103,15 +102,26 @@
     for iteration in range(ITERS):
         factors = [(5.0 * identity - scaled) * 0.25 for scaled in scaleds]
         split = [parts(factor) for factor in factors]
+        if iteration == ITERS - 1:
+            found.extend(product(parts(current), fs) for current, fs in zip(currents, split))
+            return
+        squares = [parts(product(fs, fs)) for fs in split]
+        yield
         if iteration == 0:
             currents = [current * factor for current, factor in zip(currents, factors)]
         else:
             currents = [product(parts(current), fs) for current, fs in zip(currents, split)]
-        if iteration < ITERS - 1:
-            squares = [parts(product(fs, fs)) for fs in split]
-            fourths = [parts(product(sq, sq)) for sq in squares]
-            scaleds = [product(fo, parts(scaled)) for fo, scaled in zip(fourths, scaleds)]
-    return currents
+        fourths = [parts(product(sq, sq)) for sq in squares]
+        yield
+        scaleds = [product(fo, parts(scaled)) for fo, scaled in zip(fourths, scaleds)]
+        yield
+
+
+def roots(statistics):
+    found = []
+    for _ in root_steps(statistics, found):
+        pass
+    return found
 
 
 def fetched(sources, buffer, sems):
@@ -175,48 +185,28 @@
             out[s * PACK + BLOCK : (s + 1) * PACK, :] = jnp.broadcast_to(total[1], (8, HALF))
 
 
-def share_kernel(arrived, out, buffer, sem):
-    copy = pltpu.make_async_copy(arrived.at[:, pl.ds(BLOCK, EXTRA), :], buffer, sem)
-    copy.start()
-    copy.wait()
-    total = buffer[0]
-    for slot in range(1, ROWS):
-        total = total + buffer[slot]
-    for slot in range(ROWS):
-        out[slot] = total
-
-
-def roots_kernel(arrived, left_own, left_other, right_out, left_out, buffer, sems):
-    copies = [
-        pltpu.make_async_copy(arrived.at[slot, pl.ds(0, PACK), :], buffer.at[slot], sems.at[slot])
-        for slot in range(ROWS)
-    ]
+def right_roots_kernel(arrived, right_out, diagonals, buffer, sems):
+    copies = [pltpu.make_async_copy(arrived.at[slot], buffer.at[slot], sems.at[slot]) for slot in range(ROWS)]
     for copy in copies:
         copy.start()
-    left_total = left_own[...] + left_other[...]
     copies[0].wait()
     total = buffer[0]
     for slot in range(1, ROWS):
         copies[slot].wait()
         total = total + buffer[slot]
-    right_root, left_root = roots([unpacked(total), unpacked(left_total)])
-    quarters, diagonal = packed_parts(right_root)
+    for slot in range(ROWS):
+        right_out[slot, PACK:, :] = total[PACK:]
+    diagonals[...] = total[BLOCK:PACK]
+    (root,) = roots([unpacked(total[:PACK])])
+    quarters, diagonal = packed_parts(root)
     for slot in range(ROWS):
         right_out[slot, :BLOCK, :] = quarters
-        right_out[slot, BLOCK:, :] = jnp.broadcast_to(diagonal, (8, HALF))
-    store_packed(left_out, 0, left_root)
-
-
-def shared_roots_kernel(gathered, out):
-    half = ROWS // 2
-    statistics = [
-        unpacked(
-            gathered[s * half : (s + 1) * half, 8:, :].reshape(BLOCK, HALF), gathered[0, 1 + s : 2 + s, :]
-        )
-        for s in range(2)
-    ]
-    for s, root in enumerate(roots(statistics)):
-        out[s] = root
+        right_out[slot, BLOCK:PACK, :] = jnp.broadcast_to(diagonal, (8, HALF))
+
+
+def left_root_kernel(own, other, out):
+    (root,) = roots([unpacked(own[...] + other[...])])
+    store_packed(out, 0, root)
 
 
 def halfway_kernel(info, first, second, mine, other, out, buffer, results, sems, out_sems):
@@ -238,29 +228,66 @@
         copy.wait()
 
 
-def apply_kernel(halfway, gathered, shared, out, held, roots_in, buffer, sems, root_sems, out_sems):
-    order = (RIGHT - 1, *range(RIGHT - 1))
+def applied(held, b, one, two, buffer):
+    (h1, l1), (h2, l2) = one, two
+    weights = jnp.concatenate([h1, h1, l1, h2, h2, l2], axis=0)
+    for start in (0, BLOCK):
+        rows = slice(start, start + BLOCK)
+        high_one, low_one, high_two, low_two = [held[b, q, rows, :] for q in range(4)]
+        lhs = jnp.concatenate([low_one, high_one, high_one, low_two, high_two, high_two], axis=1)
+        buffer[b, rows, :] = dot(lhs, weights)
+        yield
+
+
+def finish_kernel(
+    halfway, gathered, diagonals, out, held, roots_in, shares, buffer, sems, root_sems, share_sem, out_sems
+):
+    share_copy = pltpu.make_async_copy(gathered.at[:, pl.ds(PACK, SHARE), :], shares, share_sem)
+    share_copy.start()
     fetches = []
-    for b in order:
-        fetches.append([pltpu.make_async_copy(halfway.at[b], held.at[b], sems.at[b])])
+    for b in range(RIGHT):
+        fetches.append([])
         if b < RIGHT - 1:
-            fetches[-1].append(
-                pltpu.make_async_copy(gathered.at[pl.ds(2 * b, 2)], roots_in.at[pl.ds(2 * b, 2)], root_sems.at[b])
+            pair = pl.ds(2 * b, 2)
+            fetches[b].append(
+                pltpu.make_async_copy(
+                    gathered.at[pair, pl.ds(0, PACK), :], roots_in.at[pair], root_sems.at[b]
+                )
             )
-        for copy in fetches[-1]:
+        fetches[b].append(pltpu.make_async_copy(halfway.at[b], held.at[b], sems.at[b]))
+        for copy in fetches[b]:
             copy.start()
+    half = ROWS // 2
+    share_copy.wait()
+    statistics = [
+        unpacked(shares[s * half : (s + 1) * half].reshape(BLOCK, HALF), diagonals[1 + s : 2 + s, :])
+        for s in range(2)
+    ]
+    found = []
+    chain = root_steps(statistics, found)
     copies = []
-    for b, fetch in zip(order, fetches):
-        for copy in fetch:
-            copy.wait()
-        if b == RIGHT - 1:
-            one, two = parts(shared[0]), parts(shared[1])
-        else:
-            one, two = parts(unpacked(roots_in[2 * b])), parts(unpacked(roots_in[2 * b + 1]))
-        buffer[b] = product((held[b, 0], held[b, 1]), one) + product((held[b, 2], held[b, 3]), two)
+
+    def stored(b):
         copy = pltpu.make_async_copy(buffer.at[b], out.at[:, pl.ds(b * BLOCK, BLOCK)], out_sems.at[b])
         copy.start()
         copies.append(copy)
+
+    next(chain)
+    for b in range(RIGHT - 1):
+        for copy in fetches[b]:
+            copy.wait()
+        one, two = parts(unpacked(roots_in[2 * b])), parts(unpacked(roots_in[2 * b + 1]))
+        for _ in applied(held, b, one, two, buffer):
+            next(chain, None)
+        stored(b)
+        next(chain, None)
+    for _ in chain:
+        pass
+    last = RIGHT - 1
+    fetches[last][0].wait()
+    for _ in applied(held, last, parts(found[0]), parts(found[1]), buffer):
+        pass
+    stored(last)
     for copy in copies:
         copy.wait()
 
@@ -324,32 +351,32 @@
     own = lax.dynamic_index_in_dim(both, low_y, 0, keepdims=False)
     rest = lax.dynamic_index_in_dim(both, 1 - low_y, 0, keepdims=False)
     own = (own + swap(rest, 4)) + (swap(own, 8) + swap(rest, 12))
+    own, arrived = lax.optimization_barrier((own, arrived))
     left_in = [own, swap(own, 2)]
 
-    shares = exchanged(
-        pl.pallas_call(
-            share_kernel,
-            in_specs=[ANY],
-            out_specs=VMEM,
-            out_shape=jax.ShapeDtypeStruct((ROWS, EXTRA, HALF), f32),
-            scratch_shapes=[pltpu.VMEM((ROWS, EXTRA, HALF), f32), pltpu.SemaphoreType.DMA(())],
-            compiler_params=params(),
-            cost_estimate=cost(0, 2 * ROWS * EXTRA * HALF * 4),
-            name="share",
-        )(arrived)
-    )
-    right_root, left_root = pl.pallas_call(
-        roots_kernel,
-        in_specs=[ANY] + [VMEM] * 2,
+    slots = jax.ShapeDtypeStruct((ROWS, SLOT, HALF), f32)
+    right_root, diagonals = pl.pallas_call(
+        right_roots_kernel,
+        in_specs=[ANY],
         out_specs=[VMEM, VMEM],
-        out_shape=[jax.ShapeDtypeStruct((ROWS, PACK, HALF), f32), single],
-        scratch_shapes=[pltpu.VMEM((ROWS, PACK, HALF), f32), pltpu.SemaphoreType.DMA((ROWS,))],
-        compiler_params=params(),
-        cost_estimate=cost(2 * newton, 2 * ROWS * PACK * HALF * 4),
-        name="roots",
-    )(arrived, *left_in)
+        out_shape=[slots, jax.ShapeDtypeStruct((8, HALF), f32)],
+        scratch_shapes=[pltpu.VMEM((ROWS, SLOT, HALF), f32), pltpu.SemaphoreType.DMA((ROWS,))],
+        compiler_params=params(),
+        cost_estimate=cost(newton, 2 * ROWS * SLOT * HALF * 4),
+        name="right_roots",
+    )(arrived)
+    left_in, right_root = lax.optimization_barrier((left_in, right_root))
     gathered = exchanged(right_root)
-
+    left_in, right_root = lax.optimization_barrier((left_in, right_root))
+    left_root = pl.pallas_call(
+        left_root_kernel,
+        in_specs=[VMEM, VMEM],
+        out_specs=VMEM,
+        out_shape=single,
+        compiler_params=params(),
+        cost_estimate=cost(newton, 3 * PACK * HALF * 4),
+        name="left_root",
+    )(*left_in)
     left_other = swap(left_root, 4)
     mine = jnp.where(
         low_y == 0,
@@ -357,15 +384,6 @@
         jnp.concatenate([left_other, left_root]),
     )
     other = swap(mine, 1)
-    shared = pl.pallas_call(
-        shared_roots_kernel,
-        in_specs=[VMEM],
-        out_specs=VMEM,
-        out_shape=jax.ShapeDtypeStruct((2, BLOCK, BLOCK), f32),
-        compiler_params=params(),
-        cost_estimate=cost(2 * newton, 4 * PACK * HALF * 4),
-        name="shared_roots",
-    )(shares)
 
     held = (RIGHT, 4, rows, BLOCK)
     tile_sem = pltpu.SemaphoreType.DMA((RIGHT,))
@@ -381,22 +399,24 @@
     )(info, *in_hbm(grad_first, grad_second), mine, other)
 
     return pl.pallas_call(
-        apply_kernel,
+        finish_kernel,
         in_specs=[HBM, ANY, VMEM],
         out_specs=HBM,
         scratch_shapes=[
             pltpu.VMEM(held, bf16),
             pltpu.VMEM((ROWS, PACK, HALF), f32),
+            pltpu.VMEM((ROWS, SHARE, HALF), f32),
             pltpu.VMEM((RIGHT, rows, BLOCK), f32),
             tile_sem,
             tile_sem,
+            pltpu.SemaphoreType.DMA(()),
             tile_sem,
         ],
         out_shape=jax.ShapeDtypeStruct((rows, cols), f32),
         compiler_params=params(),
-        cost_estimate=cost(passes, 2 * grads),
-        name="apply",
-    )(*in_hbm(halfway), gathered, shared)
+        cost_estimate=cost(passes + 2 * newton, 2 * grads),
+        name="finish",
+    )(*in_hbm(halfway), gathered, diagonals)
 
 
 def solution(mesh):

time: 79.8 us -> 75.2 us (0.942)
  starting transfers between devices: 28.3 us -> 21.9 us
  waiting for transfers between devices: 11.1 us -> 13 us
    all_to_all x3 -> x2, starting transfers between devices: 16.8 us -> 10.6 us  [exchanged(): return lax.all_to_all(slots, 'row', split_axis=0, concat_axis=0, tiled=True)]
    all_to_all x3 -> x2, waiting for transfers between devices: 0.01 us -> 1.68 us  [exchanged(): return lax.all_to_all(slots, 'row', split_axis=0, concat_axis=0, tiled=True)]
    pallas_call x4 -> x3, Pallas kernels: 23.2 us -> 23.4 us  [the longest x1 10 us: body(): pl.pallas_call(finish_kernel, in_specs=[HBM, ANY, VMEM], out_specs=HBM, s...]
  transfers between devices with their start and end apart: 10 -> 9, of which waited for: 5 -> 7; matrix products, arithmetic and copies ran while one was open for 0% -> 0% of each run, Pallas kernels for 33% -> 31%
where the time goes in v2:
time: 75.2 us; the launch traced here: 75 us
  Pallas kernels  39.8 us (53%)
  starting transfers between devices  21.9 us (29%)
  waiting for transfers between devices  13 us (17%)
    ppermute x7, starting transfers between devices, swap(): return lax.ppermute(value, 'col', [(i, i ^ d) for i in range(COLS)])  11.3 us
    ppermute x7, waiting for transfers between devices, swap(): return lax.ppermute(value, 'col', [(i, i ^ d) for i in range(COLS)])  11.3 us
    all_to_all x2, starting transfers between devices, exchanged(): return lax.all_to_all(slots, 'row', split_axis=0, concat_axis=0, tiled=True)  10.6 us
    pallas_call x1, Pallas kernels, body(): pl.pallas_call(finish_kernel, in_specs=[HBM, ANY, VMEM], out_specs=HBM, s...  10 us
    pallas_call x1, Pallas kernels, body(): pl.pallas_call(right_roots_kernel, in_specs=[ANY], out_specs=[VMEM, VMEM]...  8.14 us
    pallas_call x1, Pallas kernels, body(): pl.pallas_call(halfway_kernel, in_specs=[SMEM, HBM, HBM, VMEM, VMEM], out...  6.32 us
    pallas_call x1, Pallas kernels, body(): pl.pallas_call(right_stats_kernel, in_specs=[HBM, HBM], out_specs=VMEM, o...  6.22 us
    pallas_call x1, Pallas kernels, body(): pl.pallas_call(left_root_kernel, in_specs=[VMEM, VMEM], out_specs=VMEM, o...  5.23 us
  transfers between devices with their start and end apart: 9, of which 7 were waited for; matrix products, arithmetic and copies ran while one was open for 0% of the time, Pallas kernels for 31%

profile of v2, /device:TPU:1, one launch (start us, length us, event | category | flops | bytes accessed | tf_op | source)
XLA Modules:
  0.0 75.0 jit_solution(7311094263297680156)
XLA Ops:
  0.0 6.2 %right_stats.1 = f32[8,328,128]{2,1,0:T(8,128)} custom-call(f32[512,1280]{1,0:T(8,128)} %first.5, f32[512,1280]{1,0:T(8,128)} %second.5), custom_call_target="tpu_custom_call" | custom-call | flops 2013265920 | bytes 5242880 | tf_op jit(solution)/shard_map/right_stats/pallas_call | solution.py:327
  6.2 6.8 %all-to-all-start = ((f32[8,328,128]{2,1,0:T(8,128)}), f32[8,328,128]{2,1,0:T(8,128)S(1)}, u32[]{:S(2)}, u32[]{:S(2)}) async-start(f32[8,328,128]{2,1,0:T(8,128)} %right_stats.1), calls=%async_computation | async-start | bytes 2686976 | tf_op jit(solution)/shard_map/all_to_all | solution.py:29
  13.0 3.9 %left_stats.1 = (f32[528,128]{1,0:T(8,128)S(1)}, f32[528,128]{1,0:T(8,128)S(1)}) custom-call(s32[1]{0:T(128)} %bitcast.info, f32[512,1280]{1,0:T(8,128)} %first.5, f32[512,1280]{1,0:T(8,128)} %second.5), custom_call_target="tpu_custom_call" | custom-call | flops 2013265920 | bytes 5242880 | tf_op jit(solution)/shard_map/left_stats/pallas_call | solution.py:340
  16.9 1.0 %collective-permute-start = (f32[528,128]{1,0:T(8,128)S(1)}, f32[528,128]{1,0:T(8,128)S(1)}, u32[]{:S(2)}, u32[]{:S(2)}) collective-permute-start(f32[528,128]{1,0:T(8,128)S(1)} %get-tuple-element.21), channel_id=1, source_target_pairs={{0,1},{1,0},{2,3},{3,2},{4,5},{5,4},{6,7},{7,6},{8,9},{9,8},{10,11... | collective-permute-start | bytes 811016 | tf_op jit(solution)/shard_map/ppermute | solution.py:25
  18.0 1.2 %collective-permute-done = f32[528,128]{1,0:T(8,128)S(1)} collective-permute-done((f32[528,128]{1,0:T(8,128)S(1)}, f32[528,128]{1,0:T(8,128)S(1)}, u32[]{:S(2)}, u32[]{:S(2)}) %collective-permute-start) | collective-permute-done | bytes 270368 | tf_op jit(solution)/shard_map/ppermute | solution.py:25
  19.2 2.8 %collective-permute-start.3 = (f32[264,128]{1,0:T(8,128)S(1)}, f32[264,128]{1,0:T(8,128)S(1)}, u32[]{:S(2)}, u32[]{:S(2)}) collective-permute-start(f32[264,128]{1,0:T(8,128)S(1)} %get-tuple-element.31), channel_id=1, source_target_pairs={{0,12},{1,13},{2,14},{3,15},{4,8},{5,9},{6,10},{7,11},{8,4},{9,5},... | collective-permute-start | bytes 405512 | tf_op jit(solution)/shard_map/ppermute | solution.py:25
  22.0 0.0 collective-permute-start.1
  22.0 1.3 %collective-permute-start.2 = (f32[264,128]{1,0:T(8,128)S(1)}, f32[264,128]{1,0:T(8,128)S(1)}, u32[]{:S(2)}, u32[]{:S(2)}) collective-permute-start(f32[264,128]{1,0:T(8,128)S(1)} %get-tuple-element.32), channel_id=1, source_target_pairs={{0,8},{1,9},{2,10},{3,11},{4,12},{5,13},{6,14},{7,15},{8,0},{9,1},... | collective-permute-start | bytes 405512 | tf_op jit(solution)/shard_map/ppermute | solution.py:25
  23.3 2.1 %collective-permute-done.3 = f32[264,128]{1,0:T(8,128)S(1)} collective-permute-done((f32[264,128]{1,0:T(8,128)S(1)}, f32[264,128]{1,0:T(8,128)S(1)}, u32[]{:S(2)}, u32[]{:S(2)}) %collective-permute-start.3) | collective-permute-done | bytes 135200 | tf_op jit(solution)/shard_map/ppermute | solution.py:25
  25.4 1.1 %collective-permute-done.1 = f32[264,128]{1,0:T(8,128)S(1)} collective-permute-done((f32[264,128]{1,0:T(8,128)S(1)}, f32[264,128]{1,0:T(8,128)S(1)}, u32[]{:S(2)}, u32[]{:S(2)}) %collective-permute-start.1) | collective-permute-done | bytes 135200 | tf_op jit(solution)/shard_map/ppermute | solution.py:25
  26.5 2.9 %collective-permute-done.2 = f32[264,128]{1,0:T(8,128)S(1)} collective-permute-done((f32[264,128]{1,0:T(8,128)S(1)}, f32[264,128]{1,0:T(8,128)S(1)}, u32[]{:S(2)}, u32[]{:S(2)}) %collective-permute-start.2) | collective-permute-done | bytes 135200 | tf_op jit(solution)/shard_map/ppermute | solution.py:25
  29.4 1.7 %all-to-all-done.arrived = f32[8,328,128]{2,1,0:T(8,128)S(1)} async-done(((f32[8,328,128]{2,1,0:T(8,128)}), f32[8,328,128]{2,1,0:T(8,128)S(1)}, u32[]{:S(2)}, u32[]{:S(2)}) %all-to-all-start) | async-done | bytes 1343520 | tf_op jit(solution)/shard_map/all_to_all | solution.py:29
  31.1 2.4 %collective-permute-start.4 = (f32[264,128]{1,0:T(8,128)S(1)}, f32[264,128]{1,0:T(8,128)S(1)}, u32[]{:S(2)}, u32[]{:S(2)}) collective-permute-start(f32[264,128]{1,0:T(8,128)S(1)} %add_add_fusion.own), channel_id=1, source_target_pairs={{0,2},{1,3},{2,0},{3,1},{4,6},{5,7},{6,4},{7,5},{8,10},{9,11},{10,... | collective-permute-start | bytes 405512 | tf_op jit(solution)/shard_map/ppermute | solution.py:25
  33.6 8.1 %right_roots.1 = (f32[8,328,128]{2,1,0:T(8,128)}, f32[8,128]{1,0:T(8,128)S(1)}) custom-call(f32[8,328,128]{2,1,0:T(8,128)S(1)} %all-to-all-done.arrived), custom_call_target="tpu_custom_call" | custom-call | flops 2013265920 | bytes 2686976 | tf_op jit(solution)/shard_map/right_roots/pallas_call | solution.py:358
  41.7 0.0 collective-permute-done.4.other
  41.7 3.8 %all-to-all-start.1 = ((f32[8,328,128]{2,1,0:T(8,128)}), f32[8,328,128]{2,1,0:T(8,128)S(1)}, u32[]{:S(2)}, u32[]{:S(2)}) async-start(f32[8,328,128]{2,1,0:T(8,128)} %get-tuple-element.29), calls=%async_computation.1 | async-start | bytes 2686976 | tf_op jit(solution)/shard_map/all_to_all | solution.py:29
  45.5 5.2 %left_root.1 = f32[264,128]{1,0:T(8,128)S(1)} custom-call(f32[264,128]{1,0:T(8,128)S(1)} %add_add_fusion.own, f32[264,128]{1,0:T(8,128)S(1)} %collective-permute-done.4.other), custom_call_target="tpu_custom_call" | custom-call | flops 2013265920 | bytes 405504 | tf_op jit(solution)/shard_map/left_root/pallas_call | solution.py:371
  50.7 1.4 %collective-permute-start.5 = (f32[264,128]{1,0:T(8,128)S(1)}, f32[264,128]{1,0:T(8,128)S(1)}, u32[]{:S(2)}, u32[]{:S(2)}) collective-permute-start(f32[264,128]{1,0:T(8,128)S(1)} %left_root.1), channel_id=1, source_target_pairs={{0,4},{1,5},{2,6},{3,7},{4,0},{5,1},{6,2},{7,3},{8,12},{9,13},{10,... | collective-permute-start | bytes 405512 | tf_op jit(solution)/shard_map/ppermute | solution.py:25
  52.1 2.8 %collective-permute-done.5 = f32[264,128]{1,0:T(8,128)S(1)} collective-permute-done((f32[264,128]{1,0:T(8,128)S(1)}, f32[264,128]{1,0:T(8,128)S(1)}, u32[]{:S(2)}, u32[]{:S(2)}) %collective-permute-start.5) | collective-permute-done | bytes 135200 | tf_op jit(solution)/shard_map/ppermute | solution.py:25
  55.0 2.3 %collective-permute-start.6 = (f32[528,128]{1,0:T(8,128)S(1)}, f32[528,128]{1,0:T(8,128)S(1)}, u32[]{:S(2)}, u32[]{:S(2)}) collective-permute-start(f32[528,128]{1,0:T(8,128)S(1)} %maximum_select_fusion.mine), channel_id=1, source_target_pairs={{0,1},{1,0},{2,3},{3,2},{4,5},{5,4},{6,7},{7,6},{8,9},{9,8},{10,11... | collective-permute-start | bytes 811016 | tf_op jit(solution)/shard_map/ppermute | solution.py:25
  57.3 1.2 %collective-permute-done.6.other = f32[528,128]{1,0:T(8,128)S(1)} collective-permute-done((f32[528,128]{1,0:T(8,128)S(1)}, f32[528,128]{1,0:T(8,128)S(1)}, u32[]{:S(2)}, u32[]{:S(2)}) %collective-permute-start.6) | collective-permute-done | bytes 270368 | tf_op jit(solution)/shard_map/ppermute | solution.py:25
  58.5 6.3 %halfway.1 = bf16[5,4,512,256]{3,2,1,0:T(8,128)(2,1)} custom-call(s32[1]{0:T(128)} %bitcast.info, f32[512,1280]{1,0:T(8,128)} %first.5, f32[512,1280]{1,0:T(8,128)} %second.5, f32[528,128]{1,0:T(8,128)S(1)} %maximum_select_fusion.mine, f32[528,128]{1,0:T(8,128)S(1)} %collective-permute-done.6.other), custom_call_target="tpu_custom_call" | custom-call | flops 2013265920 | bytes 10485760 | tf_op jit(solution)/shard_map/halfway/pallas_call | solution.py:390
  64.8 0.0 all-to-all-done.1.gathered
  64.8 10.0 %finish.1 = f32[512,1280]{1,0:T(8,128)} custom-call(bf16[5,4,512,256]{3,2,1,0:T(8,128)(2,1)} %halfway.1, f32[8,328,128]{2,1,0:T(8,128)S(1)} %all-to-all-done.1.gathered, f32[8,128]{1,0:T(8,128)S(1)} %get-tuple-element.30.diagonals), custom_call_target="tpu_custom_call" | custom-call | flops 6039797760 | bytes 10485760 | tf_op jit(solution)/shard_map/finish/pallas_call | solution.py:401
  (4 shorter events, 0.1 us)
Async XLA Ops:
  6.2 24.9 %all-to-all-start = ((f32[8,328,128]{2,1,0:T(8,128)}), f32[8,328,128]{2,1,0:T(8,128)S(1)}, u32[]{:S(2)}, u32[]{:S(2)}) async-start(f32[8,328,128]{2,1,0:T(8,128)} %right_stats.1), calls=%async_computation | async-start | bytes 2686976 | tf_op jit(solution)/shard_map/all_to_all | solution.py:29
  16.9 2.2 %collective-permute-start = (f32[528,128]{1,0:T(8,128)S(1)}, f32[528,128]{1,0:T(8,128)S(1)}, u32[]{:S(2)}, u32[]{:S(2)}) collective-permute-start(f32[528,128]{1,0:T(8,128)S(1)} %get-tuple-element.21), channel_id=1, source_target_pairs={{0,1},{1,0},{2,3},{3,2},{4,5},{5,4},{6,7},{7,6},{8,9},{9,8},{10,11... | collective-permute-start | bytes 811016 | tf_op jit(solution)/shard_map/ppermute | solution.py:25
  19.2 6.2 %collective-permute-start.3 = (f32[264,128]{1,0:T(8,128)S(1)}, f32[264,128]{1,0:T(8,128)S(1)}, u32[]{:S(2)}, u32[]{:S(2)}) collective-permute-start(f32[264,128]{1,0:T(8,128)S(1)} %get-tuple-element.31), channel_id=1, source_target_pairs={{0,12},{1,13},{2,14},{3,15},{4,8},{5,9},{6,10},{7,11},{8,4},{9,5},... | collective-permute-start | bytes 405512 | tf_op jit(solution)/shard_map/ppermute | solution.py:25
  22.0 4.5 %collective-permute-start.1 = (f32[264,128]{1,0:T(8,128)S(1)}, f32[264,128]{1,0:T(8,128)S(1)}, u32[]{:S(2)}, u32[]{:S(2)}) collective-permute-start(f32[264,128]{1,0:T(8,128)S(1)} %get-tuple-element.31), channel_id=1, source_target_pairs={{0,4},{1,5},{2,6},{3,7},{4,0},{5,1},{6,2},{7,3},{8,12},{9,13},{10,... | collective-permute-start | bytes 405512 | tf_op jit(solution)/shard_map/ppermute | solution.py:25
  22.0 7.4 %collective-permute-start.2 = (f32[264,128]{1,0:T(8,128)S(1)}, f32[264,128]{1,0:T(8,128)S(1)}, u32[]{:S(2)}, u32[]{:S(2)}) collective-permute-start(f32[264,128]{1,0:T(8,128)S(1)} %get-tuple-element.32), channel_id=1, source_target_pairs={{0,8},{1,9},{2,10},{3,11},{4,12},{5,13},{6,14},{7,15},{8,0},{9,1},... | collective-permute-start | bytes 405512 | tf_op jit(solution)/shard_map/ppermute | solution.py:25
  31.1 10.6 %collective-permute-start.4 = (f32[264,128]{1,0:T(8,128)S(1)}, f32[264,128]{1,0:T(8,128)S(1)}, u32[]{:S(2)}, u32[]{:S(2)}) collective-permute-start(f32[264,128]{1,0:T(8,128)S(1)} %add_add_fusion.own), channel_id=1, source_target_pairs={{0,2},{1,3},{2,0},{3,1},{4,6},{5,7},{6,4},{7,5},{8,10},{9,11},{10,... | collective-permute-start | bytes 405512 | tf_op jit(solution)/shard_map/ppermute | solution.py:25
  41.7 23.1 %all-to-all-start.1 = ((f32[8,328,128]{2,1,0:T(8,128)}), f32[8,328,128]{2,1,0:T(8,128)S(1)}, u32[]{:S(2)}, u32[]{:S(2)}) async-start(f32[8,328,128]{2,1,0:T(8,128)} %get-tuple-element.29), calls=%async_computation.1 | async-start | bytes 2686976 | tf_op jit(solution)/shard_map/all_to_all | solution.py:29
  50.7 4.2 %collective-permute-start.5 = (f32[264,128]{1,0:T(8,128)S(1)}, f32[264,128]{1,0:T(8,128)S(1)}, u32[]{:S(2)}, u32[]{:S(2)}) collective-permute-start(f32[264,128]{1,0:T(8,128)S(1)} %left_root.1), channel_id=1, source_target_pairs={{0,4},{1,5},{2,6},{3,7},{4,0},{5,1},{6,2},{7,3},{8,12},{9,13},{10,... | collective-permute-start | bytes 405512 | tf_op jit(solution)/shard_map/ppermute | solution.py:25
  55.0 3.5 %collective-permute-start.6 = (f32[528,128]{1,0:T(8,128)S(1)}, f32[528,128]{1,0:T(8,128)S(1)}, u32[]{:S(2)}, u32[]{:S(2)}) collective-permute-start(f32[528,128]{1,0:T(8,128)S(1)} %maximum_select_fusion.mine), channel_id=1, source_target_pairs={{0,1},{1,0},{2,3},{3,2},{4,5},{5,4},{6,7},{7,6},{8,9},{9,8},{10,11... | collective-permute-start | bytes 811016 | tf_op jit(solution)/shard_map/ppermute | solution.py:25

commit v3 on v2

--- a/solution.py
+++ b/solution.py
@@ -38,9 +38,15 @@
     return lax.dot_general(left, right, (dims, ((), ())), preferred_element_type=f32)
 
 
-def product(left, right, dims=((1,), (0,))):
+def product(left, right):
     (lh, ll), (rh, rl) = left, right
-    return dot(lh, rh, dims) + (dot(lh, rl, dims) + dot(ll, rh, dims))
+    return dot(lh, rh) + (dot(lh, rl) + dot(ll, rh))
+
+
+def halves_product(left, right):
+    return jnp.concatenate(
+        [product([part[k : k + HALF] for part in left], right) for k in (0, HALF)], axis=0
+    )
 
 
 def iotas(n):
@@ -93,27 +99,35 @@
 def root_steps(statistics, found):
     i, j = iotas(BLOCK)
     identity = jnp.where(i == j, 1.0, 0.0).astype(f32)
-    currents, scaleds = [], []
+    currents, scaleds, squares = [], [], []
     for statistic in statistics:
         damped = statistic + DAMPING * identity
+        split = parts(damped)
+        square = halves_product(split, split)
         norm = jnp.sqrt(jnp.sum(damped * damped, axis=(0, 1), keepdims=True))
+        inverse = 1.0 / norm
+        scaled = damped * inverse
         currents.append(lax.rsqrt(jnp.sqrt(norm)))
-        scaleds.append(damped / norm)
+        scaleds.append(scaled)
+        squares.append(
+            parts((25.0 / 16.0) * identity - (10.0 / 16.0) * scaled + (square * inverse) * (inverse * (1.0 / 16.0)))
+        )
+    yield
     for iteration in range(ITERS):
         factors = [(5.0 * identity - scaled) * 0.25 for scaled in scaleds]
         split = [parts(factor) for factor in factors]
         if iteration == ITERS - 1:
-            found.extend(product(parts(current), fs) for current, fs in zip(currents, split))
+            found.extend(halves_product(parts(current), fs) for current, fs in zip(currents, split))
             return
-        squares = [parts(product(fs, fs)) for fs in split]
-        yield
         if iteration == 0:
             currents = [current * factor for current, factor in zip(currents, factors)]
         else:
-            currents = [product(parts(current), fs) for current, fs in zip(currents, split)]
-        fourths = [parts(product(sq, sq)) for sq in squares]
+            squares = [parts(halves_product(fs, fs)) for fs in split]
+            yield
+            currents = [halves_product(parts(current), fs) for current, fs in zip(currents, split)]
+        fourths = [parts(halves_product(sq, sq)) for sq in squares]
         yield
-        scaleds = [product(fo, parts(scaled)) for fo, scaled in zip(fourths, scaleds)]
+        scaleds = [halves_product(fo, parts(scaled)) for fo, scaled in zip(fourths, scaleds)]
         yield
 
 
@@ -143,21 +157,26 @@
 def right_stats_kernel(first, second, out, buffer, sems):
     tiles = fetched((first, second), buffer, sems)
     half = ROWS // 2
-    for b in range(RIGHT):
-        total = None
-        for s in range(2):
-            tiles[b][s].wait()
-            high, low = parts(buffer[s, b])
-            gram = dot(high, jnp.concatenate([high, low], axis=1), ((0,), (0,))) * (1.0 / D)
-            gram = packed_gram(gram[:, :BLOCK], gram[:, BLOCK:])
-            total = gram if s == 0 else (total[0] + gram[0], total[1] + gram[1])
-            if b < RIGHT - 1:
-                out[2 * b + s, :BLOCK, :] = total[0]
-                out[2 * b + s, BLOCK : BLOCK + 1, :] = total[1]
-            else:
-                out[s * half : (s + 1) * half, BLOCK + 8 :, :] = total[0].reshape(half, SHARE, HALF)
-                for slot in range(ROWS):
-                    out[slot, BLOCK + 1 + s : BLOCK + 2 + s, :] = total[1]
+    for group in ((0,), (1, 2), (3, 4)):
+        for b in group:
+            for copy in tiles[b]:
+                copy.wait()
+        packed = []
+        for b in group:
+            for s in range(2):
+                high, low = parts(buffer[s, b])
+                gram = dot(high, jnp.concatenate([high, low], axis=1), ((0,), (0,))) * (1.0 / D)
+                packed.append(packed_gram(gram[:, :BLOCK], gram[:, BLOCK:]))
+        for k, b in enumerate(group):
+            one, two = packed[2 * k : 2 * k + 2]
+            for s, (quarters, diagonal) in enumerate((one, (one[0] + two[0], one[1] + two[1]))):
+                if b < RIGHT - 1:
+                    out[2 * b + s, :BLOCK, :] = quarters
+                    out[2 * b + s, BLOCK : BLOCK + 1, :] = diagonal
+                else:
+                    out[s * half : (s + 1) * half, BLOCK + 8 :, :] = quarters.reshape(half, SHARE, HALF)
+                    for slot in range(ROWS):
+                        out[slot, BLOCK + 1 + s : BLOCK + 2 + s, :] = diagonal
     for slot in range(ROWS):
         out[slot, BLOCK + 3 : BLOCK + 8, :] = jnp.zeros((5, HALF), f32)
 
@@ -166,8 +185,9 @@
     core = info[0]
     tiles = fetched((first, second), buffer, sems)
     for b in range(RIGHT):
+        for copy in tiles[b]:
+            copy.wait()
         for s in range(2):
-            tiles[b][s].wait()
             for block in range(2):
                 high, low = parts(buffer[s, b, block * BLOCK : (block + 1) * BLOCK, :])
                 gram = dot(high, jnp.concatenate([high, low], axis=0), ((1,), (1,)))
@@ -215,8 +235,9 @@
     split = [[parts(unpacked(ref[s * PACK : (s + 1) * PACK, :])) for s in range(2)] for ref in (mine, other)]
     copies = []
     for b in range(RIGHT):
+        for copy in tiles[b]:
+            copy.wait()
         for s in range(2):
-            tiles[b][s].wait()
             for place, block in enumerate((core, 1 - core)):
                 rows = pl.ds(pl.multiple_of(block * BLOCK, BLOCK), BLOCK)
                 result = product(split[place][s], parts(buffer[s, b, rows, :]))
@@ -272,10 +293,12 @@
         copy.start()
         copies.append(copy)
 
-    next(chain)
+    for _ in range(4):
+        next(chain)
     for b in range(RIGHT - 1):
         for copy in fetches[b]:
             copy.wait()
+    for b in range(RIGHT - 1):
         one, two = parts(unpacked(roots_in[2 * b])), parts(unpacked(roots_in[2 * b + 1]))
         for _ in applied(held, b, one, two, buffer):
             next(chain, None)

time: 75.2 us -> 70.1 us (0.932)
  Pallas kernels: 39.8 us -> 34.1 us
  waiting for transfers between devices: 13 us -> 13.8 us
    pallas_call x1, Pallas kernels: 6.22 us -> 4.66 us  [body(): pl.pallas_call(right_stats_kernel, in_specs=[HBM, HBM], out_specs=VMEM, o...]
    pallas_call x1, Pallas kernels: 5.23 us -> 4.14 us  [body(): pl.pallas_call(left_root_kernel, in_specs=[VMEM, VMEM], out_specs=VMEM, o...]
    pallas_call x1, Pallas kernels: 8.14 us -> 7.07 us  [body(): pl.pallas_call(right_roots_kernel, in_specs=[ANY], out_specs=[VMEM, VMEM]...]
    pallas_call x1, Pallas kernels: 10 us -> 9.05 us  [body(): pl.pallas_call(finish_kernel, in_specs=[HBM, ANY, VMEM], out_specs=HBM, s...]
    all_to_all x2, waiting for transfers between devices: 1.68 us -> 2.53 us  [exchanged(): return lax.all_to_all(slots, 'row', split_axis=0, concat_axis=0, tiled=True)]
  transfers between devices with their start and end apart: 9 -> 9, of which waited for: 7 -> 8; matrix products, arithmetic and copies ran while one was open for 0% -> 0% of each run, Pallas kernels for 31% -> 29%
where the time goes in v3:
time: 70.1 us; the launch traced here: 69.9 us
  Pallas kernels  34.1 us (49%)
  starting transfers between devices  21.6 us (31%)
  waiting for transfers between devices  13.8 us (20%)
    ppermute x7, waiting for transfers between devices, swap(): return lax.ppermute(value, 'col', [(i, i ^ d) for i in range(COLS)])  11.3 us
    ppermute x7, starting transfers between devices, swap(): return lax.ppermute(value, 'col', [(i, i ^ d) for i in range(COLS)])  11.2 us
    all_to_all x2, starting transfers between devices, exchanged(): return lax.all_to_all(slots, 'row', split_axis=0, concat_axis=0, tiled=True)  10.4 us
    pallas_call x1, Pallas kernels, body(): pl.pallas_call(finish_kernel, in_specs=[HBM, ANY, VMEM], out_specs=HBM, s...  9.05 us
    pallas_call x1, Pallas kernels, body(): pl.pallas_call(right_roots_kernel, in_specs=[ANY], out_specs=[VMEM, VMEM]...  7.07 us
    pallas_call x1, Pallas kernels, body(): pl.pallas_call(halfway_kernel, in_specs=[SMEM, HBM, HBM, VMEM, VMEM], out...  5.64 us
    pallas_call x1, Pallas kernels, body(): pl.pallas_call(right_stats_kernel, in_specs=[HBM, HBM], out_specs=VMEM, o...  4.66 us
    pallas_call x1, Pallas kernels, body(): pl.pallas_call(left_root_kernel, in_specs=[VMEM, VMEM], out_specs=VMEM, o...  4.14 us
  transfers between devices with their start and end apart: 9, of which 8 were waited for; matrix products, arithmetic and copies ran while one was open for 0% of the time, Pallas kernels for 29%

profile of v3, /device:TPU:1, one launch (start us, length us, event | category | flops | bytes accessed | tf_op | source)
XLA Modules:
  0.0 69.9 jit_solution(14921196461724565063)
XLA Ops:
  0.0 4.7 %right_stats.1 = f32[8,328,128]{2,1,0:T(8,128)} custom-call(f32[512,1280]{1,0:T(8,128)} %first.5, f32[512,1280]{1,0:T(8,128)} %second.5), custom_call_target="tpu_custom_call" | custom-call | flops 2013265920 | bytes 5242880 | tf_op jit(solution)/shard_map/right_stats/pallas_call | solution.py:350
  4.7 6.8 %all-to-all-start = ((f32[8,328,128]{2,1,0:T(8,128)}), f32[8,328,128]{2,1,0:T(8,128)S(1)}, u32[]{:S(2)}, u32[]{:S(2)}) async-start(f32[8,328,128]{2,1,0:T(8,128)} %right_stats.1), calls=%async_computation | async-start | bytes 2686976 | tf_op jit(solution)/shard_map/all_to_all | solution.py:29
  11.5 3.5 %left_stats.1 = (f32[528,128]{1,0:T(8,128)S(1)}, f32[528,128]{1,0:T(8,128)S(1)}) custom-call(s32[1]{0:T(128)} %bitcast.info, f32[512,1280]{1,0:T(8,128)} %first.5, f32[512,1280]{1,0:T(8,128)} %second.5), custom_call_target="tpu_custom_call" | custom-call | flops 2013265920 | bytes 5242880 | tf_op jit(solution)/shard_map/left_stats/pallas_call | solution.py:363
  15.0 1.0 %collective-permute-start = (f32[528,128]{1,0:T(8,128)S(1)}, f32[528,128]{1,0:T(8,128)S(1)}, u32[]{:S(2)}, u32[]{:S(2)}) collective-permute-start(f32[528,128]{1,0:T(8,128)S(1)} %get-tuple-element.21), channel_id=1, source_target_pairs={{0,1},{1,0},{2,3},{3,2},{4,5},{5,4},{6,7},{7,6},{8,9},{9,8},{10,11... | collective-permute-start | bytes 811016 | tf_op jit(solution)/shard_map/ppermute | solution.py:25
  16.0 1.2 %collective-permute-done = f32[528,128]{1,0:T(8,128)S(1)} collective-permute-done((f32[528,128]{1,0:T(8,128)S(1)}, f32[528,128]{1,0:T(8,128)S(1)}, u32[]{:S(2)}, u32[]{:S(2)}) %collective-permute-start) | collective-permute-done | bytes 270368 | tf_op jit(solution)/shard_map/ppermute | solution.py:25
  17.3 2.8 %collective-permute-start.3 = (f32[264,128]{1,0:T(8,128)S(1)}, f32[264,128]{1,0:T(8,128)S(1)}, u32[]{:S(2)}, u32[]{:S(2)}) collective-permute-start(f32[264,128]{1,0:T(8,128)S(1)} %get-tuple-element.31), channel_id=1, source_target_pairs={{0,12},{1,13},{2,14},{3,15},{4,8},{5,9},{6,10},{7,11},{8,4},{9,5},... | collective-permute-start | bytes 405512 | tf_op jit(solution)/shard_map/ppermute | solution.py:25
  20.1 0.0 collective-permute-start.1
  20.1 1.3 %collective-permute-start.2 = (f32[264,128]{1,0:T(8,128)S(1)}, f32[264,128]{1,0:T(8,128)S(1)}, u32[]{:S(2)}, u32[]{:S(2)}) collective-permute-start(f32[264,128]{1,0:T(8,128)S(1)} %get-tuple-element.32), channel_id=1, source_target_pairs={{0,8},{1,9},{2,10},{3,11},{4,12},{5,13},{6,14},{7,15},{8,0},{9,1},... | collective-permute-start | bytes 405512 | tf_op jit(solution)/shard_map/ppermute | solution.py:25
  21.4 2.1 %collective-permute-done.3 = f32[264,128]{1,0:T(8,128)S(1)} collective-permute-done((f32[264,128]{1,0:T(8,128)S(1)}, f32[264,128]{1,0:T(8,128)S(1)}, u32[]{:S(2)}, u32[]{:S(2)}) %collective-permute-start.3) | collective-permute-done | bytes 135200 | tf_op jit(solution)/shard_map/ppermute | solution.py:25
  23.5 1.1 %collective-permute-done.1 = f32[264,128]{1,0:T(8,128)S(1)} collective-permute-done((f32[264,128]{1,0:T(8,128)S(1)}, f32[264,128]{1,0:T(8,128)S(1)}, u32[]{:S(2)}, u32[]{:S(2)}) %collective-permute-start.1) | collective-permute-done | bytes 135200 | tf_op jit(solution)/shard_map/ppermute | solution.py:25
  24.6 2.9 %collective-permute-done.2 = f32[264,128]{1,0:T(8,128)S(1)} collective-permute-done((f32[264,128]{1,0:T(8,128)S(1)}, f32[264,128]{1,0:T(8,128)S(1)}, u32[]{:S(2)}, u32[]{:S(2)}) %collective-permute-start.2) | collective-permute-done | bytes 135200 | tf_op jit(solution)/shard_map/ppermute | solution.py:25
  27.5 2.1 %all-to-all-done.arrived = f32[8,328,128]{2,1,0:T(8,128)S(1)} async-done(((f32[8,328,128]{2,1,0:T(8,128)}), f32[8,328,128]{2,1,0:T(8,128)S(1)}, u32[]{:S(2)}, u32[]{:S(2)}) %all-to-all-start) | async-done | bytes 1343520 | tf_op jit(solution)/shard_map/all_to_all | solution.py:29
  29.5 2.4 %collective-permute-start.4 = (f32[264,128]{1,0:T(8,128)S(1)}, f32[264,128]{1,0:T(8,128)S(1)}, u32[]{:S(2)}, u32[]{:S(2)}) collective-permute-start(f32[264,128]{1,0:T(8,128)S(1)} %add_add_fusion.own), channel_id=1, source_target_pairs={{0,2},{1,3},{2,0},{3,1},{4,6},{5,7},{6,4},{7,5},{8,10},{9,11},{10,... | collective-permute-start | bytes 405512 | tf_op jit(solution)/shard_map/ppermute | solution.py:25
  32.0 7.1 %right_roots.1 = (f32[8,328,128]{2,1,0:T(8,128)}, f32[8,128]{1,0:T(8,128)S(1)}) custom-call(f32[8,328,128]{2,1,0:T(8,128)S(1)} %all-to-all-done.arrived), custom_call_target="tpu_custom_call" | custom-call | flops 2013265920 | bytes 2686976 | tf_op jit(solution)/shard_map/right_roots/pallas_call | solution.py:381
  39.1 0.0 collective-permute-done.4.other
  39.1 3.6 %all-to-all-start.1 = ((f32[8,328,128]{2,1,0:T(8,128)}), f32[8,328,128]{2,1,0:T(8,128)S(1)}, u32[]{:S(2)}, u32[]{:S(2)}) async-start(f32[8,328,128]{2,1,0:T(8,128)} %get-tuple-element.29), calls=%async_computation.1 | async-start | bytes 2686976 | tf_op jit(solution)/shard_map/all_to_all | solution.py:29
  42.7 4.1 %left_root.1 = f32[264,128]{1,0:T(8,128)S(1)} custom-call(f32[264,128]{1,0:T(8,128)S(1)} %add_add_fusion.own, f32[264,128]{1,0:T(8,128)S(1)} %collective-permute-done.4.other), custom_call_target="tpu_custom_call" | custom-call | flops 2013265920 | bytes 405504 | tf_op jit(solution)/shard_map/left_root/pallas_call | solution.py:394
  46.8 1.4 %collective-permute-start.5 = (f32[264,128]{1,0:T(8,128)S(1)}, f32[264,128]{1,0:T(8,128)S(1)}, u32[]{:S(2)}, u32[]{:S(2)}) collective-permute-start(f32[264,128]{1,0:T(8,128)S(1)} %left_root.1), channel_id=1, source_target_pairs={{0,4},{1,5},{2,6},{3,7},{4,0},{5,1},{6,2},{7,3},{8,12},{9,13},{10,... | collective-permute-start | bytes 405512 | tf_op jit(solution)/shard_map/ppermute | solution.py:25
  48.2 2.9 %collective-permute-done.5 = f32[264,128]{1,0:T(8,128)S(1)} collective-permute-done((f32[264,128]{1,0:T(8,128)S(1)}, f32[264,128]{1,0:T(8,128)S(1)}, u32[]{:S(2)}, u32[]{:S(2)}) %collective-permute-start.5) | collective-permute-done | bytes 135200 | tf_op jit(solution)/shard_map/ppermute | solution.py:25
  51.1 2.3 %collective-permute-start.6 = (f32[528,128]{1,0:T(8,128)S(1)}, f32[528,128]{1,0:T(8,128)S(1)}, u32[]{:S(2)}, u32[]{:S(2)}) collective-permute-start(f32[528,128]{1,0:T(8,128)S(1)} %maximum_select_fusion.mine), channel_id=1, source_target_pairs={{0,1},{1,0},{2,3},{3,2},{4,5},{5,4},{6,7},{7,6},{8,9},{9,8},{10,11... | collective-permute-start | bytes 811016 | tf_op jit(solution)/shard_map/ppermute | solution.py:25
  53.4 1.2 %collective-permute-done.6.other = f32[528,128]{1,0:T(8,128)S(1)} collective-permute-done((f32[528,128]{1,0:T(8,128)S(1)}, f32[528,128]{1,0:T(8,128)S(1)}, u32[]{:S(2)}, u32[]{:S(2)}) %collective-permute-start.6) | collective-permute-done | bytes 270368 | tf_op jit(solution)/shard_map/ppermute | solution.py:25
  54.5 5.6 %halfway.1 = bf16[5,4,512,256]{3,2,1,0:T(8,128)(2,1)} custom-call(s32[1]{0:T(128)} %bitcast.info, f32[512,1280]{1,0:T(8,128)} %first.5, f32[512,1280]{1,0:T(8,128)} %second.5, f32[528,128]{1,0:T(8,128)S(1)} %maximum_select_fusion.mine, f32[528,128]{1,0:T(8,128)S(1)} %collective-permute-done.6.other), custom_call_target="tpu_custom_call" | custom-call | flops 2013265920 | bytes 10485760 | tf_op jit(solution)/shard_map/halfway/pallas_call | solution.py:413
  60.2 0.5 all-to-all-done.1.gathered
  60.6 9.0 %finish.1 = f32[512,1280]{1,0:T(8,128)} custom-call(bf16[5,4,512,256]{3,2,1,0:T(8,128)(2,1)} %halfway.1, f32[8,328,128]{2,1,0:T(8,128)S(1)} %all-to-all-done.1.gathered, f32[8,128]{1,0:T(8,128)S(1)} %get-tuple-element.30.diagonals), custom_call_target="tpu_custom_call" | custom-call | flops 6039797760 | bytes 10485760 | tf_op jit(solution)/shard_map/finish/pallas_call | solution.py:424
  (4 shorter events, 0.1 us)
Async XLA Ops:
  4.7 24.9 %all-to-all-start = ((f32[8,328,128]{2,1,0:T(8,128)}), f32[8,328,128]{2,1,0:T(8,128)S(1)}, u32[]{:S(2)}, u32[]{:S(2)}) async-start(f32[8,328,128]{2,1,0:T(8,128)} %right_stats.1), calls=%async_computation | async-start | bytes 2686976 | tf_op jit(solution)/shard_map/all_to_all | solution.py:29
  15.0 2.2 %collective-permute-start = (f32[528,128]{1,0:T(8,128)S(1)}, f32[528,128]{1,0:T(8,128)S(1)}, u32[]{:S(2)}, u32[]{:S(2)}) collective-permute-start(f32[528,128]{1,0:T(8,128)S(1)} %get-tuple-element.21), channel_id=1, source_target_pairs={{0,1},{1,0},{2,3},{3,2},{4,5},{5,4},{6,7},{7,6},{8,9},{9,8},{10,11... | collective-permute-start | bytes 811016 | tf_op jit(solution)/shard_map/ppermute | solution.py:25
  17.3 6.2 %collective-permute-start.3 = (f32[264,128]{1,0:T(8,128)S(1)}, f32[264,128]{1,0:T(8,128)S(1)}, u32[]{:S(2)}, u32[]{:S(2)}) collective-permute-start(f32[264,128]{1,0:T(8,128)S(1)} %get-tuple-element.31), channel_id=1, source_target_pairs={{0,12},{1,13},{2,14},{3,15},{4,8},{5,9},{6,10},{7,11},{8,4},{9,5},... | collective-permute-start | bytes 405512 | tf_op jit(solution)/shard_map/ppermute | solution.py:25
  20.1 4.5 %collective-permute-start.1 = (f32[264,128]{1,0:T(8,128)S(1)}, f32[264,128]{1,0:T(8,128)S(1)}, u32[]{:S(2)}, u32[]{:S(2)}) collective-permute-start(f32[264,128]{1,0:T(8,128)S(1)} %get-tuple-element.31), channel_id=1, source_target_pairs={{0,4},{1,5},{2,6},{3,7},{4,0},{5,1},{6,2},{7,3},{8,12},{9,13},{10,... | collective-permute-start | bytes 405512 | tf_op jit(solution)/shard_map/ppermute | solution.py:25
  20.1 7.3 %collective-permute-start.2 = (f32[264,128]{1,0:T(8,128)S(1)}, f32[264,128]{1,0:T(8,128)S(1)}, u32[]{:S(2)}, u32[]{:S(2)}) collective-permute-start(f32[264,128]{1,0:T(8,128)S(1)} %get-tuple-element.32), channel_id=1, source_target_pairs={{0,8},{1,9},{2,10},{3,11},{4,12},{5,13},{6,14},{7,15},{8,0},{9,1},... | collective-permute-start | bytes 405512 | tf_op jit(solution)/shard_map/ppermute | solution.py:25
  29.5 9.5 %collective-permute-start.4 = (f32[264,128]{1,0:T(8,128)S(1)}, f32[264,128]{1,0:T(8,128)S(1)}, u32[]{:S(2)}, u32[]{:S(2)}) collective-permute-start(f32[264,128]{1,0:T(8,128)S(1)} %add_add_fusion.own), channel_id=1, source_target_pairs={{0,2},{1,3},{2,0},{3,1},{4,6},{5,7},{6,4},{7,5},{8,10},{9,11},{10,... | collective-permute-start | bytes 405512 | tf_op jit(solution)/shard_map/ppermute | solution.py:25
  39.1 21.6 %all-to-all-start.1 = ((f32[8,328,128]{2,1,0:T(8,128)}), f32[8,328,128]{2,1,0:T(8,128)S(1)}, u32[]{:S(2)}, u32[]{:S(2)}) async-start(f32[8,328,128]{2,1,0:T(8,128)} %get-tuple-element.29), calls=%async_computation.1 | async-start | bytes 2686976 | tf_op jit(solution)/shard_map/all_to_all | solution.py:29
  46.8 4.2 %collective-permute-start.5 = (f32[264,128]{1,0:T(8,128)S(1)}, f32[264,128]{1,0:T(8,128)S(1)}, u32[]{:S(2)}, u32[]{:S(2)}) collective-permute-start(f32[264,128]{1,0:T(8,128)S(1)} %left_root.1), channel_id=1, source_target_pairs={{0,4},{1,5},{2,6},{3,7},{4,0},{5,1},{6,2},{7,3},{8,12},{9,13},{10,... | collective-permute-start | bytes 405512 | tf_op jit(solution)/shard_map/ppermute | solution.py:25
  51.1 3.5 %collective-permute-start.6 = (f32[528,128]{1,0:T(8,128)S(1)}, f32[528,128]{1,0:T(8,128)S(1)}, u32[]{:S(2)}, u32[]{:S(2)}) collective-permute-start(f32[528,128]{1,0:T(8,128)S(1)} %maximum_select_fusion.mine), channel_id=1, source_target_pairs={{0,1},{1,0},{2,3},{3,2},{4,5},{5,4},{6,7},{7,6},{8,9},{9,8},{10,11... | collective-permute-start | bytes 811016 | tf_op jit(solution)/shard_map/ppermute | solution.py:25

commit v4 on v3

--- a/solution.py
+++ b/solution.py
@@ -205,15 +205,10 @@
             out[s * PACK + BLOCK : (s + 1) * PACK, :] = jnp.broadcast_to(total[1], (8, HALF))
 
 
-def right_roots_kernel(arrived, right_out, diagonals, buffer, sems):
-    copies = [pltpu.make_async_copy(arrived.at[slot], buffer.at[slot], sems.at[slot]) for slot in range(ROWS)]
-    for copy in copies:
-        copy.start()
-    copies[0].wait()
-    total = buffer[0]
+def right_roots_kernel(arrived, right_out, diagonals):
+    total = arrived[0]
     for slot in range(1, ROWS):
-        copies[slot].wait()
-        total = total + buffer[slot]
+        total = total + arrived[slot]
     for slot in range(ROWS):
         right_out[slot, PACK:, :] = total[PACK:]
     diagonals[...] = total[BLOCK:PACK]
@@ -261,27 +256,14 @@
 
 
 def finish_kernel(
-    halfway, gathered, diagonals, out, held, roots_in, shares, buffer, sems, root_sems, share_sem, out_sems
+    halfway, gathered, diagonals, out, held, buffer, sems, out_sems
 ):
-    share_copy = pltpu.make_async_copy(gathered.at[:, pl.ds(PACK, SHARE), :], shares, share_sem)
-    share_copy.start()
-    fetches = []
-    for b in range(RIGHT):
-        fetches.append([])
-        if b < RIGHT - 1:
-            pair = pl.ds(2 * b, 2)
-            fetches[b].append(
-                pltpu.make_async_copy(
-                    gathered.at[pair, pl.ds(0, PACK), :], roots_in.at[pair], root_sems.at[b]
-                )
-            )
-        fetches[b].append(pltpu.make_async_copy(halfway.at[b], held.at[b], sems.at[b]))
-        for copy in fetches[b]:
-            copy.start()
+    fetches = [pltpu.make_async_copy(halfway.at[b], held.at[b], sems.at[b]) for b in range(RIGHT)]
+    for copy in fetches:
+        copy.start()
     half = ROWS // 2
-    share_copy.wait()
     statistics = [
-        unpacked(shares[s * half : (s + 1) * half].reshape(BLOCK, HALF), diagonals[1 + s : 2 + s, :])
+        unpacked(gathered[s * half : (s + 1) * half, PACK:, :].reshape(BLOCK, HALF), diagonals[1 + s : 2 + s, :])
         for s in range(2)
     ]
     found = []
@@ -295,11 +277,10 @@
 
     for _ in range(4):
         next(chain)
+    for copy in fetches:
+        copy.wait()
     for b in range(RIGHT - 1):
-        for copy in fetches[b]:
-            copy.wait()
-    for b in range(RIGHT - 1):
-        one, two = parts(unpacked(roots_in[2 * b])), parts(unpacked(roots_in[2 * b + 1]))
+        one, two = [parts(unpacked(gathered[2 * b + s, :PACK, :])) for s in range(2)]
         for _ in applied(held, b, one, two, buffer):
             next(chain, None)
         stored(b)
@@ -307,7 +288,6 @@
     for _ in chain:
         pass
     last = RIGHT - 1
-    fetches[last][0].wait()
     for _ in applied(held, last, parts(found[0]), parts(found[1]), buffer):
         pass
     stored(last)
@@ -318,7 +298,6 @@
 VMEM = pl.BlockSpec(memory_space=pltpu.VMEM)
 SMEM = pl.BlockSpec(memory_space=pltpu.SMEM)
 HBM = pl.BlockSpec(memory_space=pltpu.HBM)
-ANY = pl.BlockSpec(memory_space=pl.ANY)
 
 
 def in_hbm(*values):
@@ -374,16 +353,14 @@
     own = lax.dynamic_index_in_dim(both, low_y, 0, keepdims=False)
     rest = lax.dynamic_index_in_dim(both, 1 - low_y, 0, keepdims=False)
     own = (own + swap(rest, 4)) + (swap(own, 8) + swap(rest, 12))
+    left_in = [own, swap(own, 2)]
     own, arrived = lax.optimization_barrier((own, arrived))
-    left_in = [own, swap(own, 2)]
-
-    slots = jax.ShapeDtypeStruct((ROWS, SLOT, HALF), f32)
+
     right_root, diagonals = pl.pallas_call(
         right_roots_kernel,
-        in_specs=[ANY],
+        in_specs=[VMEM],
         out_specs=[VMEM, VMEM],
-        out_shape=[slots, jax.ShapeDtypeStruct((8, HALF), f32)],
-        scratch_shapes=[pltpu.VMEM((ROWS, SLOT, HALF), f32), pltpu.SemaphoreType.DMA((ROWS,))],
+        out_shape=[jax.ShapeDtypeStruct((ROWS, SLOT, HALF), f32), jax.ShapeDtypeStruct((8, HALF), f32)],
         compiler_params=params(),
         cost_estimate=cost(newton, 2 * ROWS * SLOT * HALF * 4),
         name="right_roots",
@@ -423,16 +400,12 @@
 
     return pl.pallas_call(
         finish_kernel,
-        in_specs=[HBM, ANY, VMEM],
+        in_specs=[HBM, VMEM, VMEM],
         out_specs=HBM,
         scratch_shapes=[
             pltpu.VMEM(held, bf16),
-            pltpu.VMEM((ROWS, PACK, HALF), f32),
-            pltpu.VMEM((ROWS, SHARE, HALF), f32),
             pltpu.VMEM((RIGHT, rows, BLOCK), f32),
             tile_sem,
-            tile_sem,
-            pltpu.SemaphoreType.DMA(()),
             tile_sem,
         ],
         out_shape=jax.ShapeDtypeStruct((rows, cols), f32),

time: 70.1 us -> 67.9 us (0.969)
  Pallas kernels: 34.1 us -> 32.3 us
  waiting for transfers between devices: 13.8 us -> 12.6 us
  starting transfers between devices: 21.6 us -> 22.4 us
    all_to_all x2, waiting for transfers between devices: 2.53 us -> 0.01 us  [exchanged(): return lax.all_to_all(slots, 'row', split_axis=0, concat_axis=0, tiled=True)]
    pallas_call x2, Pallas kernels: 16.1 us -> 14.4 us  [the longest x1 9.12 us: body(): pl.pallas_call(finish_kernel, in_specs=[HBM, VMEM, VMEM], out_specs=HBM,...]
    ppermute x7, waiting for transfers between devices: 11.3 us -> 12.6 us  [swap(): return lax.ppermute(value, 'col', [(i, i ^ d) for i in range(COLS)])]
    all_to_all x2, starting transfers between devices: 10.4 us -> 11.6 us  [exchanged(): return lax.all_to_all(slots, 'row', split_axis=0, concat_axis=0, tiled=True)]
  transfers between devices with their start and end apart: 9 -> 9, of which waited for: 8 -> 6; matrix products, arithmetic and copies ran while one was open for 0% -> 0% of each run, Pallas kernels for 29% -> 27%
where the time goes in v4:
time: 67.9 us; the launch traced here: 67.6 us
  Pallas kernels  32.3 us (48%)
  starting transfers between devices  22.4 us (33%)
  waiting for transfers between devices  12.6 us (19%)
    ppermute x7, waiting for transfers between devices, swap(): return lax.ppermute(value, 'col', [(i, i ^ d) for i in range(COLS)])  12.6 us
    all_to_all x2, starting transfers between devices, exchanged(): return lax.all_to_all(slots, 'row', split_axis=0, concat_axis=0, tiled=True)  11.6 us
    ppermute x7, starting transfers between devices, swap(): return lax.ppermute(value, 'col', [(i, i ^ d) for i in range(COLS)])  10.8 us
    pallas_call x1, Pallas kernels, body(): pl.pallas_call(finish_kernel, in_specs=[HBM, VMEM, VMEM], out_specs=HBM,...  9.12 us
    pallas_call x1, Pallas kernels, body(): pl.pallas_call(halfway_kernel, in_specs=[SMEM, HBM, HBM, VMEM, VMEM], out...  5.64 us
    pallas_call x1, Pallas kernels, body(): pl.pallas_call(right_roots_kernel, in_specs=[VMEM], out_specs=[VMEM, VMEM...  5.24 us
    pallas_call x1, Pallas kernels, body(): pl.pallas_call(right_stats_kernel, in_specs=[HBM, HBM], out_specs=VMEM, o...  4.66 us
    pallas_call x1, Pallas kernels, body(): pl.pallas_call(left_root_kernel, in_specs=[VMEM, VMEM], out_specs=VMEM, o...  4.14 us
  transfers between devices with their start and end apart: 9, of which 6 were waited for; matrix products, arithmetic and copies ran while one was open for 0% of the time, Pallas kernels for 27%

profile of v4, /device:TPU:1, one launch (start us, length us, event | category | flops | bytes accessed | tf_op | source)
XLA Modules:
  0.0 67.6 jit_solution(18044633653351611443)
XLA Ops:
  0.0 4.7 %right_stats.1 = f32[8,328,128]{2,1,0:T(8,128)} custom-call(f32[512,1280]{1,0:T(8,128)} %first.5, f32[512,1280]{1,0:T(8,128)} %second.5), custom_call_target="tpu_custom_call" | custom-call | flops 2013265920 | bytes 5242880 | tf_op jit(solution)/shard_map/right_stats/pallas_call | solution.py:329
  4.7 6.8 %all-to-all-start = ((f32[8,328,128]{2,1,0:T(8,128)}), f32[8,328,128]{2,1,0:T(8,128)S(1)}, u32[]{:S(2)}, u32[]{:S(2)}) async-start(f32[8,328,128]{2,1,0:T(8,128)} %right_stats.1), calls=%async_computation | async-start | bytes 2686976 | tf_op jit(solution)/shard_map/all_to_all | solution.py:29
  11.5 3.5 %left_stats.1 = (f32[528,128]{1,0:T(8,128)S(1)}, f32[528,128]{1,0:T(8,128)S(1)}) custom-call(s32[1]{0:T(128)} %bitcast.info, f32[512,1280]{1,0:T(8,128)} %first.5, f32[512,1280]{1,0:T(8,128)} %second.5), custom_call_target="tpu_custom_call" | custom-call | flops 2013265920 | bytes 5242880 | tf_op jit(solution)/shard_map/left_stats/pallas_call | solution.py:342
  15.0 1.0 %collective-permute-start = (f32[528,128]{1,0:T(8,128)S(1)}, f32[528,128]{1,0:T(8,128)S(1)}, u32[]{:S(2)}, u32[]{:S(2)}) collective-permute-start(f32[528,128]{1,0:T(8,128)S(1)} %get-tuple-element.20), channel_id=1, source_target_pairs={{0,1},{1,0},{2,3},{3,2},{4,5},{5,4},{6,7},{7,6},{8,9},{9,8},{10,11... | collective-permute-start | bytes 811016 | tf_op jit(solution)/shard_map/ppermute | solution.py:25
  16.0 1.2 %collective-permute-done = f32[528,128]{1,0:T(8,128)S(1)} collective-permute-done((f32[528,128]{1,0:T(8,128)S(1)}, f32[528,128]{1,0:T(8,128)S(1)}, u32[]{:S(2)}, u32[]{:S(2)}) %collective-permute-start) | collective-permute-done | bytes 270368 | tf_op jit(solution)/shard_map/ppermute | solution.py:25
  17.3 2.8 %collective-permute-start.3 = (f32[264,128]{1,0:T(8,128)S(1)}, f32[264,128]{1,0:T(8,128)S(1)}, u32[]{:S(2)}, u32[]{:S(2)}) collective-permute-start(f32[264,128]{1,0:T(8,128)S(1)} %get-tuple-element.29), channel_id=1, source_target_pairs={{0,12},{1,13},{2,14},{3,15},{4,8},{5,9},{6,10},{7,11},{8,4},{9,5},... | collective-permute-start | bytes 405512 | tf_op jit(solution)/shard_map/ppermute | solution.py:25
  20.1 0.0 collective-permute-start.1
  20.1 1.3 %collective-permute-start.2 = (f32[264,128]{1,0:T(8,128)S(1)}, f32[264,128]{1,0:T(8,128)S(1)}, u32[]{:S(2)}, u32[]{:S(2)}) collective-permute-start(f32[264,128]{1,0:T(8,128)S(1)} %get-tuple-element.30), channel_id=1, source_target_pairs={{0,8},{1,9},{2,10},{3,11},{4,12},{5,13},{6,14},{7,15},{8,0},{9,1},... | collective-permute-start | bytes 405512 | tf_op jit(solution)/shard_map/ppermute | solution.py:25
  21.4 2.1 %collective-permute-done.3 = f32[264,128]{1,0:T(8,128)S(1)} collective-permute-done((f32[264,128]{1,0:T(8,128)S(1)}, f32[264,128]{1,0:T(8,128)S(1)}, u32[]{:S(2)}, u32[]{:S(2)}) %collective-permute-start.3) | collective-permute-done | bytes 135200 | tf_op jit(solution)/shard_map/ppermute | solution.py:25
  23.5 1.1 %collective-permute-done.1 = f32[264,128]{1,0:T(8,128)S(1)} collective-permute-done((f32[264,128]{1,0:T(8,128)S(1)}, f32[264,128]{1,0:T(8,128)S(1)}, u32[]{:S(2)}, u32[]{:S(2)}) %collective-permute-start.1) | collective-permute-done | bytes 135200 | tf_op jit(solution)/shard_map/ppermute | solution.py:25
  24.6 2.9 %collective-permute-done.2 = f32[264,128]{1,0:T(8,128)S(1)} collective-permute-done((f32[264,128]{1,0:T(8,128)S(1)}, f32[264,128]{1,0:T(8,128)S(1)}, u32[]{:S(2)}, u32[]{:S(2)}) %collective-permute-start.2) | collective-permute-done | bytes 135200 | tf_op jit(solution)/shard_map/ppermute | solution.py:25
  27.5 2.5 %collective-permute-start.4 = (f32[264,128]{1,0:T(8,128)S(1)}, f32[264,128]{1,0:T(8,128)S(1)}, u32[]{:S(2)}, u32[]{:S(2)}) collective-permute-start(f32[264,128]{1,0:T(8,128)S(1)} %add_add_fusion.own), channel_id=1, source_target_pairs={{0,2},{1,3},{2,0},{3,1},{4,6},{5,7},{6,4},{7,5},{8,10},{9,11},{10,... | collective-permute-start | bytes 405512 | tf_op jit(solution)/shard_map/ppermute | solution.py:25
  30.0 0.0 all-to-all-done.arrived
  30.0 5.2 %right_roots.1 = (f32[8,328,128]{2,1,0:T(8,128)}, f32[8,128]{1,0:T(8,128)S(1)}) custom-call(f32[8,328,128]{2,1,0:T(8,128)S(1)} %all-to-all-done.arrived), custom_call_target="tpu_custom_call" | custom-call | flops 2013265920 | bytes 2686976 | tf_op jit(solution)/shard_map/right_roots/pallas_call | solution.py:359
  35.2 0.0 collective-permute-done.4.other
  35.2 4.8 %all-to-all-start.1 = ((f32[8,328,128]{2,1,0:T(8,128)}), f32[8,328,128]{2,1,0:T(8,128)S(1)}, u32[]{:S(2)}, u32[]{:S(2)}) async-start(f32[8,328,128]{2,1,0:T(8,128)} %get-tuple-element.27), calls=%async_computation.1 | async-start | bytes 2686976 | tf_op jit(solution)/shard_map/all_to_all | solution.py:29
  40.1 4.1 %left_root.1 = f32[264,128]{1,0:T(8,128)S(1)} custom-call(f32[264,128]{1,0:T(8,128)S(1)} %add_add_fusion.own, f32[264,128]{1,0:T(8,128)S(1)} %collective-permute-done.4.other), custom_call_target="tpu_custom_call" | custom-call | flops 2013265920 | bytes 405504 | tf_op jit(solution)/shard_map/left_root/pallas_call | solution.py:371
  44.2 0.1 collective-permute-start.5
  44.3 4.1 %collective-permute-done.5 = f32[264,128]{1,0:T(8,128)S(1)} collective-permute-done((f32[264,128]{1,0:T(8,128)S(1)}, f32[264,128]{1,0:T(8,128)S(1)}, u32[]{:S(2)}, u32[]{:S(2)}) %collective-permute-start.5) | collective-permute-done | bytes 135200 | tf_op jit(solution)/shard_map/ppermute | solution.py:25
  48.5 3.0 %collective-permute-start.6 = (f32[528,128]{1,0:T(8,128)S(1)}, f32[528,128]{1,0:T(8,128)S(1)}, u32[]{:S(2)}, u32[]{:S(2)}) collective-permute-start(f32[528,128]{1,0:T(8,128)S(1)} %maximum_select_fusion.mine), channel_id=1, source_target_pairs={{0,1},{1,0},{2,3},{3,2},{4,5},{5,4},{6,7},{7,6},{8,9},{9,8},{10,11... | collective-permute-start | bytes 811016 | tf_op jit(solution)/shard_map/ppermute | solution.py:25
  51.5 1.2 %collective-permute-done.6.other = f32[528,128]{1,0:T(8,128)S(1)} collective-permute-done((f32[528,128]{1,0:T(8,128)S(1)}, f32[528,128]{1,0:T(8,128)S(1)}, u32[]{:S(2)}, u32[]{:S(2)}) %collective-permute-start.6) | collective-permute-done | bytes 270368 | tf_op jit(solution)/shard_map/ppermute | solution.py:25
  52.7 5.6 %halfway.1 = bf16[5,4,512,256]{3,2,1,0:T(8,128)(2,1)} custom-call(s32[1]{0:T(128)} %bitcast.info, f32[512,1280]{1,0:T(8,128)} %first.5, f32[512,1280]{1,0:T(8,128)} %second.5, f32[528,128]{1,0:T(8,128)S(1)} %maximum_select_fusion.mine, f32[528,128]{1,0:T(8,128)S(1)} %collective-permute-done.6.other), custom_call_target="tpu_custom_call" | custom-call | flops 2013265920 | bytes 10485760 | tf_op jit(solution)/shard_map/halfway/pallas_call | solution.py:390
  58.3 0.0 all-to-all-done.1.gathered
  58.3 9.1 %finish.1 = f32[512,1280]{1,0:T(8,128)} custom-call(bf16[5,4,512,256]{3,2,1,0:T(8,128)(2,1)} %halfway.1, f32[8,328,128]{2,1,0:T(8,128)S(1)} %all-to-all-done.1.gathered, f32[8,128]{1,0:T(8,128)S(1)} %get-tuple-element.28.diagonals), custom_call_target="tpu_custom_call" | custom-call | flops 6039797760 | bytes 10485760 | tf_op jit(solution)/shard_map/finish/pallas_call | solution.py:401
  (4 shorter events, 0.1 us)
Async XLA Ops:
  4.7 25.3 %all-to-all-start = ((f32[8,328,128]{2,1,0:T(8,128)}), f32[8,328,128]{2,1,0:T(8,128)S(1)}, u32[]{:S(2)}, u32[]{:S(2)}) async-start(f32[8,328,128]{2,1,0:T(8,128)} %right_stats.1), calls=%async_computation | async-start | bytes 2686976 | tf_op jit(solution)/shard_map/all_to_all | solution.py:29
  15.0 2.2 %collective-permute-start = (f32[528,128]{1,0:T(8,128)S(1)}, f32[528,128]{1,0:T(8,128)S(1)}, u32[]{:S(2)}, u32[]{:S(2)}) collective-permute-start(f32[528,128]{1,0:T(8,128)S(1)} %get-tuple-element.20), channel_id=1, source_target_pairs={{0,1},{1,0},{2,3},{3,2},{4,5},{5,4},{6,7},{7,6},{8,9},{9,8},{10,11... | collective-permute-start | bytes 811016 | tf_op jit(solution)/shard_map/ppermute | solution.py:25
  17.3 6.2 %collective-permute-start.3 = (f32[264,128]{1,0:T(8,128)S(1)}, f32[264,128]{1,0:T(8,128)S(1)}, u32[]{:S(2)}, u32[]{:S(2)}) collective-permute-start(f32[264,128]{1,0:T(8,128)S(1)} %get-tuple-element.29), channel_id=1, source_target_pairs={{0,12},{1,13},{2,14},{3,15},{4,8},{5,9},{6,10},{7,11},{8,4},{9,5},... | collective-permute-start | bytes 405512 | tf_op jit(solution)/shard_map/ppermute | solution.py:25
  20.1 4.5 %collective-permute-start.1 = (f32[264,128]{1,0:T(8,128)S(1)}, f32[264,128]{1,0:T(8,128)S(1)}, u32[]{:S(2)}, u32[]{:S(2)}) collective-permute-start(f32[264,128]{1,0:T(8,128)S(1)} %get-tuple-element.29), channel_id=1, source_target_pairs={{0,4},{1,5},{2,6},{3,7},{4,0},{5,1},{6,2},{7,3},{8,12},{9,13},{10,... | collective-permute-start | bytes 405512 | tf_op jit(solution)/shard_map/ppermute | solution.py:25
  20.1 7.3 %collective-permute-start.2 = (f32[264,128]{1,0:T(8,128)S(1)}, f32[264,128]{1,0:T(8,128)S(1)}, u32[]{:S(2)}, u32[]{:S(2)}) collective-permute-start(f32[264,128]{1,0:T(8,128)S(1)} %get-tuple-element.30), channel_id=1, source_target_pairs={{0,8},{1,9},{2,10},{3,11},{4,12},{5,13},{6,14},{7,15},{8,0},{9,1},... | collective-permute-start | bytes 405512 | tf_op jit(solution)/shard_map/ppermute | solution.py:25
  27.5 7.8 %collective-permute-start.4 = (f32[264,128]{1,0:T(8,128)S(1)}, f32[264,128]{1,0:T(8,128)S(1)}, u32[]{:S(2)}, u32[]{:S(2)}) collective-permute-start(f32[264,128]{1,0:T(8,128)S(1)} %add_add_fusion.own), channel_id=1, source_target_pairs={{0,2},{1,3},{2,0},{3,1},{4,6},{5,7},{6,4},{7,5},{8,10},{9,11},{10,... | collective-permute-start | bytes 405512 | tf_op jit(solution)/shard_map/ppermute | solution.py:25
  35.2 23.1 %all-to-all-start.1 = ((f32[8,328,128]{2,1,0:T(8,128)}), f32[8,328,128]{2,1,0:T(8,128)S(1)}, u32[]{:S(2)}, u32[]{:S(2)}) async-start(f32[8,328,128]{2,1,0:T(8,128)} %get-tuple-element.27), calls=%async_computation.1 | async-start | bytes 2686976 | tf_op jit(solution)/shard_map/all_to_all | solution.py:29
  44.2 4.2 %collective-permute-start.5 = (f32[264,128]{1,0:T(8,128)S(1)}, f32[264,128]{1,0:T(8,128)S(1)}, u32[]{:S(2)}, u32[]{:S(2)}) collective-permute-start(f32[264,128]{1,0:T(8,128)S(1)} %left_root.1), channel_id=1, source_target_pairs={{0,4},{1,5},{2,6},{3,7},{4,0},{5,1},{6,2},{7,3},{8,12},{9,13},{10,... | collective-permute-start | bytes 405512 | tf_op jit(solution)/shard_map/ppermute | solution.py:25
  48.5 4.2 %collective-permute-start.6 = (f32[528,128]{1,0:T(8,128)S(1)}, f32[528,128]{1,0:T(8,128)S(1)}, u32[]{:S(2)}, u32[]{:S(2)}) collective-permute-start(f32[528,128]{1,0:T(8,128)S(1)} %maximum_select_fusion.mine), channel_id=1, source_target_pairs={{0,1},{1,0},{2,3},{3,2},{4,5},{5,4},{6,7},{7,6},{8,9},{9,8},{10,11... | collective-permute-start | bytes 811016 | tf_op jit(solution)/shard_map/ppermute | solution.py:25

commit v5 on v4

--- a/solution.py
+++ b/solution.py
@@ -138,26 +138,27 @@
     return found
 
 
-def fetched(sources, buffer, sems):
-    tiles = []
-    for b in range(RIGHT):
+def fetched(sources, buffer, sems, order=range(RIGHT)):
+    tiles = {}
+    for b in order:
         columns = pl.ds(b * BLOCK, BLOCK)
-        tiles.append(
-            [
-                pltpu.make_async_copy(source.at[:, columns], buffer.at[s, b], sems.at[s, b])
-                for s, source in enumerate(sources)
-            ]
-        )
-    for copies in tiles:
-        for copy in copies:
+        tiles[b] = [
+            pltpu.make_async_copy(source.at[:, columns], buffer.at[s, b], sems.at[s, b])
+            for s, source in enumerate(sources)
+        ]
+        for copy in tiles[b]:
             copy.start()
     return tiles
 
 
-def right_stats_kernel(first, second, out, buffer, sems):
-    tiles = fetched((first, second), buffer, sems)
+def right_stats_kernel(first, second, out, buffer, slots, sems, out_sems):
+    groups = ((RIGHT - 1,), (0, 1), (2, 3))
+    tiles = fetched((first, second), buffer, sems, sum(groups, ()))
     half = ROWS // 2
-    for group in ((0,), (1, 2), (3, 4)):
+    copies = []
+    for slot in range(ROWS):
+        slots[slot, BLOCK + 3 : BLOCK + 8, :] = jnp.zeros((5, HALF), f32)
+    for group in groups:
         for b in group:
             for copy in tiles[b]:
                 copy.wait()
@@ -171,14 +172,19 @@
             one, two = packed[2 * k : 2 * k + 2]
             for s, (quarters, diagonal) in enumerate((one, (one[0] + two[0], one[1] + two[1]))):
                 if b < RIGHT - 1:
-                    out[2 * b + s, :BLOCK, :] = quarters
-                    out[2 * b + s, BLOCK : BLOCK + 1, :] = diagonal
+                    slots[2 * b + s, :BLOCK, :] = quarters
+                    slots[2 * b + s, BLOCK : BLOCK + 1, :] = diagonal
                 else:
-                    out[s * half : (s + 1) * half, BLOCK + 8 :, :] = quarters.reshape(half, SHARE, HALF)
+                    slots[s * half : (s + 1) * half, BLOCK + 8 :, :] = quarters.reshape(half, SHARE, HALF)
                     for slot in range(ROWS):
-                        out[slot, BLOCK + 1 + s : BLOCK + 2 + s, :] = diagonal
-    for slot in range(ROWS):
-        out[slot, BLOCK + 3 : BLOCK + 8, :] = jnp.zeros((5, HALF), f32)
+                        slots[slot, BLOCK + 1 + s : BLOCK + 2 + s, :] = diagonal
+        for b in group:
+            if b < RIGHT - 1:
+                pair = pl.ds(2 * b, 2)
+                copies.append(pltpu.make_async_copy(slots.at[pair], out.at[pair], out_sems.at[b]))
+                copies[-1].start()
+    for copy in copies:
+        copy.wait()
 
 
 def left_stats_kernel(info, first, second, keep, send, buffer, sums, sems):
@@ -270,27 +276,28 @@
     chain = root_steps(statistics, found)
     copies = []
 
-    def stored(b):
-        copy = pltpu.make_async_copy(buffer.at[b], out.at[:, pl.ds(b * BLOCK, BLOCK)], out_sems.at[b])
+    def stored(b, start, size, sem):
+        rows = pl.ds(start, size)
+        copy = pltpu.make_async_copy(
+            buffer.at[b, rows], out.at[rows, pl.ds(b * BLOCK, BLOCK)], out_sems.at[sem]
+        )
         copy.start()
         copies.append(copy)
 
-    for _ in range(4):
+    for _ in range(7):
         next(chain)
     for copy in fetches:
         copy.wait()
     for b in range(RIGHT - 1):
         one, two = [parts(unpacked(gathered[2 * b + s, :PACK, :])) for s in range(2)]
         for _ in applied(held, b, one, two, buffer):
-            next(chain, None)
-        stored(b)
-        next(chain, None)
+            next(chain)
+        stored(b, 0, 2 * BLOCK, b)
     for _ in chain:
         pass
     last = RIGHT - 1
-    for _ in applied(held, last, parts(found[0]), parts(found[1]), buffer):
-        pass
-    stored(last)
+    for k, _ in enumerate(applied(held, last, parts(found[0]), parts(found[1]), buffer)):
+        stored(last, k * BLOCK, BLOCK, last + k)
     for copy in copies:
         copy.wait()
 
@@ -329,9 +336,12 @@
     right_parts = pl.pallas_call(
         right_stats_kernel,
         in_specs=[HBM, HBM],
-        out_specs=VMEM,
-        out_shape=jax.ShapeDtypeStruct((ROWS, SLOT, HALF), f32),
-        scratch_shapes=tiles + tile_sems,
+        out_specs=HBM,
+        out_shape=pltpu.HBM((ROWS, SLOT, HALF), f32),
+        scratch_shapes=tiles
+        + [pltpu.VMEM((ROWS, SLOT, HALF), f32)]
+        + tile_sems
+        + [pltpu.SemaphoreType.DMA((RIGHT - 1,))],
         compiler_params=params(),
         cost_estimate=cost(passes, grads),
         name="right_stats",
@@ -406,7 +416,7 @@
             pltpu.VMEM(held, bf16),
             pltpu.VMEM((RIGHT, rows, BLOCK), f32),
             tile_sem,
-            tile_sem,
+            pltpu.SemaphoreType.DMA((RIGHT + 1,)),
         ],
         out_shape=jax.ShapeDtypeStruct((rows, cols), f32),
         compiler_params=params(),

time: 67.9 us -> 66.8 us (0.984)
  Pallas kernels: 32.3 us -> 31.3 us
    pallas_call x1, Pallas kernels: 9.12 us -> 8.3 us  [body(): pl.pallas_call(finish_kernel, in_specs=[HBM, VMEM, VMEM], out_specs=HBM,...]
  transfers between devices with their start and end apart: 9 -> 9, of which waited for: 6 -> 6; matrix products, arithmetic and copies ran while one was open for 0% -> 0% of each run, Pallas kernels for 27% -> 28%
where the time goes in v5:
time: 66.8 us; the launch traced here: 66.6 us
  Pallas kernels  31.3 us (47%)
  starting transfers between devices  22.4 us (34%)
  waiting for transfers between devices  12.6 us (19%)
    ppermute x7, waiting for transfers between devices, swap(): return lax.ppermute(value, 'col', [(i, i ^ d) for i in range(COLS)])  12.6 us
    all_to_all x2, starting transfers between devices, exchanged(): return lax.all_to_all(slots, 'row', split_axis=0, concat_axis=0, tiled=True)  11.6 us
    ppermute x7, starting transfers between devices, swap(): return lax.ppermute(value, 'col', [(i, i ^ d) for i in range(COLS)])  10.8 us
    pallas_call x1, Pallas kernels, body(): pl.pallas_call(finish_kernel, in_specs=[HBM, VMEM, VMEM], out_specs=HBM,...  8.3 us
    pallas_call x1, Pallas kernels, body(): pl.pallas_call(halfway_kernel, in_specs=[SMEM, HBM, HBM, VMEM, VMEM], out...  5.65 us
    pallas_call x1, Pallas kernels, body(): pl.pallas_call(right_roots_kernel, in_specs=[VMEM], out_specs=[VMEM, VMEM...  5.24 us
    pallas_call x1, Pallas kernels, body(): pl.pallas_call(right_stats_kernel, in_specs=[HBM, HBM], out_specs=HBM, ou...  4.47 us
    pallas_call x1, Pallas kernels, body(): pl.pallas_call(left_root_kernel, in_specs=[VMEM, VMEM], out_specs=VMEM, o...  4.14 us
  transfers between devices with their start and end apart: 9, of which 6 were waited for; matrix products, arithmetic and copies ran while one was open for 0% of the time, Pallas kernels for 28%

profile of v5, /device:TPU:1, one launch (start us, length us, event | category | flops | bytes accessed | tf_op | source)
XLA Modules:
  0.0 66.6 jit_solution(1709977973895703114)
XLA Ops:
  0.0 4.5 %right_stats.1 = f32[8,328,128]{2,1,0:T(8,128)} custom-call(f32[512,1280]{1,0:T(8,128)} %first.5, f32[512,1280]{1,0:T(8,128)} %second.5), custom_call_target="tpu_custom_call" | custom-call | flops 2013265920 | bytes 5242880 | tf_op jit(solution)/shard_map/right_stats/pallas_call | solution.py:336
  4.5 6.8 %all-to-all-start = ((f32[8,328,128]{2,1,0:T(8,128)}), f32[8,328,128]{2,1,0:T(8,128)S(1)}, u32[]{:S(2)}, u32[]{:S(2)}) async-start(f32[8,328,128]{2,1,0:T(8,128)} %right_stats.1), calls=%async_computation | async-start | bytes 2686976 | tf_op jit(solution)/shard_map/all_to_all | solution.py:29
  11.3 3.5 %left_stats.1 = (f32[528,128]{1,0:T(8,128)S(1)}, f32[528,128]{1,0:T(8,128)S(1)}) custom-call(s32[1]{0:T(128)} %bitcast.info, f32[512,1280]{1,0:T(8,128)} %first.5, f32[512,1280]{1,0:T(8,128)} %second.5), custom_call_target="tpu_custom_call" | custom-call | flops 2013265920 | bytes 5242880 | tf_op jit(solution)/shard_map/left_stats/pallas_call | solution.py:352
  14.8 1.0 %collective-permute-start = (f32[528,128]{1,0:T(8,128)S(1)}, f32[528,128]{1,0:T(8,128)S(1)}, u32[]{:S(2)}, u32[]{:S(2)}) collective-permute-start(f32[528,128]{1,0:T(8,128)S(1)} %get-tuple-element.20), channel_id=1, source_target_pairs={{0,1},{1,0},{2,3},{3,2},{4,5},{5,4},{6,7},{7,6},{8,9},{9,8},{10,11... | collective-permute-start | bytes 811016 | tf_op jit(solution)/shard_map/ppermute | solution.py:25
  15.8 1.2 %collective-permute-done = f32[528,128]{1,0:T(8,128)S(1)} collective-permute-done((f32[528,128]{1,0:T(8,128)S(1)}, f32[528,128]{1,0:T(8,128)S(1)}, u32[]{:S(2)}, u32[]{:S(2)}) %collective-permute-start) | collective-permute-done | bytes 270368 | tf_op jit(solution)/shard_map/ppermute | solution.py:25
  17.1 2.8 %collective-permute-start.3 = (f32[264,128]{1,0:T(8,128)S(1)}, f32[264,128]{1,0:T(8,128)S(1)}, u32[]{:S(2)}, u32[]{:S(2)}) collective-permute-start(f32[264,128]{1,0:T(8,128)S(1)} %get-tuple-element.29), channel_id=1, source_target_pairs={{0,12},{1,13},{2,14},{3,15},{4,8},{5,9},{6,10},{7,11},{8,4},{9,5},... | collective-permute-start | bytes 405512 | tf_op jit(solution)/shard_map/ppermute | solution.py:25
  19.9 0.0 collective-permute-start.1
  19.9 1.3 %collective-permute-start.2 = (f32[264,128]{1,0:T(8,128)S(1)}, f32[264,128]{1,0:T(8,128)S(1)}, u32[]{:S(2)}, u32[]{:S(2)}) collective-permute-start(f32[264,128]{1,0:T(8,128)S(1)} %get-tuple-element.30), channel_id=1, source_target_pairs={{0,8},{1,9},{2,10},{3,11},{4,12},{5,13},{6,14},{7,15},{8,0},{9,1},... | collective-permute-start | bytes 405512 | tf_op jit(solution)/shard_map/ppermute | solution.py:25
  21.2 2.1 %collective-permute-done.3 = f32[264,128]{1,0:T(8,128)S(1)} collective-permute-done((f32[264,128]{1,0:T(8,128)S(1)}, f32[264,128]{1,0:T(8,128)S(1)}, u32[]{:S(2)}, u32[]{:S(2)}) %collective-permute-start.3) | collective-permute-done | bytes 135200 | tf_op jit(solution)/shard_map/ppermute | solution.py:25
  23.3 1.1 %collective-permute-done.1 = f32[264,128]{1,0:T(8,128)S(1)} collective-permute-done((f32[264,128]{1,0:T(8,128)S(1)}, f32[264,128]{1,0:T(8,128)S(1)}, u32[]{:S(2)}, u32[]{:S(2)}) %collective-permute-start.1) | collective-permute-done | bytes 135200 | tf_op jit(solution)/shard_map/ppermute | solution.py:25
  24.4 2.9 %collective-permute-done.2 = f32[264,128]{1,0:T(8,128)S(1)} collective-permute-done((f32[264,128]{1,0:T(8,128)S(1)}, f32[264,128]{1,0:T(8,128)S(1)}, u32[]{:S(2)}, u32[]{:S(2)}) %collective-permute-start.2) | collective-permute-done | bytes 135200 | tf_op jit(solution)/shard_map/ppermute | solution.py:25
  27.3 2.5 %collective-permute-start.4 = (f32[264,128]{1,0:T(8,128)S(1)}, f32[264,128]{1,0:T(8,128)S(1)}, u32[]{:S(2)}, u32[]{:S(2)}) collective-permute-start(f32[264,128]{1,0:T(8,128)S(1)} %add_add_fusion.own), channel_id=1, source_target_pairs={{0,2},{1,3},{2,0},{3,1},{4,6},{5,7},{6,4},{7,5},{8,10},{9,11},{10,... | collective-permute-start | bytes 405512 | tf_op jit(solution)/shard_map/ppermute | solution.py:25
  29.8 0.0 all-to-all-done.arrived
  29.8 5.2 %right_roots.1 = (f32[8,328,128]{2,1,0:T(8,128)}, f32[8,128]{1,0:T(8,128)S(1)}) custom-call(f32[8,328,128]{2,1,0:T(8,128)S(1)} %all-to-all-done.arrived), custom_call_target="tpu_custom_call" | custom-call | flops 2013265920 | bytes 2686976 | tf_op jit(solution)/shard_map/right_roots/pallas_call | solution.py:369
  35.1 0.0 collective-permute-done.4.other
  35.1 4.8 %all-to-all-start.1 = ((f32[8,328,128]{2,1,0:T(8,128)}), f32[8,328,128]{2,1,0:T(8,128)S(1)}, u32[]{:S(2)}, u32[]{:S(2)}) async-start(f32[8,328,128]{2,1,0:T(8,128)} %get-tuple-element.27), calls=%async_computation.1 | async-start | bytes 2686976 | tf_op jit(solution)/shard_map/all_to_all | solution.py:29
  39.9 4.1 %left_root.1 = f32[264,128]{1,0:T(8,128)S(1)} custom-call(f32[264,128]{1,0:T(8,128)S(1)} %add_add_fusion.own, f32[264,128]{1,0:T(8,128)S(1)} %collective-permute-done.4.other), custom_call_target="tpu_custom_call" | custom-call | flops 2013265920 | bytes 405504 | tf_op jit(solution)/shard_map/left_root/pallas_call | solution.py:381
  44.0 0.1 collective-permute-start.5
  44.1 4.1 %collective-permute-done.5 = f32[264,128]{1,0:T(8,128)S(1)} collective-permute-done((f32[264,128]{1,0:T(8,128)S(1)}, f32[264,128]{1,0:T(8,128)S(1)}, u32[]{:S(2)}, u32[]{:S(2)}) %collective-permute-start.5) | collective-permute-done | bytes 135200 | tf_op jit(solution)/shard_map/ppermute | solution.py:25
  48.3 3.0 %collective-permute-start.6 = (f32[528,128]{1,0:T(8,128)S(1)}, f32[528,128]{1,0:T(8,128)S(1)}, u32[]{:S(2)}, u32[]{:S(2)}) collective-permute-start(f32[528,128]{1,0:T(8,128)S(1)} %maximum_select_fusion.mine), channel_id=1, source_target_pairs={{0,1},{1,0},{2,3},{3,2},{4,5},{5,4},{6,7},{7,6},{8,9},{9,8},{10,11... | collective-permute-start | bytes 811016 | tf_op jit(solution)/shard_map/ppermute | solution.py:25
  51.3 1.2 %collective-permute-done.6.other = f32[528,128]{1,0:T(8,128)S(1)} collective-permute-done((f32[528,128]{1,0:T(8,128)S(1)}, f32[528,128]{1,0:T(8,128)S(1)}, u32[]{:S(2)}, u32[]{:S(2)}) %collective-permute-start.6) | collective-permute-done | bytes 270368 | tf_op jit(solution)/shard_map/ppermute | solution.py:25
  52.5 5.6 %halfway.1 = bf16[5,4,512,256]{3,2,1,0:T(8,128)(2,1)} custom-call(s32[1]{0:T(128)} %bitcast.info, f32[512,1280]{1,0:T(8,128)} %first.5, f32[512,1280]{1,0:T(8,128)} %second.5, f32[528,128]{1,0:T(8,128)S(1)} %maximum_select_fusion.mine, f32[528,128]{1,0:T(8,128)S(1)} %collective-permute-done.6.other), custom_call_target="tpu_custom_call" | custom-call | flops 2013265920 | bytes 10485760 | tf_op jit(solution)/shard_map/halfway/pallas_call | solution.py:400
  58.1 0.0 all-to-all-done.1.gathered
  58.2 8.3 %finish.1 = f32[512,1280]{1,0:T(8,128)} custom-call(bf16[5,4,512,256]{3,2,1,0:T(8,128)(2,1)} %halfway.1, f32[8,328,128]{2,1,0:T(8,128)S(1)} %all-to-all-done.1.gathered, f32[8,128]{1,0:T(8,128)S(1)} %get-tuple-element.28.diagonals), custom_call_target="tpu_custom_call" | custom-call | flops 6039797760 | bytes 10485760 | tf_op jit(solution)/shard_map/finish/pallas_call | solution.py:411
  (4 shorter events, 0.1 us)
Async XLA Ops:
  4.5 25.4 %all-to-all-start = ((f32[8,328,128]{2,1,0:T(8,128)}), f32[8,328,128]{2,1,0:T(8,128)S(1)}, u32[]{:S(2)}, u32[]{:S(2)}) async-start(f32[8,328,128]{2,1,0:T(8,128)} %right_stats.1), calls=%async_computation | async-start | bytes 2686976 | tf_op jit(solution)/shard_map/all_to_all | solution.py:29
  14.8 2.2 %collective-permute-start = (f32[528,128]{1,0:T(8,128)S(1)}, f32[528,128]{1,0:T(8,128)S(1)}, u32[]{:S(2)}, u32[]{:S(2)}) collective-permute-start(f32[528,128]{1,0:T(8,128)S(1)} %get-tuple-element.20), channel_id=1, source_target_pairs={{0,1},{1,0},{2,3},{3,2},{4,5},{5,4},{6,7},{7,6},{8,9},{9,8},{10,11... | collective-permute-start | bytes 811016 | tf_op jit(solution)/shard_map/ppermute | solution.py:25
  17.1 6.2 %collective-permute-start.3 = (f32[264,128]{1,0:T(8,128)S(1)}, f32[264,128]{1,0:T(8,128)S(1)}, u32[]{:S(2)}, u32[]{:S(2)}) collective-permute-start(f32[264,128]{1,0:T(8,128)S(1)} %get-tuple-element.29), channel_id=1, source_target_pairs={{0,12},{1,13},{2,14},{3,15},{4,8},{5,9},{6,10},{7,11},{8,4},{9,5},... | collective-permute-start | bytes 405512 | tf_op jit(solution)/shard_map/ppermute | solution.py:25
  19.9 4.5 %collective-permute-start.1 = (f32[264,128]{1,0:T(8,128)S(1)}, f32[264,128]{1,0:T(8,128)S(1)}, u32[]{:S(2)}, u32[]{:S(2)}) collective-permute-start(f32[264,128]{1,0:T(8,128)S(1)} %get-tuple-element.29), channel_id=1, source_target_pairs={{0,4},{1,5},{2,6},{3,7},{4,0},{5,1},{6,2},{7,3},{8,12},{9,13},{10,... | collective-permute-start | bytes 405512 | tf_op jit(solution)/shard_map/ppermute | solution.py:25
  19.9 7.4 %collective-permute-start.2 = (f32[264,128]{1,0:T(8,128)S(1)}, f32[264,128]{1,0:T(8,128)S(1)}, u32[]{:S(2)}, u32[]{:S(2)}) collective-permute-start(f32[264,128]{1,0:T(8,128)S(1)} %get-tuple-element.30), channel_id=1, source_target_pairs={{0,8},{1,9},{2,10},{3,11},{4,12},{5,13},{6,14},{7,15},{8,0},{9,1},... | collective-permute-start | bytes 405512 | tf_op jit(solution)/shard_map/ppermute | solution.py:25
  27.3 7.8 %collective-permute-start.4 = (f32[264,128]{1,0:T(8,128)S(1)}, f32[264,128]{1,0:T(8,128)S(1)}, u32[]{:S(2)}, u32[]{:S(2)}) collective-permute-start(f32[264,128]{1,0:T(8,128)S(1)} %add_add_fusion.own), channel_id=1, source_target_pairs={{0,2},{1,3},{2,0},{3,1},{4,6},{5,7},{6,4},{7,5},{8,10},{9,11},{10,... | collective-permute-start | bytes 405512 | tf_op jit(solution)/shard_map/ppermute | solution.py:25
  35.1 23.1 %all-to-all-start.1 = ((f32[8,328,128]{2,1,0:T(8,128)}), f32[8,328,128]{2,1,0:T(8,128)S(1)}, u32[]{:S(2)}, u32[]{:S(2)}) async-start(f32[8,328,128]{2,1,0:T(8,128)} %get-tuple-element.27), calls=%async_computation.1 | async-start | bytes 2686976 | tf_op jit(solution)/shard_map/all_to_all | solution.py:29
  44.0 4.2 %collective-permute-start.5 = (f32[264,128]{1,0:T(8,128)S(1)}, f32[264,128]{1,0:T(8,128)S(1)}, u32[]{:S(2)}, u32[]{:S(2)}) collective-permute-start(f32[264,128]{1,0:T(8,128)S(1)} %left_root.1), channel_id=1, source_target_pairs={{0,4},{1,5},{2,6},{3,7},{4,0},{5,1},{6,2},{7,3},{8,12},{9,13},{10,... | collective-permute-start | bytes 405512 | tf_op jit(solution)/shard_map/ppermute | solution.py:25
  48.3 4.2 %collective-permute-start.6 = (f32[528,128]{1,0:T(8,128)S(1)}, f32[528,128]{1,0:T(8,128)S(1)}, u32[]{:S(2)}, u32[]{:S(2)}) collective-permute-start(f32[528,128]{1,0:T(8,128)S(1)} %maximum_select_fusion.mine), channel_id=1, source_target_pairs={{0,1},{1,0},{2,3},{3,2},{4,5},{5,4},{6,7},{7,6},{8,9},{9,8},{10,11... | collective-permute-start | bytes 811016 | tf_op jit(solution)/shard_map/ppermute | solution.py:25

commit v6 on v5

--- a/solution.py
+++ b/solution.py
@@ -387,13 +387,15 @@
         cost_estimate=cost(newton, 3 * PACK * HALF * 4),
         name="left_root",
     )(*left_in)
-    left_other = swap(left_root, 4)
-    mine = jnp.where(
-        low_y == 0,
-        jnp.concatenate([left_root, left_other]),
-        jnp.concatenate([left_other, left_root]),
-    )
-    other = swap(mine, 1)
+    def ordered(own_step, other_step):
+        return jnp.where(
+            low_y == 0,
+            jnp.concatenate([own_step, other_step]),
+            jnp.concatenate([other_step, own_step]),
+        )
+
+    from_y, from_core, from_both = swap(left_root, 4), swap(left_root, 1), swap(left_root, 5)
+    mine, other = ordered(left_root, from_y), ordered(from_core, from_both)
 
     held = (RIGHT, 4, rows, BLOCK)
     tile_sem = pltpu.SemaphoreType.DMA((RIGHT,))

time: 66.8 us -> 67.9 us (1.016)
    ppermute x7 -> x8, starting transfers between devices: 10.8 us -> 11.3 us  [swap(): return lax.ppermute(value, 'col', [(i, i ^ d) for i in range(COLS)])]
    ppermute x7 -> x8, waiting for transfers between devices: 12.6 us -> 13.1 us  [swap(): return lax.ppermute(value, 'col', [(i, i ^ d) for i in range(COLS)])]
  transfers between devices with their start and end apart: 9 -> 10, of which waited for: 6 -> 6; matrix products, arithmetic and copies ran while one was open for 0% -> 0% of each run, Pallas kernels for 28% -> 27%
where the time goes in v6:
time: 67.9 us; the launch traced here: 67.7 us
  Pallas kernels  31.3 us (46%)
  starting transfers between devices  22.9 us (34%)
  waiting for transfers between devices  13.1 us (19%)
    ppermute x8, waiting for transfers between devices, swap(): return lax.ppermute(value, 'col', [(i, i ^ d) for i in range(COLS)])  13.1 us
    all_to_all x2, starting transfers between devices, exchanged(): return lax.all_to_all(slots, 'row', split_axis=0, concat_axis=0, tiled=True)  11.6 us
    ppermute x8, starting transfers between devices, swap(): return lax.ppermute(value, 'col', [(i, i ^ d) for i in range(COLS)])  11.3 us
    pallas_call x1, Pallas kernels, body(): pl.pallas_call(finish_kernel, in_specs=[HBM, VMEM, VMEM], out_specs=HBM,...  8.31 us
    pallas_call x1, Pallas kernels, body(): pl.pallas_call(halfway_kernel, in_specs=[SMEM, HBM, HBM, VMEM, VMEM], out...  5.67 us
    pallas_call x1, Pallas kernels, body(): pl.pallas_call(right_roots_kernel, in_specs=[VMEM], out_specs=[VMEM, VMEM...  5.24 us
    pallas_call x1, Pallas kernels, body(): pl.pallas_call(right_stats_kernel, in_specs=[HBM, HBM], out_specs=HBM, ou...  4.47 us
    pallas_call x1, Pallas kernels, body(): pl.pallas_call(left_root_kernel, in_specs=[VMEM, VMEM], out_specs=VMEM, o...  4.14 us
  transfers between devices with their start and end apart: 10, of which 6 were waited for; matrix products, arithmetic and copies ran while one was open for 0% of the time, Pallas kernels for 27%

profile of v6, /device:TPU:1, one launch (start us, length us, event | category | flops | bytes accessed | tf_op | source)
XLA Modules:
  0.0 67.7 jit_solution(16393437012416721245)
XLA Ops:
  0.0 4.5 %right_stats.1 = f32[8,328,128]{2,1,0:T(8,128)} custom-call(f32[512,1280]{1,0:T(8,128)} %first.5, f32[512,1280]{1,0:T(8,128)} %second.5), custom_call_target="tpu_custom_call" | custom-call | flops 2013265920 | bytes 5242880 | tf_op jit(solution)/shard_map/right_stats/pallas_call | solution.py:336
  4.5 6.8 %all-to-all-start = ((f32[8,328,128]{2,1,0:T(8,128)}), f32[8,328,128]{2,1,0:T(8,128)S(1)}, u32[]{:S(2)}, u32[]{:S(2)}) async-start(f32[8,328,128]{2,1,0:T(8,128)} %right_stats.1), calls=%async_computation | async-start | bytes 2686976 | tf_op jit(solution)/shard_map/all_to_all | solution.py:29
  11.3 3.5 %left_stats.1 = (f32[528,128]{1,0:T(8,128)S(1)}, f32[528,128]{1,0:T(8,128)S(1)}) custom-call(s32[1]{0:T(128)} %bitcast.info, f32[512,1280]{1,0:T(8,128)} %first.5, f32[512,1280]{1,0:T(8,128)} %second.5), custom_call_target="tpu_custom_call" | custom-call | flops 2013265920 | bytes 5242880 | tf_op jit(solution)/shard_map/left_stats/pallas_call | solution.py:352
  14.8 1.0 %collective-permute-start = (f32[528,128]{1,0:T(8,128)S(1)}, f32[528,128]{1,0:T(8,128)S(1)}, u32[]{:S(2)}, u32[]{:S(2)}) collective-permute-start(f32[528,128]{1,0:T(8,128)S(1)} %get-tuple-element.20), channel_id=1, source_target_pairs={{0,1},{1,0},{2,3},{3,2},{4,5},{5,4},{6,7},{7,6},{8,9},{9,8},{10,11... | collective-permute-start | bytes 811016 | tf_op jit(solution)/shard_map/ppermute | solution.py:25
  15.8 1.2 %collective-permute-done = f32[528,128]{1,0:T(8,128)S(1)} collective-permute-done((f32[528,128]{1,0:T(8,128)S(1)}, f32[528,128]{1,0:T(8,128)S(1)}, u32[]{:S(2)}, u32[]{:S(2)}) %collective-permute-start) | collective-permute-done | bytes 270368 | tf_op jit(solution)/shard_map/ppermute | solution.py:25
  17.1 2.8 %collective-permute-start.3 = (f32[264,128]{1,0:T(8,128)S(1)}, f32[264,128]{1,0:T(8,128)S(1)}, u32[]{:S(2)}, u32[]{:S(2)}) collective-permute-start(f32[264,128]{1,0:T(8,128)S(1)} %get-tuple-element.29), channel_id=1, source_target_pairs={{0,12},{1,13},{2,14},{3,15},{4,8},{5,9},{6,10},{7,11},{8,4},{9,5},... | collective-permute-start | bytes 405512 | tf_op jit(solution)/shard_map/ppermute | solution.py:25
  19.9 0.0 collective-permute-start.1
  19.9 1.3 %collective-permute-start.2 = (f32[264,128]{1,0:T(8,128)S(1)}, f32[264,128]{1,0:T(8,128)S(1)}, u32[]{:S(2)}, u32[]{:S(2)}) collective-permute-start(f32[264,128]{1,0:T(8,128)S(1)} %get-tuple-element.30), channel_id=1, source_target_pairs={{0,8},{1,9},{2,10},{3,11},{4,12},{5,13},{6,14},{7,15},{8,0},{9,1},... | collective-permute-start | bytes 405512 | tf_op jit(solution)/shard_map/ppermute | solution.py:25
  21.2 2.1 %collective-permute-done.3 = f32[264,128]{1,0:T(8,128)S(1)} collective-permute-done((f32[264,128]{1,0:T(8,128)S(1)}, f32[264,128]{1,0:T(8,128)S(1)}, u32[]{:S(2)}, u32[]{:S(2)}) %collective-permute-start.3) | collective-permute-done | bytes 135200 | tf_op jit(solution)/shard_map/ppermute | solution.py:25
  23.3 1.1 %collective-permute-done.1 = f32[264,128]{1,0:T(8,128)S(1)} collective-permute-done((f32[264,128]{1,0:T(8,128)S(1)}, f32[264,128]{1,0:T(8,128)S(1)}, u32[]{:S(2)}, u32[]{:S(2)}) %collective-permute-start.1) | collective-permute-done | bytes 135200 | tf_op jit(solution)/shard_map/ppermute | solution.py:25
  24.4 2.9 %collective-permute-done.2 = f32[264,128]{1,0:T(8,128)S(1)} collective-permute-done((f32[264,128]{1,0:T(8,128)S(1)}, f32[264,128]{1,0:T(8,128)S(1)}, u32[]{:S(2)}, u32[]{:S(2)}) %collective-permute-start.2) | collective-permute-done | bytes 135200 | tf_op jit(solution)/shard_map/ppermute | solution.py:25
  27.3 2.5 %collective-permute-start.4 = (f32[264,128]{1,0:T(8,128)S(1)}, f32[264,128]{1,0:T(8,128)S(1)}, u32[]{:S(2)}, u32[]{:S(2)}) collective-permute-start(f32[264,128]{1,0:T(8,128)S(1)} %add_add_fusion.own), channel_id=1, source_target_pairs={{0,2},{1,3},{2,0},{3,1},{4,6},{5,7},{6,4},{7,5},{8,10},{9,11},{10,... | collective-permute-start | bytes 405512 | tf_op jit(solution)/shard_map/ppermute | solution.py:25
  29.8 0.0 all-to-all-done.arrived
  29.8 5.2 %right_roots.1 = (f32[8,328,128]{2,1,0:T(8,128)}, f32[8,128]{1,0:T(8,128)S(1)}) custom-call(f32[8,328,128]{2,1,0:T(8,128)S(1)} %all-to-all-done.arrived), custom_call_target="tpu_custom_call" | custom-call | flops 2013265920 | bytes 2686976 | tf_op jit(solution)/shard_map/right_roots/pallas_call | solution.py:369
  35.1 0.0 collective-permute-done.4.other
  35.1 4.8 %all-to-all-start.1 = ((f32[8,328,128]{2,1,0:T(8,128)}), f32[8,328,128]{2,1,0:T(8,128)S(1)}, u32[]{:S(2)}, u32[]{:S(2)}) async-start(f32[8,328,128]{2,1,0:T(8,128)} %get-tuple-element.27), calls=%async_computation.1 | async-start | bytes 2686976 | tf_op jit(solution)/shard_map/all_to_all | solution.py:29
  39.9 4.1 %left_root.1 = f32[264,128]{1,0:T(8,128)S(1)} custom-call(f32[264,128]{1,0:T(8,128)S(1)} %add_add_fusion.own, f32[264,128]{1,0:T(8,128)S(1)} %collective-permute-done.4.other), custom_call_target="tpu_custom_call" | custom-call | flops 2013265920 | bytes 405504 | tf_op jit(solution)/shard_map/left_root/pallas_call | solution.py:381
  44.0 0.1 collective-permute-start.5
  44.1 2.4 %collective-permute-start.6 = (f32[264,128]{1,0:T(8,128)S(1)}, f32[264,128]{1,0:T(8,128)S(1)}, u32[]{:S(2)}, u32[]{:S(2)}) collective-permute-start(f32[264,128]{1,0:T(8,128)S(1)} %left_root.1), channel_id=1, source_target_pairs={{0,1},{1,0},{2,3},{3,2},{4,5},{5,4},{6,7},{7,6},{8,9},{9,8},{10,11... | collective-permute-start | bytes 405512 | tf_op jit(solution)/shard_map/ppermute | solution.py:25
  46.5 1.1 %collective-permute-start.7 = (f32[264,128]{1,0:T(8,128)S(1)}, f32[264,128]{1,0:T(8,128)S(1)}, u32[]{:S(2)}, u32[]{:S(2)}) collective-permute-start(f32[264,128]{1,0:T(8,128)S(1)} %left_root.1), channel_id=1, source_target_pairs={{0,5},{1,4},{2,7},{3,6},{4,1},{5,0},{6,3},{7,2},{8,13},{9,12},{10,... | collective-permute-start | bytes 405512 | tf_op jit(solution)/shard_map/ppermute | solution.py:25
  47.6 0.6 collective-permute-done.5
  48.3 0.0 collective-permute-done.6
  48.3 5.2 %collective-permute-done.7 = f32[264,128]{1,0:T(8,128)S(1)} collective-permute-done((f32[264,128]{1,0:T(8,128)S(1)}, f32[264,128]{1,0:T(8,128)S(1)}, u32[]{:S(2)}, u32[]{:S(2)}) %collective-permute-start.7) | collective-permute-done | bytes 135200 | tf_op jit(solution)/shard_map/ppermute | solution.py:25
  53.5 5.7 %halfway.1 = bf16[5,4,512,256]{3,2,1,0:T(8,128)(2,1)} custom-call(s32[1]{0:T(128)} %bitcast.info, f32[512,1280]{1,0:T(8,128)} %first.5, f32[512,1280]{1,0:T(8,128)} %second.5, f32[528,128]{1,0:T(8,128)S(1)} %maximum_select_fusion.mine, f32[528,128]{1,0:T(8,128)S(1)} %maximum_select_fusion.1.other), custom_call_target="tpu_custom_call" | custom-call | flops 2013265920 | bytes 10485760 | tf_op jit(solution)/shard_map/halfway/pallas_call | solution.py:402
  59.2 0.0 all-to-all-done.1.gathered
  59.2 8.3 %finish.1 = f32[512,1280]{1,0:T(8,128)} custom-call(bf16[5,4,512,256]{3,2,1,0:T(8,128)(2,1)} %halfway.1, f32[8,328,128]{2,1,0:T(8,128)S(1)} %all-to-all-done.1.gathered, f32[8,128]{1,0:T(8,128)S(1)} %get-tuple-element.28.diagonals), custom_call_target="tpu_custom_call" | custom-call | flops 6039797760 | bytes 10485760 | tf_op jit(solution)/shard_map/finish/pallas_call | solution.py:413
  (5 shorter events, 0.1 us)
Async XLA Ops:
  4.5 25.4 %all-to-all-start = ((f32[8,328,128]{2,1,0:T(8,128)}), f32[8,328,128]{2,1,0:T(8,128)S(1)}, u32[]{:S(2)}, u32[]{:S(2)}) async-start(f32[8,328,128]{2,1,0:T(8,128)} %right_stats.1), calls=%async_computation | async-start | bytes 2686976 | tf_op jit(solution)/shard_map/all_to_all | solution.py:29
  14.8 2.2 %collective-permute-start = (f32[528,128]{1,0:T(8,128)S(1)}, f32[528,128]{1,0:T(8,128)S(1)}, u32[]{:S(2)}, u32[]{:S(2)}) collective-permute-start(f32[528,128]{1,0:T(8,128)S(1)} %get-tuple-element.20), channel_id=1, source_target_pairs={{0,1},{1,0},{2,3},{3,2},{4,5},{5,4},{6,7},{7,6},{8,9},{9,8},{10,11... | collective-permute-start | bytes 811016 | tf_op jit(solution)/shard_map/ppermute | solution.py:25
  17.1 6.2 %collective-permute-start.3 = (f32[264,128]{1,0:T(8,128)S(1)}, f32[264,128]{1,0:T(8,128)S(1)}, u32[]{:S(2)}, u32[]{:S(2)}) collective-permute-start(f32[264,128]{1,0:T(8,128)S(1)} %get-tuple-element.29), channel_id=1, source_target_pairs={{0,12},{1,13},{2,14},{3,15},{4,8},{5,9},{6,10},{7,11},{8,4},{9,5},... | collective-permute-start | bytes 405512 | tf_op jit(solution)/shard_map/ppermute | solution.py:25
  19.9 4.5 %collective-permute-start.1 = (f32[264,128]{1,0:T(8,128)S(1)}, f32[264,128]{1,0:T(8,128)S(1)}, u32[]{:S(2)}, u32[]{:S(2)}) collective-permute-start(f32[264,128]{1,0:T(8,128)S(1)} %get-tuple-element.29), channel_id=1, source_target_pairs={{0,4},{1,5},{2,6},{3,7},{4,0},{5,1},{6,2},{7,3},{8,12},{9,13},{10,... | collective-permute-start | bytes 405512 | tf_op jit(solution)/shard_map/ppermute | solution.py:25
  19.9 7.4 %collective-permute-start.2 = (f32[264,128]{1,0:T(8,128)S(1)}, f32[264,128]{1,0:T(8,128)S(1)}, u32[]{:S(2)}, u32[]{:S(2)}) collective-permute-start(f32[264,128]{1,0:T(8,128)S(1)} %get-tuple-element.30), channel_id=1, source_target_pairs={{0,8},{1,9},{2,10},{3,11},{4,12},{5,13},{6,14},{7,15},{8,0},{9,1},... | collective-permute-start | bytes 405512 | tf_op jit(solution)/shard_map/ppermute | solution.py:25
  27.3 7.8 %collective-permute-start.4 = (f32[264,128]{1,0:T(8,128)S(1)}, f32[264,128]{1,0:T(8,128)S(1)}, u32[]{:S(2)}, u32[]{:S(2)}) collective-permute-start(f32[264,128]{1,0:T(8,128)S(1)} %add_add_fusion.own), channel_id=1, source_target_pairs={{0,2},{1,3},{2,0},{3,1},{4,6},{5,7},{6,4},{7,5},{8,10},{9,11},{10,... | collective-permute-start | bytes 405512 | tf_op jit(solution)/shard_map/ppermute | solution.py:25
  35.1 24.1 %all-to-all-start.1 = ((f32[8,328,128]{2,1,0:T(8,128)}), f32[8,328,128]{2,1,0:T(8,128)S(1)}, u32[]{:S(2)}, u32[]{:S(2)}) async-start(f32[8,328,128]{2,1,0:T(8,128)} %get-tuple-element.27), calls=%async_computation.1 | async-start | bytes 2686976 | tf_op jit(solution)/shard_map/all_to_all | solution.py:29
  44.0 4.2 %collective-permute-start.5 = (f32[264,128]{1,0:T(8,128)S(1)}, f32[264,128]{1,0:T(8,128)S(1)}, u32[]{:S(2)}, u32[]{:S(2)}) collective-permute-start(f32[264,128]{1,0:T(8,128)S(1)} %left_root.1), channel_id=1, source_target_pairs={{0,4},{1,5},{2,6},{3,7},{4,0},{5,1},{6,2},{7,3},{8,12},{9,13},{10,... | collective-permute-start | bytes 405512 | tf_op jit(solution)/shard_map/ppermute | solution.py:25
  44.1 4.2 %collective-permute-start.6 = (f32[264,128]{1,0:T(8,128)S(1)}, f32[264,128]{1,0:T(8,128)S(1)}, u32[]{:S(2)}, u32[]{:S(2)}) collective-permute-start(f32[264,128]{1,0:T(8,128)S(1)} %left_root.1), channel_id=1, source_target_pairs={{0,1},{1,0},{2,3},{3,2},{4,5},{5,4},{6,7},{7,6},{8,9},{9,8},{10,11... | collective-permute-start | bytes 405512 | tf_op jit(solution)/shard_map/ppermute | solution.py:25
  46.5 6.9 %collective-permute-start.7 = (f32[264,128]{1,0:T(8,128)S(1)}, f32[264,128]{1,0:T(8,128)S(1)}, u32[]{:S(2)}, u32[]{:S(2)}) collective-permute-start(f32[264,128]{1,0:T(8,128)S(1)} %left_root.1), channel_id=1, source_target_pairs={{0,5},{1,4},{2,7},{3,6},{4,1},{5,0},{6,3},{7,2},{8,13},{9,12},{10,... | collective-permute-start | bytes 405512 | tf_op jit(solution)/shard_map/ppermute | solution.py:25

commit v7 on v5

--- a/solution.py
+++ b/solution.py
@@ -362,7 +362,7 @@
     both = (keep + swap(send, 1)).reshape(2, PACK, HALF)
     own = lax.dynamic_index_in_dim(both, low_y, 0, keepdims=False)
     rest = lax.dynamic_index_in_dim(both, 1 - low_y, 0, keepdims=False)
-    own = (own + swap(rest, 4)) + (swap(own, 8) + swap(rest, 12))
+    own = (own + swap(own, 8)) + (swap(rest, 4) + swap(rest, 12))
     left_in = [own, swap(own, 2)]
     own, arrived = lax.optimization_barrier((own, arrived))
 

time: 66.8 us -> 66.1 us (0.990)
  waiting for transfers between devices: 12.6 us -> 11 us
  starting transfers between devices: 22.4 us -> 23.3 us
    ppermute x7, waiting for transfers between devices: 12.6 us -> 10.9 us  [swap(): return lax.ppermute(value, 'col', [(i, i ^ d) for i in range(COLS)])]
    ppermute x7, starting transfers between devices: 10.8 us -> 11.8 us  [swap(): return lax.ppermute(value, 'col', [(i, i ^ d) for i in range(COLS)])]
  transfers between devices with their start and end apart: 9 -> 9, of which waited for: 6 -> 7; matrix products, arithmetic and copies ran while one was open for 0% -> 0% of each run, Pallas kernels for 28% -> 28%
where the time goes in v7:
time: 66.1 us; the launch traced here: 65.9 us
  Pallas kernels  31.3 us (47%)
  starting transfers between devices  23.3 us (35%)
  waiting for transfers between devices  11 us (17%)
    ppermute x7, starting transfers between devices, swap(): return lax.ppermute(value, 'col', [(i, i ^ d) for i in range(COLS)])  11.8 us
    all_to_all x2, starting transfers between devices, exchanged(): return lax.all_to_all(slots, 'row', split_axis=0, concat_axis=0, tiled=True)  11.5 us
    ppermute x7, waiting for transfers between devices, swap(): return lax.ppermute(value, 'col', [(i, i ^ d) for i in range(COLS)])  10.9 us
    pallas_call x1, Pallas kernels, body(): pl.pallas_call(finish_kernel, in_specs=[HBM, VMEM, VMEM], out_specs=HBM,...  8.3 us
    pallas_call x1, Pallas kernels, body(): pl.pallas_call(halfway_kernel, in_specs=[SMEM, HBM, HBM, VMEM, VMEM], out...  5.65 us
    pallas_call x1, Pallas kernels, body(): pl.pallas_call(right_roots_kernel, in_specs=[VMEM], out_specs=[VMEM, VMEM...  5.24 us
    pallas_call x1, Pallas kernels, body(): pl.pallas_call(right_stats_kernel, in_specs=[HBM, HBM], out_specs=HBM, ou...  4.47 us
    pallas_call x1, Pallas kernels, body(): pl.pallas_call(left_root_kernel, in_specs=[VMEM, VMEM], out_specs=VMEM, o...  4.14 us
  transfers between devices with their start and end apart: 9, of which 7 were waited for; matrix products, arithmetic and copies ran while one was open for 0% of the time, Pallas kernels for 28%

profile of v7, /device:TPU:1, one launch (start us, length us, event | category | flops | bytes accessed | tf_op | source)
XLA Modules:
  0.0 65.9 jit_solution(10831445357908751836)
XLA Ops:
  0.0 4.5 %right_stats.1 = f32[8,328,128]{2,1,0:T(8,128)} custom-call(f32[512,1280]{1,0:T(8,128)} %first.5, f32[512,1280]{1,0:T(8,128)} %second.5), custom_call_target="tpu_custom_call" | custom-call | flops 2013265920 | bytes 5242880 | tf_op jit(solution)/shard_map/right_stats/pallas_call | solution.py:336
  4.5 6.8 %all-to-all-start = ((f32[8,328,128]{2,1,0:T(8,128)}), f32[8,328,128]{2,1,0:T(8,128)S(1)}, u32[]{:S(2)}, u32[]{:S(2)}) async-start(f32[8,328,128]{2,1,0:T(8,128)} %right_stats.1), calls=%async_computation | async-start | bytes 2686976 | tf_op jit(solution)/shard_map/all_to_all | solution.py:29
  11.3 3.5 %left_stats.1 = (f32[528,128]{1,0:T(8,128)S(1)}, f32[528,128]{1,0:T(8,128)S(1)}) custom-call(s32[1]{0:T(128)} %bitcast.info, f32[512,1280]{1,0:T(8,128)} %first.5, f32[512,1280]{1,0:T(8,128)} %second.5), custom_call_target="tpu_custom_call" | custom-call | flops 2013265920 | bytes 5242880 | tf_op jit(solution)/shard_map/left_stats/pallas_call | solution.py:352
  14.8 1.0 %collective-permute-start = (f32[528,128]{1,0:T(8,128)S(1)}, f32[528,128]{1,0:T(8,128)S(1)}, u32[]{:S(2)}, u32[]{:S(2)}) collective-permute-start(f32[528,128]{1,0:T(8,128)S(1)} %get-tuple-element.20), channel_id=1, source_target_pairs={{0,1},{1,0},{2,3},{3,2},{4,5},{5,4},{6,7},{7,6},{8,9},{9,8},{10,11... | collective-permute-start | bytes 811016 | tf_op jit(solution)/shard_map/ppermute | solution.py:25
  15.8 1.2 %collective-permute-done = f32[528,128]{1,0:T(8,128)S(1)} collective-permute-done((f32[528,128]{1,0:T(8,128)S(1)}, f32[528,128]{1,0:T(8,128)S(1)}, u32[]{:S(2)}, u32[]{:S(2)}) %collective-permute-start) | collective-permute-done | bytes 270368 | tf_op jit(solution)/shard_map/ppermute | solution.py:25
  17.1 3.0 %collective-permute-start.1 = (f32[264,128]{1,0:T(8,128)S(1)}, f32[264,128]{1,0:T(8,128)S(1)}, u32[]{:S(2)}, u32[]{:S(2)}) collective-permute-start(f32[264,128]{1,0:T(8,128)S(1)} %get-tuple-element.29), channel_id=1, source_target_pairs={{0,8},{1,9},{2,10},{3,11},{4,12},{5,13},{6,14},{7,15},{8,0},{9,1},... | collective-permute-start | bytes 405512 | tf_op jit(solution)/shard_map/ppermute | solution.py:25
  20.1 0.8 %collective-permute-start.3 = (f32[264,128]{1,0:T(8,128)S(1)}, f32[264,128]{1,0:T(8,128)S(1)}, u32[]{:S(2)}, u32[]{:S(2)}) collective-permute-start(f32[264,128]{1,0:T(8,128)S(1)} %get-tuple-element.30), channel_id=1, source_target_pairs={{0,12},{1,13},{2,14},{3,15},{4,8},{5,9},{6,10},{7,11},{8,4},{9,5},... | collective-permute-start | bytes 405512 | tf_op jit(solution)/shard_map/ppermute | solution.py:25
  20.8 0.0 collective-permute-start.2
  20.8 2.6 %collective-permute-done.1 = f32[264,128]{1,0:T(8,128)S(1)} collective-permute-done((f32[264,128]{1,0:T(8,128)S(1)}, f32[264,128]{1,0:T(8,128)S(1)}, u32[]{:S(2)}, u32[]{:S(2)}) %collective-permute-start.1) | collective-permute-done | bytes 135200 | tf_op jit(solution)/shard_map/ppermute | solution.py:25
  23.4 2.9 %collective-permute-done.3 = f32[264,128]{1,0:T(8,128)S(1)} collective-permute-done((f32[264,128]{1,0:T(8,128)S(1)}, f32[264,128]{1,0:T(8,128)S(1)}, u32[]{:S(2)}, u32[]{:S(2)}) %collective-permute-start.3) | collective-permute-done | bytes 135200 | tf_op jit(solution)/shard_map/ppermute | solution.py:25
  26.4 0.3 collective-permute-done.2
  26.7 2.5 %collective-permute-start.4 = (f32[264,128]{1,0:T(8,128)S(1)}, f32[264,128]{1,0:T(8,128)S(1)}, u32[]{:S(2)}, u32[]{:S(2)}) collective-permute-start(f32[264,128]{1,0:T(8,128)S(1)} %add_add_fusion.own), channel_id=1, source_target_pairs={{0,2},{1,3},{2,0},{3,1},{4,6},{5,7},{6,4},{7,5},{8,10},{9,11},{10,... | collective-permute-start | bytes 405512 | tf_op jit(solution)/shard_map/ppermute | solution.py:25
  29.3 0.1 all-to-all-done.arrived
  29.3 5.2 %right_roots.1 = (f32[8,328,128]{2,1,0:T(8,128)}, f32[8,128]{1,0:T(8,128)S(1)}) custom-call(f32[8,328,128]{2,1,0:T(8,128)S(1)} %all-to-all-done.arrived), custom_call_target="tpu_custom_call" | custom-call | flops 2013265920 | bytes 2686976 | tf_op jit(solution)/shard_map/right_roots/pallas_call | solution.py:369
  34.6 0.0 collective-permute-done.4.other
  34.6 4.7 %all-to-all-start.1 = ((f32[8,328,128]{2,1,0:T(8,128)}), f32[8,328,128]{2,1,0:T(8,128)S(1)}, u32[]{:S(2)}, u32[]{:S(2)}) async-start(f32[8,328,128]{2,1,0:T(8,128)} %get-tuple-element.27), calls=%async_computation.1 | async-start | bytes 2686976 | tf_op jit(solution)/shard_map/all_to_all | solution.py:29
  39.3 4.1 %left_root.1 = f32[264,128]{1,0:T(8,128)S(1)} custom-call(f32[264,128]{1,0:T(8,128)S(1)} %add_add_fusion.own, f32[264,128]{1,0:T(8,128)S(1)} %collective-permute-done.4.other), custom_call_target="tpu_custom_call" | custom-call | flops 2013265920 | bytes 405504 | tf_op jit(solution)/shard_map/left_root/pallas_call | solution.py:381
  43.5 1.8 %collective-permute-start.5 = (f32[264,128]{1,0:T(8,128)S(1)}, f32[264,128]{1,0:T(8,128)S(1)}, u32[]{:S(2)}, u32[]{:S(2)}) collective-permute-start(f32[264,128]{1,0:T(8,128)S(1)} %left_root.1), channel_id=1, source_target_pairs={{0,4},{1,5},{2,6},{3,7},{4,0},{5,1},{6,2},{7,3},{8,12},{9,13},{10,... | collective-permute-start | bytes 405512 | tf_op jit(solution)/shard_map/ppermute | solution.py:25
  45.2 2.7 %collective-permute-done.5 = f32[264,128]{1,0:T(8,128)S(1)} collective-permute-done((f32[264,128]{1,0:T(8,128)S(1)}, f32[264,128]{1,0:T(8,128)S(1)}, u32[]{:S(2)}, u32[]{:S(2)}) %collective-permute-start.5) | collective-permute-done | bytes 135200 | tf_op jit(solution)/shard_map/ppermute | solution.py:25
  47.9 2.7 %collective-permute-start.6 = (f32[528,128]{1,0:T(8,128)S(1)}, f32[528,128]{1,0:T(8,128)S(1)}, u32[]{:S(2)}, u32[]{:S(2)}) collective-permute-start(f32[528,128]{1,0:T(8,128)S(1)} %maximum_select_fusion.mine), channel_id=1, source_target_pairs={{0,1},{1,0},{2,3},{3,2},{4,5},{5,4},{6,7},{7,6},{8,9},{9,8},{10,11... | collective-permute-start | bytes 811016 | tf_op jit(solution)/shard_map/ppermute | solution.py:25
  50.6 1.2 %collective-permute-done.6.other = f32[528,128]{1,0:T(8,128)S(1)} collective-permute-done((f32[528,128]{1,0:T(8,128)S(1)}, f32[528,128]{1,0:T(8,128)S(1)}, u32[]{:S(2)}, u32[]{:S(2)}) %collective-permute-start.6) | collective-permute-done | bytes 270368 | tf_op jit(solution)/shard_map/ppermute | solution.py:25
  51.8 5.6 %halfway.1 = bf16[5,4,512,256]{3,2,1,0:T(8,128)(2,1)} custom-call(s32[1]{0:T(128)} %bitcast.info, f32[512,1280]{1,0:T(8,128)} %first.5, f32[512,1280]{1,0:T(8,128)} %second.5, f32[528,128]{1,0:T(8,128)S(1)} %maximum_select_fusion.mine, f32[528,128]{1,0:T(8,128)S(1)} %collective-permute-done.6.other), custom_call_target="tpu_custom_call" | custom-call | flops 2013265920 | bytes 10485760 | tf_op jit(solution)/shard_map/halfway/pallas_call | solution.py:400
  57.4 0.0 all-to-all-done.1.gathered
  57.5 8.3 %finish.1 = f32[512,1280]{1,0:T(8,128)} custom-call(bf16[5,4,512,256]{3,2,1,0:T(8,128)(2,1)} %halfway.1, f32[8,328,128]{2,1,0:T(8,128)S(1)} %all-to-all-done.1.gathered, f32[8,128]{1,0:T(8,128)S(1)} %get-tuple-element.28.diagonals), custom_call_target="tpu_custom_call" | custom-call | flops 6039797760 | bytes 10485760 | tf_op jit(solution)/shard_map/finish/pallas_call | solution.py:411
  (4 shorter events, 0.1 us)
Async XLA Ops:
  4.5 24.9 %all-to-all-start = ((f32[8,328,128]{2,1,0:T(8,128)}), f32[8,328,128]{2,1,0:T(8,128)S(1)}, u32[]{:S(2)}, u32[]{:S(2)}) async-start(f32[8,328,128]{2,1,0:T(8,128)} %right_stats.1), calls=%async_computation | async-start | bytes 2686976 | tf_op jit(solution)/shard_map/all_to_all | solution.py:29
  14.8 2.2 %collective-permute-start = (f32[528,128]{1,0:T(8,128)S(1)}, f32[528,128]{1,0:T(8,128)S(1)}, u32[]{:S(2)}, u32[]{:S(2)}) collective-permute-start(f32[528,128]{1,0:T(8,128)S(1)} %get-tuple-element.20), channel_id=1, source_target_pairs={{0,1},{1,0},{2,3},{3,2},{4,5},{5,4},{6,7},{7,6},{8,9},{9,8},{10,11... | collective-permute-start | bytes 811016 | tf_op jit(solution)/shard_map/ppermute | solution.py:25
  17.1 6.4 %collective-permute-start.1 = (f32[264,128]{1,0:T(8,128)S(1)}, f32[264,128]{1,0:T(8,128)S(1)}, u32[]{:S(2)}, u32[]{:S(2)}) collective-permute-start(f32[264,128]{1,0:T(8,128)S(1)} %get-tuple-element.29), channel_id=1, source_target_pairs={{0,8},{1,9},{2,10},{3,11},{4,12},{5,13},{6,14},{7,15},{8,0},{9,1},... | collective-permute-start | bytes 405512 | tf_op jit(solution)/shard_map/ppermute | solution.py:25
  20.1 6.3 %collective-permute-start.3 = (f32[264,128]{1,0:T(8,128)S(1)}, f32[264,128]{1,0:T(8,128)S(1)}, u32[]{:S(2)}, u32[]{:S(2)}) collective-permute-start(f32[264,128]{1,0:T(8,128)S(1)} %get-tuple-element.30), channel_id=1, source_target_pairs={{0,12},{1,13},{2,14},{3,15},{4,8},{5,9},{6,10},{7,11},{8,4},{9,5},... | collective-permute-start | bytes 405512 | tf_op jit(solution)/shard_map/ppermute | solution.py:25
  20.8 5.9 %collective-permute-start.2 = (f32[264,128]{1,0:T(8,128)S(1)}, f32[264,128]{1,0:T(8,128)S(1)}, u32[]{:S(2)}, u32[]{:S(2)}) collective-permute-start(f32[264,128]{1,0:T(8,128)S(1)} %get-tuple-element.30), channel_id=1, source_target_pairs={{0,4},{1,5},{2,6},{3,7},{4,0},{5,1},{6,2},{7,3},{8,12},{9,13},{10,... | collective-permute-start | bytes 405512 | tf_op jit(solution)/shard_map/ppermute | solution.py:25
  26.7 7.9 %collective-permute-start.4 = (f32[264,128]{1,0:T(8,128)S(1)}, f32[264,128]{1,0:T(8,128)S(1)}, u32[]{:S(2)}, u32[]{:S(2)}) collective-permute-start(f32[264,128]{1,0:T(8,128)S(1)} %add_add_fusion.own), channel_id=1, source_target_pairs={{0,2},{1,3},{2,0},{3,1},{4,6},{5,7},{6,4},{7,5},{8,10},{9,11},{10,... | collective-permute-start | bytes 405512 | tf_op jit(solution)/shard_map/ppermute | solution.py:25
  34.6 22.9 %all-to-all-start.1 = ((f32[8,328,128]{2,1,0:T(8,128)}), f32[8,328,128]{2,1,0:T(8,128)S(1)}, u32[]{:S(2)}, u32[]{:S(2)}) async-start(f32[8,328,128]{2,1,0:T(8,128)} %get-tuple-element.27), calls=%async_computation.1 | async-start | bytes 2686976 | tf_op jit(solution)/shard_map/all_to_all | solution.py:29
  43.5 4.4 %collective-permute-start.5 = (f32[264,128]{1,0:T(8,128)S(1)}, f32[264,128]{1,0:T(8,128)S(1)}, u32[]{:S(2)}, u32[]{:S(2)}) collective-permute-start(f32[264,128]{1,0:T(8,128)S(1)} %left_root.1), channel_id=1, source_target_pairs={{0,4},{1,5},{2,6},{3,7},{4,0},{5,1},{6,2},{7,3},{8,12},{9,13},{10,... | collective-permute-start | bytes 405512 | tf_op jit(solution)/shard_map/ppermute | solution.py:25
  47.9 3.8 %collective-permute-start.6 = (f32[528,128]{1,0:T(8,128)S(1)}, f32[528,128]{1,0:T(8,128)S(1)}, u32[]{:S(2)}, u32[]{:S(2)}) collective-permute-start(f32[528,128]{1,0:T(8,128)S(1)} %maximum_select_fusion.mine), channel_id=1, source_target_pairs={{0,1},{1,0},{2,3},{3,2},{4,5},{5,4},{6,7},{7,6},{8,9},{9,8},{10,11... | collective-permute-start | bytes 811016 | tf_op jit(solution)/shard_map/ppermute | solution.py:25

commit v8 on v7

--- a/solution.py
+++ b/solution.py
@@ -241,7 +241,7 @@
         for s in range(2):
             for place, block in enumerate((core, 1 - core)):
                 rows = pl.ds(pl.multiple_of(block * BLOCK, BLOCK), BLOCK)
-                result = product(split[place][s], parts(buffer[s, b, rows, :]))
+                result = halves_product(split[place][s], parts(buffer[s, b, rows, :]))
                 results[b, 2 * s, rows, :], results[b, 2 * s + 1, rows, :] = parts(result)
         copy = pltpu.make_async_copy(results.at[b], out.at[b], out_sems.at[b])
         copy.start()
@@ -284,14 +284,14 @@
         copy.start()
         copies.append(copy)
 
-    for _ in range(7):
+    for _ in range(8):
         next(chain)
     for copy in fetches:
         copy.wait()
     for b in range(RIGHT - 1):
         one, two = [parts(unpacked(gathered[2 * b + s, :PACK, :])) for s in range(2)]
         for _ in applied(held, b, one, two, buffer):
-            next(chain)
+            next(chain, None)
         stored(b, 0, 2 * BLOCK, b)
     for _ in chain:
         pass

time: 66.1 us -> 65.7 us (level)
  transfers between devices with their start and end apart: 9 -> 9, of which waited for: 7 -> 8; matrix products, arithmetic and copies ran while one was open for 0% -> 0% of each run, Pallas kernels for 28% -> 28%
where the time goes in v8:
time: 65.7 us; the launch traced here: 65.5 us
  Pallas kernels  30.7 us (47%)
  starting transfers between devices  23.3 us (35%)
  waiting for transfers between devices  11.1 us (17%)
    ppermute x7, starting transfers between devices, swap(): return lax.ppermute(value, 'col', [(i, i ^ d) for i in range(COLS)])  11.8 us
    all_to_all x2, starting transfers between devices, exchanged(): return lax.all_to_all(slots, 'row', split_axis=0, concat_axis=0, tiled=True)  11.5 us
    ppermute x7, waiting for transfers between devices, swap(): return lax.ppermute(value, 'col', [(i, i ^ d) for i in range(COLS)])  10.9 us
    pallas_call x1, Pallas kernels, body(): pl.pallas_call(finish_kernel, in_specs=[HBM, VMEM, VMEM], out_specs=HBM,...  7.96 us
    pallas_call x1, Pallas kernels, body(): pl.pallas_call(halfway_kernel, in_specs=[SMEM, HBM, HBM, VMEM, VMEM], out...  5.42 us
    pallas_call x1, Pallas kernels, body(): pl.pallas_call(right_roots_kernel, in_specs=[VMEM], out_specs=[VMEM, VMEM...  5.24 us
    pallas_call x1, Pallas kernels, body(): pl.pallas_call(right_stats_kernel, in_specs=[HBM, HBM], out_specs=HBM, ou...  4.47 us
    pallas_call x1, Pallas kernels, body(): pl.pallas_call(left_root_kernel, in_specs=[VMEM, VMEM], out_specs=VMEM, o...  4.14 us
  transfers between devices with their start and end apart: 9, of which 8 were waited for; matrix products, arithmetic and copies ran while one was open for 0% of the time, Pallas kernels for 28%

profile of v8, /device:TPU:1, one launch (start us, length us, event | category | flops | bytes accessed | tf_op | source)
XLA Modules:
  0.0 65.5 jit_solution(16619773549441333377)
XLA Ops:
  0.0 4.5 %right_stats.1 = f32[8,328,128]{2,1,0:T(8,128)} custom-call(f32[512,1280]{1,0:T(8,128)} %first.5, f32[512,1280]{1,0:T(8,128)} %second.5), custom_call_target="tpu_custom_call" | custom-call | flops 2013265920 | bytes 5242880 | tf_op jit(solution)/shard_map/right_stats/pallas_call | solution.py:336
  4.5 6.8 %all-to-all-start = ((f32[8,328,128]{2,1,0:T(8,128)}), f32[8,328,128]{2,1,0:T(8,128)S(1)}, u32[]{:S(2)}, u32[]{:S(2)}) async-start(f32[8,328,128]{2,1,0:T(8,128)} %right_stats.1), calls=%async_computation | async-start | bytes 2686976 | tf_op jit(solution)/shard_map/all_to_all | solution.py:29
  11.3 3.5 %left_stats.1 = (f32[528,128]{1,0:T(8,128)S(1)}, f32[528,128]{1,0:T(8,128)S(1)}) custom-call(s32[1]{0:T(128)} %bitcast.info, f32[512,1280]{1,0:T(8,128)} %first.5, f32[512,1280]{1,0:T(8,128)} %second.5), custom_call_target="tpu_custom_call" | custom-call | flops 2013265920 | bytes 5242880 | tf_op jit(solution)/shard_map/left_stats/pallas_call | solution.py:352
  14.8 1.0 %collective-permute-start = (f32[528,128]{1,0:T(8,128)S(1)}, f32[528,128]{1,0:T(8,128)S(1)}, u32[]{:S(2)}, u32[]{:S(2)}) collective-permute-start(f32[528,128]{1,0:T(8,128)S(1)} %get-tuple-element.20), channel_id=1, source_target_pairs={{0,1},{1,0},{2,3},{3,2},{4,5},{5,4},{6,7},{7,6},{8,9},{9,8},{10,11... | collective-permute-start | bytes 811016 | tf_op jit(solution)/shard_map/ppermute | solution.py:25
  15.8 1.2 %collective-permute-done = f32[528,128]{1,0:T(8,128)S(1)} collective-permute-done((f32[528,128]{1,0:T(8,128)S(1)}, f32[528,128]{1,0:T(8,128)S(1)}, u32[]{:S(2)}, u32[]{:S(2)}) %collective-permute-start) | collective-permute-done | bytes 270368 | tf_op jit(solution)/shard_map/ppermute | solution.py:25
  17.1 3.0 %collective-permute-start.1 = (f32[264,128]{1,0:T(8,128)S(1)}, f32[264,128]{1,0:T(8,128)S(1)}, u32[]{:S(2)}, u32[]{:S(2)}) collective-permute-start(f32[264,128]{1,0:T(8,128)S(1)} %get-tuple-element.29), channel_id=1, source_target_pairs={{0,8},{1,9},{2,10},{3,11},{4,12},{5,13},{6,14},{7,15},{8,0},{9,1},... | collective-permute-start | bytes 405512 | tf_op jit(solution)/shard_map/ppermute | solution.py:25
  20.1 0.8 %collective-permute-start.3 = (f32[264,128]{1,0:T(8,128)S(1)}, f32[264,128]{1,0:T(8,128)S(1)}, u32[]{:S(2)}, u32[]{:S(2)}) collective-permute-start(f32[264,128]{1,0:T(8,128)S(1)} %get-tuple-element.30), channel_id=1, source_target_pairs={{0,12},{1,13},{2,14},{3,15},{4,8},{5,9},{6,10},{7,11},{8,4},{9,5},... | collective-permute-start | bytes 405512 | tf_op jit(solution)/shard_map/ppermute | solution.py:25
  20.8 0.0 collective-permute-start.2
  20.8 2.6 %collective-permute-done.1 = f32[264,128]{1,0:T(8,128)S(1)} collective-permute-done((f32[264,128]{1,0:T(8,128)S(1)}, f32[264,128]{1,0:T(8,128)S(1)}, u32[]{:S(2)}, u32[]{:S(2)}) %collective-permute-start.1) | collective-permute-done | bytes 135200 | tf_op jit(solution)/shard_map/ppermute | solution.py:25
  23.4 2.9 %collective-permute-done.3 = f32[264,128]{1,0:T(8,128)S(1)} collective-permute-done((f32[264,128]{1,0:T(8,128)S(1)}, f32[264,128]{1,0:T(8,128)S(1)}, u32[]{:S(2)}, u32[]{:S(2)}) %collective-permute-start.3) | collective-permute-done | bytes 135200 | tf_op jit(solution)/shard_map/ppermute | solution.py:25
  26.4 0.3 collective-permute-done.2
  26.7 2.5 %collective-permute-start.4 = (f32[264,128]{1,0:T(8,128)S(1)}, f32[264,128]{1,0:T(8,128)S(1)}, u32[]{:S(2)}, u32[]{:S(2)}) collective-permute-start(f32[264,128]{1,0:T(8,128)S(1)} %add_add_fusion.own), channel_id=1, source_target_pairs={{0,2},{1,3},{2,0},{3,1},{4,6},{5,7},{6,4},{7,5},{8,10},{9,11},{10,... | collective-permute-start | bytes 405512 | tf_op jit(solution)/shard_map/ppermute | solution.py:25
  29.3 0.1 all-to-all-done.arrived
  29.3 5.2 %right_roots.1 = (f32[8,328,128]{2,1,0:T(8,128)}, f32[8,128]{1,0:T(8,128)S(1)}) custom-call(f32[8,328,128]{2,1,0:T(8,128)S(1)} %all-to-all-done.arrived), custom_call_target="tpu_custom_call" | custom-call | flops 2013265920 | bytes 2686976 | tf_op jit(solution)/shard_map/right_roots/pallas_call | solution.py:369
  34.6 0.0 collective-permute-done.4.other
  34.6 4.7 %all-to-all-start.1 = ((f32[8,328,128]{2,1,0:T(8,128)}), f32[8,328,128]{2,1,0:T(8,128)S(1)}, u32[]{:S(2)}, u32[]{:S(2)}) async-start(f32[8,328,128]{2,1,0:T(8,128)} %get-tuple-element.27), calls=%async_computation.1 | async-start | bytes 2686976 | tf_op jit(solution)/shard_map/all_to_all | solution.py:29
  39.3 4.1 %left_root.1 = f32[264,128]{1,0:T(8,128)S(1)} custom-call(f32[264,128]{1,0:T(8,128)S(1)} %add_add_fusion.own, f32[264,128]{1,0:T(8,128)S(1)} %collective-permute-done.4.other), custom_call_target="tpu_custom_call" | custom-call | flops 2013265920 | bytes 405504 | tf_op jit(solution)/shard_map/left_root/pallas_call | solution.py:381
  43.5 1.8 %collective-permute-start.5 = (f32[264,128]{1,0:T(8,128)S(1)}, f32[264,128]{1,0:T(8,128)S(1)}, u32[]{:S(2)}, u32[]{:S(2)}) collective-permute-start(f32[264,128]{1,0:T(8,128)S(1)} %left_root.1), channel_id=1, source_target_pairs={{0,4},{1,5},{2,6},{3,7},{4,0},{5,1},{6,2},{7,3},{8,12},{9,13},{10,... | collective-permute-start | bytes 405512 | tf_op jit(solution)/shard_map/ppermute | solution.py:25
  45.2 2.7 %collective-permute-done.5 = f32[264,128]{1,0:T(8,128)S(1)} collective-permute-done((f32[264,128]{1,0:T(8,128)S(1)}, f32[264,128]{1,0:T(8,128)S(1)}, u32[]{:S(2)}, u32[]{:S(2)}) %collective-permute-start.5) | collective-permute-done | bytes 135200 | tf_op jit(solution)/shard_map/ppermute | solution.py:25
  47.9 2.7 %collective-permute-start.6 = (f32[528,128]{1,0:T(8,128)S(1)}, f32[528,128]{1,0:T(8,128)S(1)}, u32[]{:S(2)}, u32[]{:S(2)}) collective-permute-start(f32[528,128]{1,0:T(8,128)S(1)} %maximum_select_fusion.mine), channel_id=1, source_target_pairs={{0,1},{1,0},{2,3},{3,2},{4,5},{5,4},{6,7},{7,6},{8,9},{9,8},{10,11... | collective-permute-start | bytes 811016 | tf_op jit(solution)/shard_map/ppermute | solution.py:25
  50.6 1.2 %collective-permute-done.6.other = f32[528,128]{1,0:T(8,128)S(1)} collective-permute-done((f32[528,128]{1,0:T(8,128)S(1)}, f32[528,128]{1,0:T(8,128)S(1)}, u32[]{:S(2)}, u32[]{:S(2)}) %collective-permute-start.6) | collective-permute-done | bytes 270368 | tf_op jit(solution)/shard_map/ppermute | solution.py:25
  51.8 5.4 %halfway.1 = bf16[5,4,512,256]{3,2,1,0:T(8,128)(2,1)} custom-call(s32[1]{0:T(128)} %bitcast.info, f32[512,1280]{1,0:T(8,128)} %first.5, f32[512,1280]{1,0:T(8,128)} %second.5, f32[528,128]{1,0:T(8,128)S(1)} %maximum_select_fusion.mine, f32[528,128]{1,0:T(8,128)S(1)} %collective-permute-done.6.other), custom_call_target="tpu_custom_call" | custom-call | flops 2013265920 | bytes 10485760 | tf_op jit(solution)/shard_map/halfway/pallas_call | solution.py:400
  57.2 0.1 all-to-all-done.1.gathered
  57.3 8.0 %finish.1 = f32[512,1280]{1,0:T(8,128)} custom-call(bf16[5,4,512,256]{3,2,1,0:T(8,128)(2,1)} %halfway.1, f32[8,328,128]{2,1,0:T(8,128)S(1)} %all-to-all-done.1.gathered, f32[8,128]{1,0:T(8,128)S(1)} %get-tuple-element.28.diagonals), custom_call_target="tpu_custom_call" | custom-call | flops 6039797760 | bytes 10485760 | tf_op jit(solution)/shard_map/finish/pallas_call | solution.py:411
  (4 shorter events, 0.1 us)
Async XLA Ops:
  4.5 24.9 %all-to-all-start = ((f32[8,328,128]{2,1,0:T(8,128)}), f32[8,328,128]{2,1,0:T(8,128)S(1)}, u32[]{:S(2)}, u32[]{:S(2)}) async-start(f32[8,328,128]{2,1,0:T(8,128)} %right_stats.1), calls=%async_computation | async-start | bytes 2686976 | tf_op jit(solution)/shard_map/all_to_all | solution.py:29
  14.8 2.2 %collective-permute-start = (f32[528,128]{1,0:T(8,128)S(1)}, f32[528,128]{1,0:T(8,128)S(1)}, u32[]{:S(2)}, u32[]{:S(2)}) collective-permute-start(f32[528,128]{1,0:T(8,128)S(1)} %get-tuple-element.20), channel_id=1, source_target_pairs={{0,1},{1,0},{2,3},{3,2},{4,5},{5,4},{6,7},{7,6},{8,9},{9,8},{10,11... | collective-permute-start | bytes 811016 | tf_op jit(solution)/shard_map/ppermute | solution.py:25
  17.1 6.4 %collective-permute-start.1 = (f32[264,128]{1,0:T(8,128)S(1)}, f32[264,128]{1,0:T(8,128)S(1)}, u32[]{:S(2)}, u32[]{:S(2)}) collective-permute-start(f32[264,128]{1,0:T(8,128)S(1)} %get-tuple-element.29), channel_id=1, source_target_pairs={{0,8},{1,9},{2,10},{3,11},{4,12},{5,13},{6,14},{7,15},{8,0},{9,1},... | collective-permute-start | bytes 405512 | tf_op jit(solution)/shard_map/ppermute | solution.py:25
  20.1 6.3 %collective-permute-start.3 = (f32[264,128]{1,0:T(8,128)S(1)}, f32[264,128]{1,0:T(8,128)S(1)}, u32[]{:S(2)}, u32[]{:S(2)}) collective-permute-start(f32[264,128]{1,0:T(8,128)S(1)} %get-tuple-element.30), channel_id=1, source_target_pairs={{0,12},{1,13},{2,14},{3,15},{4,8},{5,9},{6,10},{7,11},{8,4},{9,5},... | collective-permute-start | bytes 405512 | tf_op jit(solution)/shard_map/ppermute | solution.py:25
  20.8 5.9 %collective-permute-start.2 = (f32[264,128]{1,0:T(8,128)S(1)}, f32[264,128]{1,0:T(8,128)S(1)}, u32[]{:S(2)}, u32[]{:S(2)}) collective-permute-start(f32[264,128]{1,0:T(8,128)S(1)} %get-tuple-element.30), channel_id=1, source_target_pairs={{0,4},{1,5},{2,6},{3,7},{4,0},{5,1},{6,2},{7,3},{8,12},{9,13},{10,... | collective-permute-start | bytes 405512 | tf_op jit(solution)/shard_map/ppermute | solution.py:25
  26.7 7.9 %collective-permute-start.4 = (f32[264,128]{1,0:T(8,128)S(1)}, f32[264,128]{1,0:T(8,128)S(1)}, u32[]{:S(2)}, u32[]{:S(2)}) collective-permute-start(f32[264,128]{1,0:T(8,128)S(1)} %add_add_fusion.own), channel_id=1, source_target_pairs={{0,2},{1,3},{2,0},{3,1},{4,6},{5,7},{6,4},{7,5},{8,10},{9,11},{10,... | collective-permute-start | bytes 405512 | tf_op jit(solution)/shard_map/ppermute | solution.py:25
  34.6 22.8 %all-to-all-start.1 = ((f32[8,328,128]{2,1,0:T(8,128)}), f32[8,328,128]{2,1,0:T(8,128)S(1)}, u32[]{:S(2)}, u32[]{:S(2)}) async-start(f32[8,328,128]{2,1,0:T(8,128)} %get-tuple-element.27), calls=%async_computation.1 | async-start | bytes 2686976 | tf_op jit(solution)/shard_map/all_to_all | solution.py:29
  43.5 4.4 %collective-permute-start.5 = (f32[264,128]{1,0:T(8,128)S(1)}, f32[264,128]{1,0:T(8,128)S(1)}, u32[]{:S(2)}, u32[]{:S(2)}) collective-permute-start(f32[264,128]{1,0:T(8,128)S(1)} %left_root.1), channel_id=1, source_target_pairs={{0,4},{1,5},{2,6},{3,7},{4,0},{5,1},{6,2},{7,3},{8,12},{9,13},{10,... | collective-permute-start | bytes 405512 | tf_op jit(solution)/shard_map/ppermute | solution.py:25
  47.9 3.8 %collective-permute-start.6 = (f32[528,128]{1,0:T(8,128)S(1)}, f32[528,128]{1,0:T(8,128)S(1)}, u32[]{:S(2)}, u32[]{:S(2)}) collective-permute-start(f32[528,128]{1,0:T(8,128)S(1)} %maximum_select_fusion.mine), channel_id=1, source_target_pairs={{0,1},{1,0},{2,3},{3,2},{4,5},{5,4},{6,7},{7,6},{8,9},{9,8},{10,11... | collective-permute-start | bytes 811016 | tf_op jit(solution)/shard_map/ppermute | solution.py:25

commit v9 on v8

--- a/solution.py
+++ b/solution.py
@@ -284,7 +284,7 @@
         copy.start()
         copies.append(copy)
 
-    for _ in range(8):
+    for _ in range(9):
         next(chain)
     for copy in fetches:
         copy.wait()

time: 65.7 us -> 65.7 us (level)
  no operation moved by 1% of the time
where the time goes in v9:
time: 65.7 us; the launch traced here: 65.5 us
  Pallas kernels  30.8 us (47%)
  starting transfers between devices  23.3 us (35%)
  waiting for transfers between devices  11.1 us (17%)
    ppermute x7, starting transfers between devices, swap(): return lax.ppermute(value, 'col', [(i, i ^ d) for i in range(COLS)])  11.8 us
    all_to_all x2, starting transfers between devices, exchanged(): return lax.all_to_all(slots, 'row', split_axis=0, concat_axis=0, tiled=True)  11.5 us
    ppermute x7, waiting for transfers between devices, swap(): return lax.ppermute(value, 'col', [(i, i ^ d) for i in range(COLS)])  10.9 us
    pallas_call x1, Pallas kernels, body(): pl.pallas_call(finish_kernel, in_specs=[HBM, VMEM, VMEM], out_specs=HBM,...  7.99 us
    pallas_call x1, Pallas kernels, body(): pl.pallas_call(halfway_kernel, in_specs=[SMEM, HBM, HBM, VMEM, VMEM], out...  5.42 us
    pallas_call x1, Pallas kernels, body(): pl.pallas_call(right_roots_kernel, in_specs=[VMEM], out_specs=[VMEM, VMEM...  5.24 us
    pallas_call x1, Pallas kernels, body(): pl.pallas_call(right_stats_kernel, in_specs=[HBM, HBM], out_specs=HBM, ou...  4.47 us
    pallas_call x1, Pallas kernels, body(): pl.pallas_call(left_root_kernel, in_specs=[VMEM, VMEM], out_specs=VMEM, o...  4.14 us
  transfers between devices with their start and end apart: 9, of which 8 were waited for; matrix products, arithmetic and copies ran while one was open for 0% of the time, Pallas kernels for 28%

profile of v9, /device:TPU:1, one launch (start us, length us, event | category | flops | bytes accessed | tf_op | source)
XLA Modules:
  0.0 65.5 jit_solution(17696550679523204904)
XLA Ops:
  0.0 4.5 %right_stats.1 = f32[8,328,128]{2,1,0:T(8,128)} custom-call(f32[512,1280]{1,0:T(8,128)} %first.5, f32[512,1280]{1,0:T(8,128)} %second.5), custom_call_target="tpu_custom_call" | custom-call | flops 2013265920 | bytes 5242880 | tf_op jit(solution)/shard_map/right_stats/pallas_call | solution.py:336
  4.5 6.8 %all-to-all-start = ((f32[8,328,128]{2,1,0:T(8,128)}), f32[8,328,128]{2,1,0:T(8,128)S(1)}, u32[]{:S(2)}, u32[]{:S(2)}) async-start(f32[8,328,128]{2,1,0:T(8,128)} %right_stats.1), calls=%async_computation | async-start | bytes 2686976 | tf_op jit(solution)/shard_map/all_to_all | solution.py:29
  11.3 3.5 %left_stats.1 = (f32[528,128]{1,0:T(8,128)S(1)}, f32[528,128]{1,0:T(8,128)S(1)}) custom-call(s32[1]{0:T(128)} %bitcast.info, f32[512,1280]{1,0:T(8,128)} %first.5, f32[512,1280]{1,0:T(8,128)} %second.5), custom_call_target="tpu_custom_call" | custom-call | flops 2013265920 | bytes 5242880 | tf_op jit(solution)/shard_map/left_stats/pallas_call | solution.py:352
  14.8 1.0 %collective-permute-start = (f32[528,128]{1,0:T(8,128)S(1)}, f32[528,128]{1,0:T(8,128)S(1)}, u32[]{:S(2)}, u32[]{:S(2)}) collective-permute-start(f32[528,128]{1,0:T(8,128)S(1)} %get-tuple-element.20), channel_id=1, source_target_pairs={{0,1},{1,0},{2,3},{3,2},{4,5},{5,4},{6,7},{7,6},{8,9},{9,8},{10,11... | collective-permute-start | bytes 811016 | tf_op jit(solution)/shard_map/ppermute | solution.py:25
  15.8 1.2 %collective-permute-done = f32[528,128]{1,0:T(8,128)S(1)} collective-permute-done((f32[528,128]{1,0:T(8,128)S(1)}, f32[528,128]{1,0:T(8,128)S(1)}, u32[]{:S(2)}, u32[]{:S(2)}) %collective-permute-start) | collective-permute-done | bytes 270368 | tf_op jit(solution)/shard_map/ppermute | solution.py:25
  17.1 3.0 %collective-permute-start.1 = (f32[264,128]{1,0:T(8,128)S(1)}, f32[264,128]{1,0:T(8,128)S(1)}, u32[]{:S(2)}, u32[]{:S(2)}) collective-permute-start(f32[264,128]{1,0:T(8,128)S(1)} %get-tuple-element.29), channel_id=1, source_target_pairs={{0,8},{1,9},{2,10},{3,11},{4,12},{5,13},{6,14},{7,15},{8,0},{9,1},... | collective-permute-start | bytes 405512 | tf_op jit(solution)/shard_map/ppermute | solution.py:25
  20.1 0.8 %collective-permute-start.3 = (f32[264,128]{1,0:T(8,128)S(1)}, f32[264,128]{1,0:T(8,128)S(1)}, u32[]{:S(2)}, u32[]{:S(2)}) collective-permute-start(f32[264,128]{1,0:T(8,128)S(1)} %get-tuple-element.30), channel_id=1, source_target_pairs={{0,12},{1,13},{2,14},{3,15},{4,8},{5,9},{6,10},{7,11},{8,4},{9,5},... | collective-permute-start | bytes 405512 | tf_op jit(solution)/shard_map/ppermute | solution.py:25
  20.8 0.0 collective-permute-start.2
  20.8 2.6 %collective-permute-done.1 = f32[264,128]{1,0:T(8,128)S(1)} collective-permute-done((f32[264,128]{1,0:T(8,128)S(1)}, f32[264,128]{1,0:T(8,128)S(1)}, u32[]{:S(2)}, u32[]{:S(2)}) %collective-permute-start.1) | collective-permute-done | bytes 135200 | tf_op jit(solution)/shard_map/ppermute | solution.py:25
  23.4 2.9 %collective-permute-done.3 = f32[264,128]{1,0:T(8,128)S(1)} collective-permute-done((f32[264,128]{1,0:T(8,128)S(1)}, f32[264,128]{1,0:T(8,128)S(1)}, u32[]{:S(2)}, u32[]{:S(2)}) %collective-permute-start.3) | collective-permute-done | bytes 135200 | tf_op jit(solution)/shard_map/ppermute | solution.py:25
  26.4 0.3 collective-permute-done.2
  26.7 2.5 %collective-permute-start.4 = (f32[264,128]{1,0:T(8,128)S(1)}, f32[264,128]{1,0:T(8,128)S(1)}, u32[]{:S(2)}, u32[]{:S(2)}) collective-permute-start(f32[264,128]{1,0:T(8,128)S(1)} %add_add_fusion.own), channel_id=1, source_target_pairs={{0,2},{1,3},{2,0},{3,1},{4,6},{5,7},{6,4},{7,5},{8,10},{9,11},{10,... | collective-permute-start | bytes 405512 | tf_op jit(solution)/shard_map/ppermute | solution.py:25
  29.3 0.1 all-to-all-done.arrived
  29.3 5.2 %right_roots.1 = (f32[8,328,128]{2,1,0:T(8,128)}, f32[8,128]{1,0:T(8,128)S(1)}) custom-call(f32[8,328,128]{2,1,0:T(8,128)S(1)} %all-to-all-done.arrived), custom_call_target="tpu_custom_call" | custom-call | flops 2013265920 | bytes 2686976 | tf_op jit(solution)/shard_map/right_roots/pallas_call | solution.py:369
  34.6 0.0 collective-permute-done.4.other
  34.6 4.7 %all-to-all-start.1 = ((f32[8,328,128]{2,1,0:T(8,128)}), f32[8,328,128]{2,1,0:T(8,128)S(1)}, u32[]{:S(2)}, u32[]{:S(2)}) async-start(f32[8,328,128]{2,1,0:T(8,128)} %get-tuple-element.27), calls=%async_computation.1 | async-start | bytes 2686976 | tf_op jit(solution)/shard_map/all_to_all | solution.py:29
  39.3 4.1 %left_root.1 = f32[264,128]{1,0:T(8,128)S(1)} custom-call(f32[264,128]{1,0:T(8,128)S(1)} %add_add_fusion.own, f32[264,128]{1,0:T(8,128)S(1)} %collective-permute-done.4.other), custom_call_target="tpu_custom_call" | custom-call | flops 2013265920 | bytes 405504 | tf_op jit(solution)/shard_map/left_root/pallas_call | solution.py:381
  43.5 1.8 %collective-permute-start.5 = (f32[264,128]{1,0:T(8,128)S(1)}, f32[264,128]{1,0:T(8,128)S(1)}, u32[]{:S(2)}, u32[]{:S(2)}) collective-permute-start(f32[264,128]{1,0:T(8,128)S(1)} %left_root.1), channel_id=1, source_target_pairs={{0,4},{1,5},{2,6},{3,7},{4,0},{5,1},{6,2},{7,3},{8,12},{9,13},{10,... | collective-permute-start | bytes 405512 | tf_op jit(solution)/shard_map/ppermute | solution.py:25
  45.2 2.7 %collective-permute-done.5 = f32[264,128]{1,0:T(8,128)S(1)} collective-permute-done((f32[264,128]{1,0:T(8,128)S(1)}, f32[264,128]{1,0:T(8,128)S(1)}, u32[]{:S(2)}, u32[]{:S(2)}) %collective-permute-start.5) | collective-permute-done | bytes 135200 | tf_op jit(solution)/shard_map/ppermute | solution.py:25
  47.9 2.7 %collective-permute-start.6 = (f32[528,128]{1,0:T(8,128)S(1)}, f32[528,128]{1,0:T(8,128)S(1)}, u32[]{:S(2)}, u32[]{:S(2)}) collective-permute-start(f32[528,128]{1,0:T(8,128)S(1)} %maximum_select_fusion.mine), channel_id=1, source_target_pairs={{0,1},{1,0},{2,3},{3,2},{4,5},{5,4},{6,7},{7,6},{8,9},{9,8},{10,11... | collective-permute-start | bytes 811016 | tf_op jit(solution)/shard_map/ppermute | solution.py:25
  50.6 1.2 %collective-permute-done.6.other = f32[528,128]{1,0:T(8,128)S(1)} collective-permute-done((f32[528,128]{1,0:T(8,128)S(1)}, f32[528,128]{1,0:T(8,128)S(1)}, u32[]{:S(2)}, u32[]{:S(2)}) %collective-permute-start.6) | collective-permute-done | bytes 270368 | tf_op jit(solution)/shard_map/ppermute | solution.py:25
  51.8 5.4 %halfway.1 = bf16[5,4,512,256]{3,2,1,0:T(8,128)(2,1)} custom-call(s32[1]{0:T(128)} %bitcast.info, f32[512,1280]{1,0:T(8,128)} %first.5, f32[512,1280]{1,0:T(8,128)} %second.5, f32[528,128]{1,0:T(8,128)S(1)} %maximum_select_fusion.mine, f32[528,128]{1,0:T(8,128)S(1)} %collective-permute-done.6.other), custom_call_target="tpu_custom_call" | custom-call | flops 2013265920 | bytes 10485760 | tf_op jit(solution)/shard_map/halfway/pallas_call | solution.py:400
  57.2 0.1 all-to-all-done.1.gathered
  57.3 8.0 %finish.1 = f32[512,1280]{1,0:T(8,128)} custom-call(bf16[5,4,512,256]{3,2,1,0:T(8,128)(2,1)} %halfway.1, f32[8,328,128]{2,1,0:T(8,128)S(1)} %all-to-all-done.1.gathered, f32[8,128]{1,0:T(8,128)S(1)} %get-tuple-element.28.diagonals), custom_call_target="tpu_custom_call" | custom-call | flops 6039797760 | bytes 10485760 | tf_op jit(solution)/shard_map/finish/pallas_call | solution.py:411
  (4 shorter events, 0.1 us)
Async XLA Ops:
  4.5 24.9 %all-to-all-start = ((f32[8,328,128]{2,1,0:T(8,128)}), f32[8,328,128]{2,1,0:T(8,128)S(1)}, u32[]{:S(2)}, u32[]{:S(2)}) async-start(f32[8,328,128]{2,1,0:T(8,128)} %right_stats.1), calls=%async_computation | async-start | bytes 2686976 | tf_op jit(solution)/shard_map/all_to_all | solution.py:29
  14.8 2.2 %collective-permute-start = (f32[528,128]{1,0:T(8,128)S(1)}, f32[528,128]{1,0:T(8,128)S(1)}, u32[]{:S(2)}, u32[]{:S(2)}) collective-permute-start(f32[528,128]{1,0:T(8,128)S(1)} %get-tuple-element.20), channel_id=1, source_target_pairs={{0,1},{1,0},{2,3},{3,2},{4,5},{5,4},{6,7},{7,6},{8,9},{9,8},{10,11... | collective-permute-start | bytes 811016 | tf_op jit(solution)/shard_map/ppermute | solution.py:25
  17.1 6.4 %collective-permute-start.1 = (f32[264,128]{1,0:T(8,128)S(1)}, f32[264,128]{1,0:T(8,128)S(1)}, u32[]{:S(2)}, u32[]{:S(2)}) collective-permute-start(f32[264,128]{1,0:T(8,128)S(1)} %get-tuple-element.29), channel_id=1, source_target_pairs={{0,8},{1,9},{2,10},{3,11},{4,12},{5,13},{6,14},{7,15},{8,0},{9,1},... | collective-permute-start | bytes 405512 | tf_op jit(solution)/shard_map/ppermute | solution.py:25
  20.1 6.3 %collective-permute-start.3 = (f32[264,128]{1,0:T(8,128)S(1)}, f32[264,128]{1,0:T(8,128)S(1)}, u32[]{:S(2)}, u32[]{:S(2)}) collective-permute-start(f32[264,128]{1,0:T(8,128)S(1)} %get-tuple-element.30), channel_id=1, source_target_pairs={{0,12},{1,13},{2,14},{3,15},{4,8},{5,9},{6,10},{7,11},{8,4},{9,5},... | collective-permute-start | bytes 405512 | tf_op jit(solution)/shard_map/ppermute | solution.py:25
  20.8 5.9 %collective-permute-start.2 = (f32[264,128]{1,0:T(8,128)S(1)}, f32[264,128]{1,0:T(8,128)S(1)}, u32[]{:S(2)}, u32[]{:S(2)}) collective-permute-start(f32[264,128]{1,0:T(8,128)S(1)} %get-tuple-element.30), channel_id=1, source_target_pairs={{0,4},{1,5},{2,6},{3,7},{4,0},{5,1},{6,2},{7,3},{8,12},{9,13},{10,... | collective-permute-start | bytes 405512 | tf_op jit(solution)/shard_map/ppermute | solution.py:25
  26.7 7.9 %collective-permute-start.4 = (f32[264,128]{1,0:T(8,128)S(1)}, f32[264,128]{1,0:T(8,128)S(1)}, u32[]{:S(2)}, u32[]{:S(2)}) collective-permute-start(f32[264,128]{1,0:T(8,128)S(1)} %add_add_fusion.own), channel_id=1, source_target_pairs={{0,2},{1,3},{2,0},{3,1},{4,6},{5,7},{6,4},{7,5},{8,10},{9,11},{10,... | collective-permute-start | bytes 405512 | tf_op jit(solution)/shard_map/ppermute | solution.py:25
  34.6 22.8 %all-to-all-start.1 = ((f32[8,328,128]{2,1,0:T(8,128)}), f32[8,328,128]{2,1,0:T(8,128)S(1)}, u32[]{:S(2)}, u32[]{:S(2)}) async-start(f32[8,328,128]{2,1,0:T(8,128)} %get-tuple-element.27), calls=%async_computation.1 | async-start | bytes 2686976 | tf_op jit(solution)/shard_map/all_to_all | solution.py:29
  43.5 4.4 %collective-permute-start.5 = (f32[264,128]{1,0:T(8,128)S(1)}, f32[264,128]{1,0:T(8,128)S(1)}, u32[]{:S(2)}, u32[]{:S(2)}) collective-permute-start(f32[264,128]{1,0:T(8,128)S(1)} %left_root.1), channel_id=1, source_target_pairs={{0,4},{1,5},{2,6},{3,7},{4,0},{5,1},{6,2},{7,3},{8,12},{9,13},{10,... | collective-permute-start | bytes 405512 | tf_op jit(solution)/shard_map/ppermute | solution.py:25
  47.9 3.8 %collective-permute-start.6 = (f32[528,128]{1,0:T(8,128)S(1)}, f32[528,128]{1,0:T(8,128)S(1)}, u32[]{:S(2)}, u32[]{:S(2)}) collective-permute-start(f32[528,128]{1,0:T(8,128)S(1)} %maximum_select_fusion.mine), channel_id=1, source_target_pairs={{0,1},{1,0},{2,3},{3,2},{4,5},{5,4},{6,7},{7,6},{8,9},{9,8},{10,11... | collective-permute-start | bytes 811016 | tf_op jit(solution)/shard_map/ppermute | solution.py:25
